TPU v7x, 512 devices: a whole 4x8x8 slice. The times are simulated.
512 devices in a mesh: dom: 64 (over y_hi, x, z), dim: 8 (over y_lo, core).
Axes of the slice: x: 4, y: 8 (y_hi: 2, y_lo: 4; y = y_hi * 4 + y_lo), z: 8, core: 2. Of those that a mesh axis runs over, the one named last changes fastest.
Arguments:
- ent_re: float32 [200, 32768], P('dim', 'dom'), may hold values from -8 to 8
- ent_im: float32 [200, 32768], P('dim', 'dom'), may hold values from -8 to 8
- ent_acc: float32 [32768], P('dom'), may hold values from 0.001 to 0.1
- rel_re: float32 [200, 4096], P('dim'), may hold values from -2.5 to 2.5
- rel_im: float32 [200, 4096], P('dim'), may hold values from -2.5 to 2.5
- rel_acc: float32 [4096], replicated, may hold values from 0.001 to 0.1
- lhs_rows: int32 [128, 128], P('dom'), may hold values from 0 to 511
- rhs_rows: int32 [128, 128], P('dom'), may hold values from 0 to 511
- rel_ids: int32 [128, 128], P('dom'), may hold values from 0 to 4095
- neg_rows: int32 [128, 1000], P('dom'), may hold values from 0 to 511
- bucket_step: int32 [128], P('dom'), may hold values from 0 to 4
Outputs:
- new_ent_re: float32 [200, 32768], P('dim', 'dom')
- new_ent_im: float32 [200, 32768], P('dim', 'dom')
- new_ent_acc: float32 [32768], P('dom')
- new_rel_re: float32 [200, 4096], P('dim')
- new_rel_im: float32 [200, 4096], P('dim')
- new_rel_acc: float32 [4096], replicated
Inputs may be any that keep to these rules, and one draw needn't show every extreme that they name: bucket_step equal to 4 marks an empty slot.
All inputs are finite; a program needn't handle non-finite values.
Results may differ from a plain program's by a relative error of at most 0.0003.
Values sent between devices are 32-bit elements; how exact they have to be, the bound alone decides.
No kernel may reach another device: no remote copies, remote signals or barrier semaphores. Data moves between devices by JAX's collectives and lax.ppermute only.
A program may use at most 64 MiB of HBM per device.

v0:
```python
import jax
import jax.numpy as jnp
from jax import lax
from jax.sharding import PartitionSpec as P

D = 400
STEPS = 4


learn_rate = 0.1


def from_behind(block, axis, distance):
    devices = range(lax.axis_size(axis))
    route = [((i - distance) % len(devices), i) for i in devices]
    return lax.ppermute(block, axis, route)


def score_weights(pos, neg, live):
    top = jnp.maximum(jnp.max(neg, -1), pos)
    e_pos = jnp.exp(pos - top)
    e_neg = jnp.exp(neg - top[..., None])
    denom = e_pos + jnp.sum(e_neg, -1)
    w_pos = (e_pos / denom - 1.0) * live[:, None]
    w_neg = e_neg / denom[..., None] * live[:, None, None]
    return (w_pos, w_neg)


def column_sum(values, indices, count):
    full = values.shape[0]
    empty = jnp.zeros((full, count), jnp.float32)
    return empty.at[:, indices.reshape(-1)].add(values.reshape(full, -1))


def complex_product(left, right, half):
    l_re, l_im = (left[:half], left[half:])
    r_re, r_im = (right[:half], right[half:])
    return jnp.concatenate([l_re * r_re - l_im * r_im, l_re * r_im + l_im * r_re], 0)


def per_device(
    ent_re,
    ent_im,
    ent_acc,
    rel_re,
    rel_im,
    rel_acc,
    lhs_rows,
    rhs_rows,
    rel_ids,
    neg_rows,
    bucket_step,
):
    width = ent_re.shape[0]
    rows = ent_re.shape[1]
    hp = lax.Precision.HIGHEST
    own_block = jnp.concatenate([ent_re, ent_im], 0)
    relation = jnp.concatenate([rel_re, rel_im], 0)
    live = (bucket_step < STEPS).astype(jnp.float32)
    stepc = jnp.minimum(bucket_step, STEPS - 1)
    groups = lhs_rows.shape[0]
    per_edge = lhs_rows.shape[1]
    full = 2 * width
    rel_cols = relation[:, rel_ids]
    tails = jnp.zeros((full, groups, per_edge), jnp.float32)
    negatives = jnp.zeros((full, groups, neg_rows.shape[1]), jnp.float32)
    block = own_block
    for step in range(STEPS):
        if step > 0:
            block = from_behind(block, "dom", 1)
        chosen = (bucket_step == step)[None, :, None]
        tails = jnp.where(chosen, block[:, rhs_rows], tails)
        negatives = jnp.where(chosen, block[:, neg_rows], negatives)
    head = own_block[:, lhs_rows]
    h_re, h_im = (head[:width], head[width:])
    r_re, r_im = (rel_cols[:width], rel_cols[width:])
    query = complex_product(head, rel_cols, width)
    pos_part = jnp.sum(query * tails, 0)
    neg_part = jnp.einsum("kce,kcn->cen", query, negatives, precision=hp)
    pos, neg = lax.psum((pos_part, neg_part), "dim")
    w_pos, w_neg = score_weights(pos, neg, live)
    grad_query = w_pos[None] * tails + jnp.einsum("cen,kcn->kce", w_neg, negatives, precision=hp)
    grad_tail = w_pos[None] * query
    grad_negative = jnp.einsum("cen,kce->kcn", w_neg, query, precision=hp)
    gq_re, gq_im = (grad_query[:width], grad_query[width:])
    grad_head = jnp.concatenate([gq_re * r_re + gq_im * r_im, gq_im * r_re - gq_re * r_im], 0)
    grad_rel = jnp.concatenate([gq_re * h_re + gq_im * h_im, gq_im * h_re - gq_re * h_im], 0)
    lhs_grad = column_sum(grad_head, lhs_rows, rows)
    tail_ids = rhs_rows + (stepc * rows)[:, None]
    neg_ids = neg_rows + (stepc * rows)[:, None]
    step_grads = column_sum(grad_tail, tail_ids, rows * STEPS)
    step_grads = step_grads + column_sum(grad_negative, neg_ids, rows * STEPS)
    step_grads = step_grads.reshape(full, STEPS, rows)
    carried = step_grads[:, STEPS - 1]
    for turn in range(1, STEPS):
        carried = from_behind(carried, "dom", -1) + step_grads[:, STEPS - 1 - turn]
    total = lhs_grad + carried
    local_rel = column_sum(grad_rel, rel_ids, relation.shape[1])
    rel_total = lax.psum(local_rel, "dom")
    ent_sq, rel_sq = lax.psum((jnp.sum(total * total, 0), jnp.sum(rel_total * rel_total, 0)), "dim")
    new_ent_acc = ent_acc + ent_sq / D
    new_rel_acc = rel_acc + rel_sq / D
    ent_scale = learn_rate / jnp.sqrt(new_ent_acc)[None, :]
    rel_scale = learn_rate / jnp.sqrt(new_rel_acc)[None, :]
    new_ent = own_block - ent_scale * total
    new_rel = relation - rel_scale * rel_total
    return (
        new_ent[:width],
        new_ent[width:],
        new_ent_acc,
        new_rel[:width],
        new_rel[width:],
        new_rel_acc,
    )


def solution(mesh):
    return jax.shard_map(
        per_device,
        mesh=mesh,
        in_specs=(
            P("dim", "dom"),
            P("dim", "dom"),
            P("dom"),
            P("dim", None),
            P("dim", None),
            P(),
            P("dom", None),
            P("dom", None),
            P("dom", None),
            P("dom", None),
            P("dom"),
        ),
        out_specs=(P("dim", "dom"), P("dim", "dom"), P("dom"), P("dim", None), P("dim", None), P()),
        check_vma=False,
    )
```

profile of v0, /device:TPU:1, one launch (start us, length us, event | category | flops | bytes accessed | tf_op | source)
XLA Modules:
  0.0 1130.6 jit_solution(17349319869569836198)
XLA Ops:
  7.2 0.9 pad_maximum_fusion.1
  8.2 4.8 collective-permute-start
  13.1 1.2 minimum_multiply_fusion
  14.3 1.2 broadcast_compare_fusion.3
  15.5 0.7 fusion.16
  16.2 0.7 fusion.17
  16.9 0.7 gather_fusion
  17.6 0.7 copy.64
  18.3 1.3 pad_maximum_fusion
  20.3 0.7 gather_fusion.1
  21.1 0.7 broadcast_add_fusion
  21.8 0.8 multiply_subtract_fusion.4
  22.7 1.3 fusion.18
  24.2 10.9 collective-permute-done
  35.1 1.9 collective-permute-start.1
  37.0 0.7 gather_fusion.5
  37.8 12.6 %collective-permute-done.1 = f32[50,512]{0,1:T(8,128)S(1)} collective-permute-done((f32[50,512]{0,1:T(8,128)S(1)}, f32[50,512]{0,1:T(8,128)S(1)}, u32[]{:S(2)}, u32[]{:S(2)}) %collective-permute-start.1) | collective-permute-done | bytes 102432 | tf_op jit(solution)/shard_map/ppermute | solution.py:16
  50.4 1.9 collective-permute-start.2
  52.4 7.6 gather_fusion.9
  59.9 2.3 copy.79
  62.4 7.6 gather_fusion.8
  69.9 2.3 copy.80
  72.3 7.6 gather_fusion.7
  79.9 2.3 copy.81
  82.2 7.6 gather_fusion.6
  89.8 2.3 copy.82
  92.1 1.6 select_select_fusion
  93.8 0.8 copy-done.2
  94.5 2.8 fusion.9
  98.5 0.7 gather_fusion.4
  99.4 0.7 gather_fusion.3
  100.2 0.7 gather_fusion.2
  101.0 1.4 fusion.15
  102.4 24.1 %psum.35 = f32[2,128]{1,0:T(2,128)S(1)} all-reduce(f32[2,128]{1,0:T(2,128)S(1)} %get-tuple-element.30), channel_id=1, replica_groups=mesh['dom'=64,'dim'=8] {'dim'}, use_global_device_ids=true, to_apply=%region_1.2 | all-reduce | flops 256 | bytes 2048 | tf_op jit(solution)/shard_map/psum | solution.py:80
  126.5 57.2 %all-reduce.4.cloned.1.call-done = f32[2,128,1000]{1,2,0:T(8,128)} async-done(((f32[2,128,1000]{1,2,0:T(8,128)}), f32[2,128,1000]{1,2,0:T(8,128)}) %all-reduce.4.cloned.1.call-update) | async-done | bytes 1024016 | tf_op jit(solution)/shard_map/psum | solution.py:80
  183.8 1.4 reduce_max.9
  185.1 1.4 fusion.3
  186.6 2.6 convolution_bitcast_fusion
  190.1 1.4 copy.87
  191.5 12.8 %scatter_custom_fusion.1 = f32[50,2048]{0,1:T(8,128)} fusion(s32[2000]{0:T(1024)S(1)} %bitcast.105, f32[2000,50]{1,0:T(8,128)} %copy.87, f32[]{:T(128)} %constant.14.clone.1), kind=kCustom, calls=%fused_computation.25 | custom fusion | flops 100000 | bytes 410112 | tf_op jit(solution)/shard_map/scatter-add | solution.py:32
  204.3 2.6 scatter_custom_fusion
  206.9 1.8 add.158
  208.7 11.3 collective-permute-start.3
  220.1 0.9 fusion
  221.0 7.9 collective-permute-done.3
  229.0 0.7 fusion.13
  229.7 12.4 %collective-permute-start.4 = (f32[50,512]{0,1:T(8,128)}, f32[50,512]{0,1:T(8,128)}, u32[]{:S(2)}, u32[]{:S(2)}) collective-permute-start(f32[50,512]{0,1:T(8,128)} %fusion.13), channel_id=1, source_target_pairs={{8,0},{16,8},{24,16},{32,24},{40,32},{48,40},{56,48},{64,56},{72,6... | collective-permute-start | bytes 307208 | tf_op jit(solution)/shard_map/ppermute | solution.py:16
  242.2 0.8 copy.92
  243.0 3.2 scatter_custom_fusion.3
  246.2 4.9 collective-permute-done.4
  251.1 1.7 fusion.12
  252.7 12.2 %collective-permute-start.5 = (f32[50,512]{0,1:T(8,128)}, f32[50,512]{0,1:T(8,128)S(1)}, u32[]{:S(2)}, u32[]{:S(2)}) collective-permute-start(f32[50,512]{0,1:T(8,128)} %fusion.12), channel_id=1, source_target_pairs={{8,0},{16,8},{24,16},{32,24},{40,32},{48,40},{56,48},{64,56},{72,6... | collective-permute-start | bytes 307208 | tf_op jit(solution)/shard_map/ppermute | solution.py:16
  265.2 6.2 collective-permute-done.5
  271.4 1.0 fusion.11
  272.4 2.0 scatter_fusion
  274.6 767.2 %all-reduce.6.cloned.1.call-done = f32[50,4096]{0,1:T(8,128)} async-done(((f32[50,4096]{0,1:T(8,128)}), f32[50,4096]{0,1:T(8,128)}) %all-reduce.6.cloned.1.call-update) | async-done | bytes 819216 | tf_op jit(solution)/shard_map/psum | solution.py:99
  1041.8 2.2 multiply_reduce_fusion
  1044.0 68.4 %all-reduce = (f32[512]{0:T(512)S(1)}, f32[4096]{0:T(1024)S(1)}) all-reduce(f32[512]{0:T(512)S(1)} %multiply_reduce_fusion.1, f32[4096]{0:T(1024)S(1)} %multiply_reduce_fusion), channel_id=1, replica_groups=mesh['dom'=64,'dim'=8] {'dim'}, use_global_device_ids=true, to_apply=%region_9.10 | all-reduce | flops 4608 | bytes 36864 | tf_op jit(solution)/shard_map/psum | solution.py:100
  1113.3 0.8 copy.95
  1114.1 0.7 copy.94
  1115.4 1.9 multiply_subtract_fusion
  1117.4 2.0 fusion.22
  1119.4 3.0 copy.97
  1122.4 1.4 copy.96
  (82 shorter events, 5.7 us)
Async XLA Ops:
  7.2 176.6 %all-reduce.4.cloned.1.call-start = ((), (), s32[]{:S(2)}) async-start(), calls=%async_computation | async-start | bytes 2048000 | tf_op jit(solution)/shard_map/psum | solution.py:80
  8.2 26.8 %collective-permute-start = (f32[50,512]{0,1:T(8,128)S(1)}, f32[50,512]{0,1:T(8,128)S(1)}, u32[]{:S(2)}, u32[]{:S(2)}) collective-permute-start(f32[50,512]{0,1:T(8,128)S(1)} %copy.90), channel_id=1, source_target_pairs={{504,0},{0,8},{8,16},{16,24},{24,32},{32,40},{40,48},{48,56},{56,6... | collective-permute-start | bytes 307208 | tf_op jit(solution)/shard_map/ppermute | solution.py:16
  19.6 1.5 copy-start.7
  35.1 15.3 %collective-permute-start.1 = (f32[50,512]{0,1:T(8,128)S(1)}, f32[50,512]{0,1:T(8,128)S(1)}, u32[]{:S(2)}, u32[]{:S(2)}) collective-permute-start(f32[50,512]{0,1:T(8,128)S(1)} %collective-permute-done), channel_id=1, source_target_pairs={{504,0},{0,8},{8,16},{16,24},{24,32},{32,40},{40,48},{48,56},{56,6... | collective-permute-start | bytes 307208 | tf_op jit(solution)/shard_map/ppermute | solution.py:16
  50.4 31.8 %collective-permute-start.2 = (f32[50,512]{0,1:T(8,128)S(1)}, f32[50,512]{0,1:T(8,128)S(1)}, u32[]{:S(2)}, u32[]{:S(2)}) collective-permute-start(f32[50,512]{0,1:T(8,128)S(1)} %collective-permute-done.1), channel_id=1, source_target_pairs={{504,0},{0,8},{8,16},{16,24},{24,32},{32,40},{40,48},{48,56},{56,6... | collective-permute-start | bytes 307208 | tf_op jit(solution)/shard_map/ppermute | solution.py:16
  82.2 9.9 copy-start.8
  82.2 9.9 copy-start.9
  82.2 9.9 copy-start.10
  92.1 5.3 copy-start.12
  92.1 5.9 copy-start.11
  93.8 0.8 copy-start.2
  97.3 944.5 %all-reduce.6.cloned.1.call-start = ((), (), s32[]{:S(2)}) async-start(), calls=%async_computation.1 | async-start | bytes 4194304 | tf_op jit(solution)/shard_map/psum | solution.py:99
  99.3 87.2 %copy-start.15 = (f32[2]{0:T(128)S(1)}, f32[2]{0:T(128)}, u32[]{:S(2)}) copy-start(f32[2]{0:T(128)} %get-tuple-element.53) | copy-start | bytes 28
  206.9 13.1 %copy-start.1 = (f32[2,128,1000]{1,2,0:T(8,128)S(1)}, f32[2,128,1000]{1,2,0:T(8,128)}, u32[]{:S(2)}) copy-start(f32[2,128,1000]{1,2,0:T(8,128)} %all-reduce.4.cloned.1.call-done) | copy-start | bytes 3072004
  206.9 13.1 %copy-start.3 = (f32[2,1000,50]{1,2,0:T(8,128)S(1)}, f32[2,1000,50]{1,2,0:T(8,128)}, u32[]{:S(2)}) copy-start(f32[2,1000,50]{1,2,0:T(8,128)} %copy-done.2) | copy-start | bytes 1200004
  206.9 13.1 %copy-start.5 = (f32[2,128,50]{1,2,0:T(8,128)S(1)}, f32[2,128,50]{1,2,0:T(8,128)}, u32[]{:S(2)}) copy-start(f32[2,128,50]{1,2,0:T(8,128)} %get-tuple-element.31) | copy-start | bytes 153604
  206.9 13.1 %copy-start.16 = (f32[2]{0:T(128)S(1)}, f32[2]{0:T(128)}, u32[]{:S(2)}) copy-start(f32[2]{0:T(128)} %get-tuple-element.53) | copy-start | bytes 28
  208.7 42.4 %copy-start = (f32[50,2048]{0,1:T(8,128)}, f32[50,2048]{0,1:T(8,128)S(1)}, u32[]{:S(2)}) copy-start(f32[50,2048]{0,1:T(8,128)S(1)} %add.158) | copy-start | bytes 1228804
  208.7 20.3 %collective-permute-start.3 = (f32[50,512]{0,1:T(8,128)S(1)}, f32[50,512]{0,1:T(8,128)S(1)}, u32[]{:S(2)}, u32[]{:S(2)}) collective-permute-start(f32[50,512]{0,1:T(8,128)S(1)} %slice_bitcast_fusion.3), channel_id=1, source_target_pairs={{8,0},{16,8},{24,16},{32,24},{40,32},{48,40},{56,48},{64,56},{72,6... | collective-permute-start | bytes 307208 | tf_op jit(solution)/shard_map/ppermute | solution.py:16
  220.0 1.0 copy-start.4
  229.7 21.3 %collective-permute-start.4 = (f32[50,512]{0,1:T(8,128)}, f32[50,512]{0,1:T(8,128)}, u32[]{:S(2)}, u32[]{:S(2)}) collective-permute-start(f32[50,512]{0,1:T(8,128)} %fusion.13), channel_id=1, source_target_pairs={{8,0},{16,8},{24,16},{32,24},{40,32},{48,40},{56,48},{64,56},{72,6... | collective-permute-start | bytes 307208 | tf_op jit(solution)/shard_map/ppermute | solution.py:16
  243.0 22.0 %copy-start.13 = (s32[2,128]{1,0:T(2,128)S(1)}, s32[2,128]{1,0:T(2,128)}, u32[]{:S(2)}) copy-start(s32[2,128]{1,0:T(2,128)} %param.17) | copy-start | bytes 3076
  252.7 18.7 %collective-permute-start.5 = (f32[50,512]{0,1:T(8,128)}, f32[50,512]{0,1:T(8,128)S(1)}, u32[]{:S(2)}, u32[]{:S(2)}) collective-permute-start(f32[50,512]{0,1:T(8,128)} %fusion.12), channel_id=1, source_target_pairs={{8,0},{16,8},{24,16},{32,24},{40,32},{48,40},{56,48},{64,56},{72,6... | collective-permute-start | bytes 307208 | tf_op jit(solution)/shard_map/ppermute | solution.py:16
  265.2 847.3 %copy-start.14 = (f32[512]{0:T(512)S(1)}, f32[512]{0:T(512)}, u32[]{:S(2)}) copy-start(f32[512]{0:T(512)} %param.13) | copy-start | bytes 6148
  274.6 840.2 %copy-start.6 = (f32[4096]{0:T(1024)S(1)}, f32[4096]{0:T(1024)}, u32[]{:S(2)}) copy-start(f32[4096]{0:T(1024)} %param.16) | copy-start | bytes 49156
Sparse Core Ops, SparseCore 0:
  97.5 86.2 all-reduce.3
  246.3 795.4 all-reduce.5
where the time goes:
time: 1130 us
  waiting for transfers between devices  867 us (77%)
  blocking collectives  92.5 us (8%)
  local copies, waits for them, and re-layouts  58.4 us (5%)
  other arithmetic  47.3 us (4%)
  starting transfers between devices  44.6 us (4%)
  between operations  14.5 us (1%)
    psum x1, waiting for transfers between devices, per_device(): rel_total = lax.psum(local_rel, 'dom')  767 us
    psum x1, blocking collectives, per_device(): lax.psum((jnp.sum(total * total, 0), jnp.sum(rel_total * rel_total, 0)),...  68.4 us
    psum x1, waiting for transfers between devices, per_device(): pos, neg = lax.psum((pos_part, neg_part), 'dim')  57.2 us
    ppermute x6, starting transfers between devices, from_behind(): return lax.ppermute(block, axis, route)  44.5 us
    ppermute x6, waiting for transfers between devices, from_behind(): return lax.ppermute(block, axis, route)  42.6 us
    gather x8, local copies, waits for them, and re-layouts, per_device(): negatives = jnp.where(chosen, block[:, neg_rows], negatives)  39.6 us
    psum x1, blocking collectives, per_device(): pos, neg = lax.psum((pos_part, neg_part), 'dim')  24.1 us
  transfers between devices with their start and end apart: 8, of which 7 were waited for; matrix products, arithmetic and copies ran while one was open for 5% of the time, Pallas kernels for 0%

commit v1 on v0

v1 whole, which is shorter than its diff:
```python
import jax
import jax.numpy as jnp
from jax import lax
from jax.experimental import pallas as pl
from jax.experimental.pallas import tpu as pltpu
from jax.sharding import Mesh, PartitionSpec as P

D = 400
STEPS = 4
LEARN_RATE = 0.1
W = 25
ROWS = 512
CH = 128
REL = 4096
DOM = ("yh", "x", "z")
DIM = ("yl", "core")
ZY = ("yh", "z")
F32 = jnp.float32
BF16 = jnp.bfloat16
I32 = jnp.int32
HIGHEST = lax.Precision.HIGHEST
VM = pl.BlockSpec(memory_space=pltpu.VMEM)
SM = pl.BlockSpec(memory_space=pltpu.SMEM)


def call(kernel, name, outs, specs):
    single = isinstance(outs, tuple)
    shapes = [jax.ShapeDtypeStruct(s, F32) for s in ([outs] if single else outs)]
    return pl.pallas_call(
        kernel,
        out_shape=shapes[0] if single else shapes,
        in_specs=specs,
        out_specs=VM if single else [VM] * len(shapes),
        compiler_params=pltpu.CompilerParams(vmem_limit_bytes=32 * 1024 * 1024),
        name=name,
    )


def iota(shape, axis):
    return lax.broadcasted_iota(I32, shape, axis)


def split3(x):
    hi = x.astype(BF16)
    rest = x - hi.astype(F32)
    mid = rest.astype(BF16)
    lo = (rest - mid.astype(F32)).astype(BF16)
    return jnp.concatenate([hi, mid, lo], 0)


def join3(y):
    r = y.shape[0] // 3
    return y[:r] + (y[r : 2 * r] + y[2 * r :])


def nn(a, b):
    return lax.dot_general(a, b, (((1,), (0,)), ((), ())), preferred_element_type=F32)


def nt(a, b):
    return lax.dot_general(a, b, (((1,), (1,)), ((), ())), preferred_element_type=F32)


def onehot_rows(ids, count):
    return jnp.where(iota((count, ids.shape[1]), 0) == ids, 1.0, 0.0).astype(BF16)


def pad32(x):
    return jnp.concatenate([x, jnp.zeros((32 - W, x.shape[1]), F32)], 0)


def pack(block):
    return jnp.concatenate([pad32(block[:W]), pad32(block[W:])], 0)


def edge_ids(ref):
    return jnp.concatenate([ref[0:1, :], ref[1:2, :]], 1)


def query_kernel(info, ent_re, ent_im, rel_re, rel_im, racc, lhs, rel_ids, neg, head_o, relc_o, q_o, m_o, piece_o, pacc_o):
    own = jnp.concatenate([pad32(ent_re[...]), pad32(ent_im[...])], 0)
    head = join3(nn(split3(own), onehot_rows(edge_ids(lhs), ROWS)))
    ids = edge_ids(rel_ids)
    step = 1024
    acc = jnp.zeros((192, 2 * CH), F32)
    for k in range(0, REL, step):
        part = jnp.concatenate([pad32(rel_re[:, k : k + step]), pad32(rel_im[:, k : k + step])], 0)
        acc = acc + nn(split3(part), onehot_rows(ids - k, step))
    relc = join3(acc)
    head_o[...] = head
    relc_o[...] = relc
    h_re, h_im = head[:32], head[32:]
    r_re, r_im = relc[:32], relc[32:]
    q_o[...] = jnp.concatenate([h_re * r_re - h_im * r_im, h_re * r_im + h_im * r_re], 0)
    ones = jnp.ones((16, neg.shape[1]), BF16)
    for c in range(2):
        m_o[8 * c : 8 * c + 8, :] = nt(ones, onehot_rows(neg[c : c + 1, :], ROWS))[:8]
    p = info[2]
    tile = p // 2
    odd = p - 2 * tile
    lane = pl.multiple_of(tile * 128, 128)
    t_re = pad32(rel_re[:, pl.ds(lane, 128)])
    t_im = pad32(rel_im[:, pl.ds(lane, 128)])
    first = iota((32, 128), 1) < 64
    even_piece = jnp.where(first, t_re, pltpu.roll(t_im, 64, 1))
    odd_piece = jnp.where(first, pltpu.roll(t_re, 64, 1), t_im)
    piece_o[...] = jnp.where(odd == 0, even_piece, odd_piece)
    a = jnp.broadcast_to(racc[pl.ds(tile, 1), :], (8, 128))
    pacc_o[...] = jnp.where(odd == 0, a, pltpu.roll(a, 64, 1))


def choose(step, blocks):
    b = blocks[STEPS - 1]
    for s in range(STEPS - 1):
        b = jnp.where(step == s, blocks[s], b)
    return b


def score_kernel(bucket, q_r, b0, b1, b2, b3, s_o):
    blocks = [pack(b[...]) for b in (b0, b1, b2, b3)]
    for c in range(2):
        s = lax.dot_general(
            q_r[:, c * CH : (c + 1) * CH], choose(bucket[c], blocks),
            (((0,), (0,)), ((), ())), precision=HIGHEST, preferred_element_type=F32)
        for yl in range(4):
            s_o[2 * yl + c] = s[32 * yl : 32 * yl + 32]


def weight_kernel(info, bucket, parts, m_r, rhs, w_o):
    s = parts[0]
    for i in range(1, 8):
        s = s + parts[i]
    core = info[0]
    m = jnp.where(core == 0, m_r[0:1, :], m_r[8:9, :])
    live = jnp.where(jnp.where(core == 0, bucket[0], bucket[1]) < STEPS, 1.0, 0.0)
    hit = iota(s.shape, 1) == rhs[...]
    pos = jnp.sum(jnp.where(hit, s, 0.0), 1, keepdims=True)
    masked = jnp.where(m > 0.0, s, -1e30)
    top = jnp.maximum(jnp.max(masked, 1, keepdims=True), pos)
    e_pos = jnp.exp(pos - top)
    e_neg = m * jnp.exp(masked - top)
    denom = e_pos + jnp.sum(e_neg, 1, keepdims=True)
    w_pos = (e_pos / denom - 1.0) * live
    w = e_neg * (live / denom) + jnp.where(hit, w_pos, 0.0)
    for i in range(4):
        w_o[i] = w


def grad_kernel(info, bucket, q_r, head_r, relc_r, w_mine, w_other, b0, b1, b2, b3, lhs, rel_ids, s0_o, s1_o, s23_o, gr_o):
    core = info[0]
    mine = w_mine[...].reshape(CH, ROWS)
    other = w_other[...].reshape(CH, ROWS)
    blocks = [pack(b[...]) for b in (b0, b1, b2, b3)]
    gq = []
    slots = [jnp.zeros((64, ROWS), F32) for _ in range(STEPS)]
    for c in range(2):
        w = jnp.where(core == c, mine, other)
        step = jnp.minimum(bucket[c], STEPS - 1)
        block = choose(step, blocks)
        gq.append(lax.dot_general(block, w, (((1,), (1,)), ((), ())), precision=HIGHEST, preferred_element_type=F32))
        g = lax.dot_general(q_r[:, c * CH : (c + 1) * CH], w, (((1,), (0,)), ((), ())), precision=HIGHEST, preferred_element_type=F32)
        for s in range(STEPS):
            slots[s] = slots[s] + jnp.where(step == s, g, 0.0)
    gq = jnp.concatenate(gq, 1)
    g_re, g_im = gq[:32], gq[32:]
    h_re, h_im = head_r[:32, :], head_r[32:, :]
    r_re, r_im = relc_r[:32, :], relc_r[32:, :]
    gh = jnp.concatenate([g_re * r_re + g_im * r_im, g_im * r_re - g_re * r_im], 0)
    slots[0] = slots[0] + join3(nt(split3(gh), onehot_rows(edge_ids(lhs), ROWS)))
    gr_re = (g_re * h_re + g_im * h_im)[:W]
    gr_im = (g_im * h_re - g_re * h_im)[:W]
    ids = edge_ids(rel_ids).astype(F32)
    for i in range(4):
        gr_o[i, 0:W, :] = gr_re
        gr_o[i, W : 2 * W, :] = gr_im
        gr_o[i, 2 * W : 2 * W + 1, :] = ids
    for ref, at, slot in ((s0_o, 0, 0), (s1_o, 0, 1), (s23_o, 0, 3), (s23_o, 2 * W, 2)):
        ref[at : at + W, :] = slots[slot][:W]
        ref[at + W : at + 2 * W, :] = slots[slot][32 : 32 + W]


def place_kernel(info, gr, out):
    x = info[1]
    vals = []
    cols = []
    for i in range(4):
        vals.append(split3(pack(gr[i, 0 : 2 * W, :])))
        ids = gr[i, 2 * W : 2 * W + 1, :].astype(I32)
        mine = jnp.bitwise_and(jnp.right_shift(ids, 9), 3) == x
        cols.append(jnp.where(mine, jnp.right_shift(ids, 11) * 512 + jnp.bitwise_and(ids, 511), -1))
    total = join3(nt(jnp.concatenate(vals, 1), onehot_rows(jnp.concatenate(cols, 1), 1024)))
    first = iota((32, 128), 1) < 64
    for t in range(8):
        t_re = total[:32, 128 * t : 128 * t + 128]
        t_im = total[32:, 128 * t : 128 * t + 128]
        out[2 * t] = jnp.where(first, t_re, pltpu.roll(t_im, 64, 1))[:W]
        out[2 * t + 1] = jnp.where(first, pltpu.roll(t_re, 64, 1), t_im)[:W]


def square_kernel(parts, s0, got1, got23, tot_o, ent_o, sq_o):
    tot = parts[0]
    for i in range(1, 16):
        tot = tot + parts[i]
    tot_o[...] = tot
    rs = jnp.broadcast_to(jnp.sum(tot * tot, 0, keepdims=True), (8, 128))
    rs = (rs + pltpu.roll(rs, 64, 1))[0:1]
    ent = s0[...] + (got1[...] + got23[2 * W : 4 * W, :])
    ent_o[...] = ent
    es = jnp.sum(ent * ent, 0, keepdims=True)
    for i in range(8):
        sq_o[i, :, 0:ROWS] = es
        sq_o[i, :, ROWS : ROWS + 128] = rs


def update_kernel(sq, tot, ent, ent_re, ent_im, eacc, piece, pacc, re_o, im_o, acc_o, rel_o):
    s = sq[0]
    for i in range(1, 8):
        s = s + sq[i]
    acc = eacc[...] + s[:, :ROWS] / D
    acc_o[...] = acc
    scale = LEARN_RATE / jnp.sqrt(acc)
    re_o[...] = ent_re[...] - scale * ent[0:W, :]
    im_o[...] = ent_im[...] - scale * ent[W : 2 * W, :]
    racc = pacc[0:1, :] + s[:, ROWS:] / D
    racc = jnp.where(iota((1, 128), 1) < 64, racc, jnp.broadcast_to(pltpu.roll(jnp.broadcast_to(racc, (8, 128)), 64, 1)[0:1], (1, 128)))
    rel = piece[0:W, :] - (LEARN_RATE / jnp.sqrt(racc)) * tot[...]
    for i in range(64):
        rel_o[i, 0:W, :] = rel
        rel_o[i, W : W + 1, :] = racc


def unpack_kernel(rel, re_o, im_o, acc_o):
    first = iota((32, 128), 1) < 64
    pad = jnp.zeros((32 - W - 1, 128), F32)
    for t in range(32):
        a = jnp.concatenate([rel[2 * t], pad], 0)
        b = jnp.concatenate([rel[2 * t + 1], pad], 0)
        re = jnp.where(first, a, pltpu.roll(b, 64, 1))
        im = jnp.where(first, pltpu.roll(a, 64, 1), b)
        re_o[:, 128 * t : 128 * t + 128] = re[:W]
        im_o[:, 128 * t : 128 * t + 128] = im[:W]
        acc_o[t : t + 1, :] = re[W : W + 1]


def shift(block, distance):
    return lax.ppermute(block, DOM, [(i, (i + distance) % 64) for i in range(64)])


def exchange(pieces, axes):
    return lax.all_to_all(pieces, axes, 0, 0)


def per_device(ent_re, ent_im, ent_acc, rel_re, rel_im, rel_acc, lhs_rows, rhs_rows, rel_ids, neg_rows, bucket_step):
    core = lax.axis_index("core")
    yl = lax.axis_index("yl")
    info = jnp.stack([core, lax.axis_index("x"), lax.axis_index(DOM)]).astype(I32)
    own = jnp.concatenate([ent_re, ent_im], 0)
    b1, b2, b3 = [shift(own, d) for d in (1, 2, 3)]
    neg = jnp.pad(neg_rows, ((0, 0), (0, 24)), constant_values=-1)
    rhs = lax.dynamic_slice(rhs_rows, (core, 32 * yl), (1, 32)).reshape(32, 1)
    head, relc, q, m, piece, pacc = call(
        query_kernel, "query",
        [(64, 256), (64, 256), (64, 256), (16, ROWS), (32, 128), (8, 128)], [SM] + [VM] * 8,
    )(info, ent_re, ent_im, rel_re, rel_im, rel_acc.reshape(32, 128), lhs_rows, rel_ids, neg)
    s = call(score_kernel, "score", (8, 32, ROWS), [SM] + [VM] * 5)(bucket_step, q, own, b1, b2, b3)
    s = exchange(s, DIM)
    w = call(weight_kernel, "weight", (4, 32, ROWS), [SM, SM] + [VM] * 3)(info, bucket_step, s, m, rhs)
    w_mine = exchange(w, "yl")
    w_other = lax.ppermute(w_mine, "core", [(0, 1), (1, 0)])
    s0, s1, s23, gr = call(
        grad_kernel, "grad",
        [(2 * W, ROWS), (2 * W, ROWS), (4 * W, ROWS), (4, 2 * W + 1, 256)], [SM, SM] + [VM] * 11,
    )(info, bucket_step, q, head, relc, w_mine, w_other, own, b1, b2, b3, lhs_rows, rel_ids)
    got23 = shift(s23, -2)
    gr = exchange(gr, "x")
    pieces = call(place_kernel, "place", (16, W, 128), [SM, VM])(info, gr)
    got1 = shift(s1 + got23[: 2 * W], -1)
    pieces = exchange(pieces, ZY)
    tot, ent, sq = call(
        square_kernel, "square", [(W, 128), (2 * W, ROWS), (8, 1, ROWS + 128)], [VM] * 4
    )(pieces, s0, got1, got23)
    sq = exchange(sq, DIM)
    new_re, new_im, new_acc, rel = call(
        update_kernel, "update", [(W, ROWS), (W, ROWS), (1, ROWS), (64, W + 1, 128)], [VM] * 8
    )(sq, tot, ent, ent_re, ent_im, ent_acc.reshape(1, ROWS), piece, pacc)
    rel = exchange(rel, DOM)
    new_rel_re, new_rel_im, new_rel_acc = call(
        unpack_kernel, "unpack", [(W, REL), (W, REL), (32, 128)], [VM]
    )(rel)
    return new_re, new_im, new_acc.reshape(ROWS), new_rel_re, new_rel_im, new_rel_acc.reshape(REL)


def solution(mesh):
    fine = Mesh(mesh.devices.reshape(2, 4, 8, 4, 2), DOM + DIM)
    return jax.shard_map(
        per_device,
        mesh=fine,
        in_specs=(
            P(DIM, DOM), P(DIM, DOM), P(DOM), P(DIM, None), P(DIM, None), P(),
            P(DOM, None), P(DOM, None), P(DOM, None), P(DOM, None), P(DOM),
        ),
        out_specs=(P(DIM, DOM), P(DIM, DOM), P(DOM), P(DIM, None), P(DIM, None), P()),
        check_vma=False,
    )
```

time: 1130 us -> 170 us (0.15)
  the two profiles are of different devices: /device:TPU:1 before, /device:TPU:14 now
where the time goes in v1:
time: 170 us; the launch traced here: 169 us
  blocking collectives  74.4 us (44%)
  starting transfers between devices  45.3 us (27%)
  waiting for transfers between devices  32.7 us (19%)
  Pallas kernels  10.9 us (6%)
  local copies, waits for them, and re-layouts  4.3 us (3%)
    all_to_all x3, blocking collectives, exchange(): return lax.all_to_all(pieces, axes, 0, 0)  74.4 us
    all_to_all x3, starting transfers between devices, exchange(): return lax.all_to_all(pieces, axes, 0, 0)  21.9 us
    ppermute x5, starting transfers between devices, shift(): lax.ppermute(block, DOM, [(i, (i + distance) % 64) for i in range(64)])  21.5 us
    all_to_all x3, waiting for transfers between devices, exchange(): return lax.all_to_all(pieces, axes, 0, 0)  17.3 us
    ppermute x5, waiting for transfers between devices, shift(): lax.ppermute(block, DOM, [(i, (i + distance) % 64) for i in range(64)])  14 us
    unnamed x22, local copies, waits for them, and re-layouts  4.13 us
  transfers between devices with their start and end apart: 9, of which 8 were waited for; matrix products, arithmetic and copies ran while one was open for 0% of the time, Pallas kernels for 2%

profile of v1, /device:TPU:14, one launch (start us, length us, event | category | flops | bytes accessed | tf_op | source)
XLA Modules:
  0.0 169.5 jit_solution(10400977722420485202)
XLA Ops:
  0.6 0.0 copy-start
  0.6 0.0 copy-start.1
  0.7 0.0 copy-start.2
  0.7 0.9 pad_maximum_fusion.b0
  1.6 7.9 %collective-permute-start.2 = (f32[50,512]{1,0:T(8,128)S(1)}, f32[50,512]{1,0:T(8,128)S(1)}, u32[]{:S(2)}, u32[]{:S(2)}) collective-permute-start(f32[50,512]{1,0:T(8,128)S(1)} %pad_maximum_fusion.b0), channel_id=1, source_target_pairs={{0,24},{8,32},{16,40},{24,48},{32,56},{40,64},{48,72},{56,80},{64,... | collective-permute-start | bytes 307208 | tf_op jit(solution)/shard_map/ppermute | solution.py:246
  9.5 6.4 %collective-permute-start.1 = (f32[50,512]{1,0:T(8,128)S(1)}, f32[50,512]{1,0:T(8,128)S(1)}, u32[]{:S(2)}, u32[]{:S(2)}) collective-permute-start(f32[50,512]{1,0:T(8,128)S(1)} %pad_maximum_fusion.b0), channel_id=1, source_target_pairs={{0,16},{8,24},{16,32},{24,40},{32,48},{40,56},{48,64},{56,72},{64,... | collective-permute-start | bytes 307208 | tf_op jit(solution)/shard_map/ppermute | solution.py:246
  15.9 3.4 %collective-permute-start = (f32[50,512]{1,0:T(8,128)S(1)}, f32[50,512]{1,0:T(8,128)S(1)}, u32[]{:S(2)}, u32[]{:S(2)}) collective-permute-start(f32[50,512]{1,0:T(8,128)S(1)} %pad_maximum_fusion.b0), channel_id=1, source_target_pairs={{0,8},{8,16},{16,24},{24,32},{32,40},{40,48},{48,56},{56,64},{64,7... | collective-permute-start | bytes 307208 | tf_op jit(solution)/shard_map/ppermute | solution.py:246
  19.3 0.0 copy-start.10
  19.3 0.0 copy-start.5
  19.3 0.7 copy-done.10
  20.0 0.0 copy-start.8
  20.0 0.1 pad_add_fusion.info
  20.1 0.0 copy-start.7
  20.1 0.0 copy-done.1
  20.1 0.0 copy-done.2
  20.1 0.0 copy-done.5
  20.1 0.6 copy-done.8
  20.7 0.1 copy-done.7
  20.8 0.0 copy-start.3
  20.8 1.0 copy-done.3
  21.8 0.0 copy-start.4
  21.8 1.0 copy-done.4
  22.9 1.7 query.1
  24.5 0.0 copy-start.6
  24.5 0.0 collective-permute-done.2.b3
  24.6 1.3 collective-permute-done.1.b2
  25.9 2.4 %collective-permute-done.b1 = f32[50,512]{1,0:T(8,128)S(1)} collective-permute-done((f32[50,512]{1,0:T(8,128)S(1)}, f32[50,512]{1,0:T(8,128)S(1)}, u32[]{:S(2)}, u32[]{:S(2)}) %collective-permute-start) | collective-permute-done | bytes 102432 | tf_op jit(solution)/shard_map/ppermute | solution.py:246
  28.2 0.0 copy-done.6
  28.3 2.0 %score.1 = f32[8,32,512]{2,1,0:T(8,128)} custom-call(s32[2]{0:T(128)S(1)} %copy-done.6, f32[64,256]{1,0:T(8,128)S(1)} %get-tuple-element.26.q_r, f32[50,512]{1,0:T(8,128)S(1)} %pad_maximum_fusion.b0, f32[50,512]{1,0:T(8,128)S(1)} %collective-permute-done.b1, f32[50,512]{1,0:T(8,128)S(1)} %collective-permute-done.1.b2, f32[50,512]{1,0:T(8,128)S(1)} %collective-permute-done.2.b3), custom_call_target="tpu_custom_call" | custom-call | tf_op jit(solution)/shard_map/score/pallas_call | solution.py:265
  30.2 5.3 %all-to-all-start = ((f32[8,32,512]{2,1,0:T(8,128)}), f32[8,32,512]{2,1,0:T(8,128)S(1)}, u32[]{:S(2)}, u32[]{:S(2)}) async-start(f32[8,32,512]{2,1,0:T(8,128)} %score.1), calls=%async_computation | async-start | bytes 1048576 | tf_op jit(solution)/shard_map/all_to_all | solution.py:250
  35.5 0.0 copy-done
  35.5 0.1 dynamic-slice_bitcast_fusion
  35.6 0.1 copy.17.rhs
  35.7 12.0 %all-to-all-done.parts = f32[8,32,512]{2,1,0:T(8,128)S(1)} async-done(((f32[8,32,512]{2,1,0:T(8,128)}), f32[8,32,512]{2,1,0:T(8,128)S(1)}, u32[]{:S(2)}, u32[]{:S(2)}) %all-to-all-start) | async-done | bytes 524320 | tf_op jit(solution)/shard_map/all_to_all | solution.py:250
  47.7 0.8 weight.1
  48.5 12.9 %all_to_all.30.w_mine = f32[4,32,512]{2,1,0:T(8,128)S(1)} all-to-all(f32[4,32,512]{2,1,0:T(8,128)S(1)} %weight.1), channel_id=1, replica_groups=mesh['yh'=2,'x'=4,'z'=8,'yl'=4,'core'=2] {'yl'}, dimensions={0} | all-to-all | bytes 524288 | tf_op jit(solution)/shard_map/all_to_all | solution.py:250
  61.3 1.9 %collective-permute-start.3 = (f32[4,32,512]{2,1,0:T(8,128)S(1)}, f32[4,32,512]{2,1,0:T(8,128)S(1)}, u32[]{:S(2)}, u32[]{:S(2)}) collective-permute-start(f32[4,32,512]{2,1,0:T(8,128)S(1)} %all_to_all.30.w_mine), channel_id=1, source_target_pairs={{0,1},{1,0},{2,3},{3,2},{4,5},{5,4},{6,7},{7,6},{8,9},{9,8},{10,11... | collective-permute-start | bytes 786440 | tf_op jit(solution)/shard_map/ppermute | solution.py:269
  63.2 1.5 collective-permute-done.3.w_other
  64.7 2.2 %grad.1 = (f32[50,512]{1,0:T(8,128)S(1)}, f32[50,512]{1,0:T(8,128)S(1)}, f32[100,512]{1,0:T(8,128)S(1)}, f32[4,51,256]{2,1,0:T(8,128)}) custom-call(s32[3]{0:T(128)S(1)} %pad_add_fusion.info, s32[2]{0:T(128)S(1)} %copy-done.6, f32[64,256]{1,0:T(8,128)S(1)} %get-tuple-element.26.q_r, f32[64,256]{1,0:T(8,128)S(1)} %get-tuple-element.27.head_r, ...), custom_call_target="tpu_custom_call" | custom-call | tf_op jit(solution)/shard_map/grad/pallas_call | solution.py:270
  67.0 13.0 %all-to-all-start.2 = ((f32[4,51,256]{2,1,0:T(8,128)}), f32[4,51,256]{2,1,0:T(8,128)S(1)}, u32[]{:S(2)}, u32[]{:S(2)}) async-start(f32[4,51,256]{2,1,0:T(8,128)} %get-tuple-element.30), calls=%async_computation.2 | async-start | bytes 458752 | tf_op jit(solution)/shard_map/all_to_all | solution.py:250
  80.0 1.9 %collective-permute-start.4 = (f32[100,512]{1,0:T(8,128)S(1)}, f32[100,512]{1,0:T(8,128)S(1)}, u32[]{:S(2)}, u32[]{:S(2)}) collective-permute-start(f32[100,512]{1,0:T(8,128)S(1)} %get-tuple-element.33), channel_id=1, source_target_pairs={{0,496},{8,504},{16,0},{24,8},{32,16},{40,24},{48,32},{56,40},{64,... | collective-permute-start | bytes 614408 | tf_op jit(solution)/shard_map/ppermute | solution.py:246
  81.9 2.9 %all-to-all-done.2.gr = f32[4,51,256]{2,1,0:T(8,128)S(1)} async-done(((f32[4,51,256]{2,1,0:T(8,128)}), f32[4,51,256]{2,1,0:T(8,128)S(1)}, u32[]{:S(2)}, u32[]{:S(2)}) %all-to-all-start.2) | async-done | bytes 208928 | tf_op jit(solution)/shard_map/all_to_all | solution.py:250
  84.8 2.2 %place.1 = f32[16,25,128]{2,1,0:T(8,128)} custom-call(s32[3]{0:T(128)S(1)} %pad_add_fusion.info, f32[4,51,256]{2,1,0:T(8,128)S(1)} %all-to-all-done.2.gr), custom_call_target="tpu_custom_call" | custom-call | tf_op jit(solution)/shard_map/place/pallas_call | solution.py:276
  87.0 3.5 %all-to-all-start.3 = ((f32[16,25,128]{2,1,0:T(8,128)}), f32[16,25,128]{2,1,0:T(8,128)S(1)}, u32[]{:S(2)}, u32[]{:S(2)}) async-start(f32[16,25,128]{2,1,0:T(8,128)} %place.1), calls=%async_computation.3 | async-start | bytes 524288 | tf_op jit(solution)/shard_map/all_to_all | solution.py:250
  90.5 4.8 %collective-permute-done.4.got23 = f32[100,512]{1,0:T(8,128)S(1)} collective-permute-done((f32[100,512]{1,0:T(8,128)S(1)}, f32[100,512]{1,0:T(8,128)S(1)}, u32[]{:S(2)}, u32[]{:S(2)}) %collective-permute-start.4) | collective-permute-done | bytes 204832 | tf_op jit(solution)/shard_map/ppermute | solution.py:246
  95.4 1.9 %collective-permute-start.5 = (f32[50,512]{1,0:T(8,128)S(1)}, f32[50,512]{1,0:T(8,128)S(1)}, u32[]{:S(2)}, u32[]{:S(2)}) collective-permute-start(f32[50,512]{1,0:T(8,128)S(1)} %slice_add_fusion), channel_id=1, source_target_pairs={{0,504},{8,0},{16,8},{24,16},{32,24},{40,32},{48,40},{56,48},{64,5... | collective-permute-start | bytes 307208 | tf_op jit(solution)/shard_map/ppermute | solution.py:246
  97.3 5.4 %collective-permute-done.5.got1 = f32[50,512]{1,0:T(8,128)S(1)} collective-permute-done((f32[50,512]{1,0:T(8,128)S(1)}, f32[50,512]{1,0:T(8,128)S(1)}, u32[]{:S(2)}, u32[]{:S(2)}) %collective-permute-start.5) | collective-permute-done | bytes 102432 | tf_op jit(solution)/shard_map/ppermute | solution.py:246
  102.7 2.4 %all-to-all-done.3.parts = f32[16,25,128]{2,1,0:T(8,128)S(1)} async-done(((f32[16,25,128]{2,1,0:T(8,128)}), f32[16,25,128]{2,1,0:T(8,128)S(1)}, u32[]{:S(2)}, u32[]{:S(2)}) %all-to-all-start.3) | async-done | bytes 204832 | tf_op jit(solution)/shard_map/all_to_all | solution.py:250
  105.1 0.1 square.1
  105.2 7.4 %all_to_all.31.sq = f32[8,1,640]{2,1,0:T(1,128)S(1)} all-to-all(f32[8,1,640]{2,1,0:T(1,128)S(1)} %get-tuple-element.34), channel_id=1, replica_groups=mesh['yh'=2,'x'=4,'z'=8,'yl'=4,'core'=2] {'yl','core'}, dimensions={0} | all-to-all | bytes 40960 | tf_op jit(solution)/shard_map/all_to_all | solution.py:250
  112.6 0.0 copy-start.9
  112.6 0.7 copy-done.9
  113.3 0.7 update.1
  113.9 54.2 %all_to_all.32.rel = f32[64,26,128]{2,1,0:T(8,128)S(1)} all-to-all(f32[64,26,128]{2,1,0:T(8,128)S(1)} %get-tuple-element.42), channel_id=1, replica_groups=mesh['yh'=2,'x'=4,'z'=8,'yl'=4,'core'=2] {'yh','x','z'}, dimensions={0} | all-to-all | bytes 1703936 | tf_op jit(solution)/shard_map/all_to_all | solution.py:250
  168.2 1.3 unpack.1
  (2 shorter events, 0.0 us)
Async XLA Ops:
  0.6 34.9 %copy-start = (s32[2,128]{1,0:T(2,128)S(1)}, s32[2,128]{1,0:T(2,128)}, u32[]{:S(2)}) copy-start(s32[2,128]{1,0:T(2,128)} %param.18) | copy-start | bytes 3076
  0.6 19.4 %copy-start.1 = (f32[25,512]{1,0:T(8,128)S(1)}, f32[25,512]{1,0:T(8,128)}, u32[]{:S(2)}) copy-start(f32[25,512]{1,0:T(8,128)} %ent_re.3) | copy-start | bytes 153604
  0.7 19.4 %copy-start.2 = (f32[25,512]{1,0:T(8,128)S(1)}, f32[25,512]{1,0:T(8,128)}, u32[]{:S(2)}) copy-start(f32[25,512]{1,0:T(8,128)} %ent_im.3) | copy-start | bytes 153604
  1.6 23.0 %collective-permute-start.2 = (f32[50,512]{1,0:T(8,128)S(1)}, f32[50,512]{1,0:T(8,128)S(1)}, u32[]{:S(2)}, u32[]{:S(2)}) collective-permute-start(f32[50,512]{1,0:T(8,128)S(1)} %pad_maximum_fusion.b0), channel_id=1, source_target_pairs={{0,24},{8,32},{16,40},{24,48},{32,56},{40,64},{48,72},{56,80},{64,... | collective-permute-start | bytes 307208 | tf_op jit(solution)/shard_map/ppermute | solution.py:246
  9.5 16.4 %collective-permute-start.1 = (f32[50,512]{1,0:T(8,128)S(1)}, f32[50,512]{1,0:T(8,128)S(1)}, u32[]{:S(2)}, u32[]{:S(2)}) collective-permute-start(f32[50,512]{1,0:T(8,128)S(1)} %pad_maximum_fusion.b0), channel_id=1, source_target_pairs={{0,16},{8,24},{16,32},{24,40},{32,48},{40,56},{48,64},{56,72},{64,... | collective-permute-start | bytes 307208 | tf_op jit(solution)/shard_map/ppermute | solution.py:246
  15.9 12.3 %collective-permute-start = (f32[50,512]{1,0:T(8,128)S(1)}, f32[50,512]{1,0:T(8,128)S(1)}, u32[]{:S(2)}, u32[]{:S(2)}) collective-permute-start(f32[50,512]{1,0:T(8,128)S(1)} %pad_maximum_fusion.b0), channel_id=1, source_target_pairs={{0,8},{8,16},{16,24},{24,32},{32,40},{40,48},{48,56},{56,64},{64,7... | collective-permute-start | bytes 307208 | tf_op jit(solution)/shard_map/ppermute | solution.py:246
  19.3 0.7 copy-start.10
  19.3 0.8 copy-start.5
  20.0 0.7 copy-start.8
  20.1 0.7 copy-start.7
  20.8 1.0 copy-start.3
  21.8 1.0 copy-start.4
  24.5 3.7 %copy-start.6 = (s32[2]{0:T(128)S(1)}, s32[2]{0:T(128)}, u32[]{:S(2)}) copy-start(s32[2]{0:T(128)} %bucket.5) | copy-start | bytes 28
  30.2 17.4 %all-to-all-start = ((f32[8,32,512]{2,1,0:T(8,128)}), f32[8,32,512]{2,1,0:T(8,128)S(1)}, u32[]{:S(2)}, u32[]{:S(2)}) async-start(f32[8,32,512]{2,1,0:T(8,128)} %score.1), calls=%async_computation | async-start | bytes 1048576 | tf_op jit(solution)/shard_map/all_to_all | solution.py:250
  61.3 3.4 %collective-permute-start.3 = (f32[4,32,512]{2,1,0:T(8,128)S(1)}, f32[4,32,512]{2,1,0:T(8,128)S(1)}, u32[]{:S(2)}, u32[]{:S(2)}) collective-permute-start(f32[4,32,512]{2,1,0:T(8,128)S(1)} %all_to_all.30.w_mine), channel_id=1, source_target_pairs={{0,1},{1,0},{2,3},{3,2},{4,5},{5,4},{6,7},{7,6},{8,9},{9,8},{10,11... | collective-permute-start | bytes 786440 | tf_op jit(solution)/shard_map/ppermute | solution.py:269
  67.0 17.9 %all-to-all-start.2 = ((f32[4,51,256]{2,1,0:T(8,128)}), f32[4,51,256]{2,1,0:T(8,128)S(1)}, u32[]{:S(2)}, u32[]{:S(2)}) async-start(f32[4,51,256]{2,1,0:T(8,128)} %get-tuple-element.30), calls=%async_computation.2 | async-start | bytes 458752 | tf_op jit(solution)/shard_map/all_to_all | solution.py:250
  80.0 15.4 %collective-permute-start.4 = (f32[100,512]{1,0:T(8,128)S(1)}, f32[100,512]{1,0:T(8,128)S(1)}, u32[]{:S(2)}, u32[]{:S(2)}) collective-permute-start(f32[100,512]{1,0:T(8,128)S(1)} %get-tuple-element.33), channel_id=1, source_target_pairs={{0,496},{8,504},{16,0},{24,8},{32,16},{40,24},{48,32},{56,40},{64,... | collective-permute-start | bytes 614408 | tf_op jit(solution)/shard_map/ppermute | solution.py:246
  87.0 18.1 %all-to-all-start.3 = ((f32[16,25,128]{2,1,0:T(8,128)}), f32[16,25,128]{2,1,0:T(8,128)S(1)}, u32[]{:S(2)}, u32[]{:S(2)}) async-start(f32[16,25,128]{2,1,0:T(8,128)} %place.1), calls=%async_computation.3 | async-start | bytes 524288 | tf_op jit(solution)/shard_map/all_to_all | solution.py:250
  95.4 7.3 %collective-permute-start.5 = (f32[50,512]{1,0:T(8,128)S(1)}, f32[50,512]{1,0:T(8,128)S(1)}, u32[]{:S(2)}, u32[]{:S(2)}) collective-permute-start(f32[50,512]{1,0:T(8,128)S(1)} %slice_add_fusion), channel_id=1, source_target_pairs={{0,504},{8,0},{16,8},{24,16},{32,24},{40,32},{48,40},{56,48},{64,5... | collective-permute-start | bytes 307208 | tf_op jit(solution)/shard_map/ppermute | solution.py:246
  112.6 0.7 copy-start.9

commit v2 on v1

--- a/solution.py
+++ b/solution.py
@@ -14,7 +14,7 @@
 REL = 4096
 DOM = ("yh", "x", "z")
 DIM = ("yl", "core")
-ZY = ("yh", "z")
+SWAP = [(0, 1), (1, 0)]
 F32 = jnp.float32
 BF16 = jnp.bfloat16
 I32 = jnp.int32
@@ -77,7 +77,7 @@
     return jnp.concatenate([ref[0:1, :], ref[1:2, :]], 1)
 
 
-def query_kernel(info, ent_re, ent_im, rel_re, rel_im, racc, lhs, rel_ids, neg, head_o, relc_o, q_o, m_o, piece_o, pacc_o):
+def query_kernel(ent_re, ent_im, rel_re, rel_im, lhs, rel_ids, neg, head_o, relc_o, q_o, m_o):
     own = jnp.concatenate([pad32(ent_re[...]), pad32(ent_im[...])], 0)
     head = join3(nn(split3(own), onehot_rows(edge_ids(lhs), ROWS)))
     ids = edge_ids(rel_ids)
@@ -95,18 +95,6 @@
     ones = jnp.ones((16, neg.shape[1]), BF16)
     for c in range(2):
         m_o[8 * c : 8 * c + 8, :] = nt(ones, onehot_rows(neg[c : c + 1, :], ROWS))[:8]
-    p = info[2]
-    tile = p // 2
-    odd = p - 2 * tile
-    lane = pl.multiple_of(tile * 128, 128)
-    t_re = pad32(rel_re[:, pl.ds(lane, 128)])
-    t_im = pad32(rel_im[:, pl.ds(lane, 128)])
-    first = iota((32, 128), 1) < 64
-    even_piece = jnp.where(first, t_re, pltpu.roll(t_im, 64, 1))
-    odd_piece = jnp.where(first, pltpu.roll(t_re, 64, 1), t_im)
-    piece_o[...] = jnp.where(odd == 0, even_piece, odd_piece)
-    a = jnp.broadcast_to(racc[pl.ds(tile, 1), :], (8, 128))
-    pacc_o[...] = jnp.where(odd == 0, a, pltpu.roll(a, 64, 1))
 
 
 def choose(step, blocks):
@@ -116,19 +104,26 @@
     return b
 
 
-def score_kernel(bucket, q_r, b0, b1, b2, b3, s_o):
+def score_kernel(info, bucket, q_r, b0, b1, b2, b3, keep_o, send_o):
+    core = info[0]
     blocks = [pack(b[...]) for b in (b0, b1, b2, b3)]
-    for c in range(2):
+    q = [q_r[:, 0:CH], q_r[:, CH : 2 * CH]]
+    for first, out in ((1, send_o), (0, keep_o)):
+        c = core ^ first
         s = lax.dot_general(
-            q_r[:, c * CH : (c + 1) * CH], choose(bucket[c], blocks),
+            jnp.where(c == 0, q[0], q[1]), choose(bucket[c], blocks),
             (((0,), (0,)), ((), ())), precision=HIGHEST, preferred_element_type=F32)
         for yl in range(4):
-            s_o[2 * yl + c] = s[32 * yl : 32 * yl + 32]
+            out[yl] = s[32 * yl : 32 * yl + 32]
+
+
+def add_kernel(a, b, o):
+    o[...] = a[...] + b[...]
 
 
 def weight_kernel(info, bucket, parts, m_r, rhs, w_o):
     s = parts[0]
-    for i in range(1, 8):
+    for i in range(1, 4):
         s = s + parts[i]
     core = info[0]
     m = jnp.where(core == 0, m_r[0:1, :], m_r[8:9, :])
@@ -186,33 +181,46 @@
     for i in range(4):
         vals.append(split3(pack(gr[i, 0 : 2 * W, :])))
         ids = gr[i, 2 * W : 2 * W + 1, :].astype(I32)
-        mine = jnp.bitwise_and(jnp.right_shift(ids, 9), 3) == x
-        cols.append(jnp.where(mine, jnp.right_shift(ids, 11) * 512 + jnp.bitwise_and(ids, 511), -1))
+        cols.append(jnp.where(jnp.right_shift(ids, 10) == x, jnp.bitwise_and(ids, 1023), -1))
     total = join3(nt(jnp.concatenate(vals, 1), onehot_rows(jnp.concatenate(cols, 1), 1024)))
-    first = iota((32, 128), 1) < 64
-    for t in range(8):
-        t_re = total[:32, 128 * t : 128 * t + 128]
-        t_im = total[32:, 128 * t : 128 * t + 128]
-        out[2 * t] = jnp.where(first, t_re, pltpu.roll(t_im, 64, 1))[:W]
-        out[2 * t + 1] = jnp.where(first, pltpu.roll(t_re, 64, 1), t_im)[:W]
-
-
-def square_kernel(parts, s0, got1, got23, tot_o, ent_o, sq_o):
+    for z in range(8):
+        out[z, 0:W, :] = total[:W, 128 * z : 128 * z + 128]
+        out[z, W : 2 * W, :] = total[32 : 32 + W, 128 * z : 128 * z + 128]
+
+
+def fold_kernel(parts, out):
     tot = parts[0]
-    for i in range(1, 16):
+    for i in range(1, 8):
         tot = tot + parts[i]
-    tot_o[...] = tot
-    rs = jnp.broadcast_to(jnp.sum(tot * tot, 0, keepdims=True), (8, 128))
-    rs = (rs + pltpu.roll(rs, 64, 1))[0:1]
+    out[...] = tot
+
+
+def both_kernel(a, b, out):
+    tot = a[...] + b[...]
+    for z in range(8):
+        out[z] = tot
+
+
+def copies_kernel(a, out):
+    for x in range(4):
+        for z in range(8):
+            out[x, 2 * W * z : 2 * W * z + 2 * W, :] = a[z]
+
+
+def square_kernel(rel, s0, got1, got23, ent_o, sq_o):
     ent = s0[...] + (got1[...] + got23[2 * W : 4 * W, :])
     ent_o[...] = ent
     es = jnp.sum(ent * ent, 0, keepdims=True)
     for i in range(8):
         sq_o[i, :, 0:ROWS] = es
-        sq_o[i, :, ROWS : ROWS + 128] = rs
-
-
-def update_kernel(sq, tot, ent, ent_re, ent_im, eacc, piece, pacc, re_o, im_o, acc_o, rel_o):
+    for t in range(32):
+        tot = rel[t // 8, 2 * W * (t % 8) : 2 * W * (t % 8) + 2 * W, :]
+        rs = jnp.sum(tot * tot, 0, keepdims=True)
+        for i in range(8):
+            sq_o[i, :, ROWS + 128 * t : ROWS + 128 * t + 128] = rs
+
+
+def update_kernel(sq, rel, ent, ent_re, ent_im, eacc, rel_re, rel_im, racc, re_o, im_o, acc_o, rre_o, rim_o, racc_o):
     s = sq[0]
     for i in range(1, 8):
         s = s + sq[i]
@@ -221,25 +229,14 @@
     scale = LEARN_RATE / jnp.sqrt(acc)
     re_o[...] = ent_re[...] - scale * ent[0:W, :]
     im_o[...] = ent_im[...] - scale * ent[W : 2 * W, :]
-    racc = pacc[0:1, :] + s[:, ROWS:] / D
-    racc = jnp.where(iota((1, 128), 1) < 64, racc, jnp.broadcast_to(pltpu.roll(jnp.broadcast_to(racc, (8, 128)), 64, 1)[0:1], (1, 128)))
-    rel = piece[0:W, :] - (LEARN_RATE / jnp.sqrt(racc)) * tot[...]
-    for i in range(64):
-        rel_o[i, 0:W, :] = rel
-        rel_o[i, W : W + 1, :] = racc
-
-
-def unpack_kernel(rel, re_o, im_o, acc_o):
-    first = iota((32, 128), 1) < 64
-    pad = jnp.zeros((32 - W - 1, 128), F32)
+    acc = racc[...] + s[:, ROWS:] / D
+    racc_o[...] = acc
+    scale = LEARN_RATE / jnp.sqrt(acc)
     for t in range(32):
-        a = jnp.concatenate([rel[2 * t], pad], 0)
-        b = jnp.concatenate([rel[2 * t + 1], pad], 0)
-        re = jnp.where(first, a, pltpu.roll(b, 64, 1))
-        im = jnp.where(first, pltpu.roll(a, 64, 1), b)
-        re_o[:, 128 * t : 128 * t + 128] = re[:W]
-        im_o[:, 128 * t : 128 * t + 128] = im[:W]
-        acc_o[t : t + 1, :] = re[W : W + 1]
+        at = slice(128 * t, 128 * t + 128)
+        tot = rel[t // 8, 2 * W * (t % 8) : 2 * W * (t % 8) + 2 * W, :]
+        rre_o[:, at] = rel_re[:, at] - scale[:, at] * tot[:W]
+        rim_o[:, at] = rel_im[:, at] - scale[:, at] * tot[W:]
 
 
 def shift(block, distance):
@@ -253,40 +250,39 @@
 def per_device(ent_re, ent_im, ent_acc, rel_re, rel_im, rel_acc, lhs_rows, rhs_rows, rel_ids, neg_rows, bucket_step):
     core = lax.axis_index("core")
     yl = lax.axis_index("yl")
-    info = jnp.stack([core, lax.axis_index("x"), lax.axis_index(DOM)]).astype(I32)
+    info = jnp.stack([core, lax.axis_index("x")]).astype(I32)
     own = jnp.concatenate([ent_re, ent_im], 0)
     b1, b2, b3 = [shift(own, d) for d in (1, 2, 3)]
     neg = jnp.pad(neg_rows, ((0, 0), (0, 24)), constant_values=-1)
     rhs = lax.dynamic_slice(rhs_rows, (core, 32 * yl), (1, 32)).reshape(32, 1)
-    head, relc, q, m, piece, pacc = call(
-        query_kernel, "query",
-        [(64, 256), (64, 256), (64, 256), (16, ROWS), (32, 128), (8, 128)], [SM] + [VM] * 8,
-    )(info, ent_re, ent_im, rel_re, rel_im, rel_acc.reshape(32, 128), lhs_rows, rel_ids, neg)
-    s = call(score_kernel, "score", (8, 32, ROWS), [SM] + [VM] * 5)(bucket_step, q, own, b1, b2, b3)
-    s = exchange(s, DIM)
-    w = call(weight_kernel, "weight", (4, 32, ROWS), [SM, SM] + [VM] * 3)(info, bucket_step, s, m, rhs)
+    head, relc, q, m = call(
+        query_kernel, "query", [(64, 256), (64, 256), (64, 256), (16, ROWS)], [VM] * 7,
+    )(ent_re, ent_im, rel_re, rel_im, lhs_rows, rel_ids, neg)
+    quarter = (4, 32, ROWS)
+    keep, send = call(score_kernel, "score", [quarter, quarter], [SM, SM] + [VM] * 5)(info, bucket_step, q, own, b1, b2, b3)
+    s = call(add_kernel, "add", quarter, [VM] * 2)(keep, lax.ppermute(send, "core", SWAP))
+    s = exchange(s, "yl")
+    w = call(weight_kernel, "weight", quarter, [SM, SM] + [VM] * 3)(info, bucket_step, s, m, rhs)
     w_mine = exchange(w, "yl")
-    w_other = lax.ppermute(w_mine, "core", [(0, 1), (1, 0)])
+    w_other = lax.ppermute(w_mine, "core", SWAP)
     s0, s1, s23, gr = call(
         grad_kernel, "grad",
         [(2 * W, ROWS), (2 * W, ROWS), (4 * W, ROWS), (4, 2 * W + 1, 256)], [SM, SM] + [VM] * 11,
     )(info, bucket_step, q, head, relc, w_mine, w_other, own, b1, b2, b3, lhs_rows, rel_ids)
     got23 = shift(s23, -2)
     gr = exchange(gr, "x")
-    pieces = call(place_kernel, "place", (16, W, 128), [SM, VM])(info, gr)
+    pieces = call(place_kernel, "place", (8, 2 * W, 128), [SM, VM])(info, gr)
     got1 = shift(s1 + got23[: 2 * W], -1)
-    pieces = exchange(pieces, ZY)
-    tot, ent, sq = call(
-        square_kernel, "square", [(W, 128), (2 * W, ROWS), (8, 1, ROWS + 128)], [VM] * 4
-    )(pieces, s0, got1, got23)
+    pieces = exchange(pieces, "z")
+    half = call(fold_kernel, "fold", (2 * W, 128), [VM])(pieces)
+    rel = call(both_kernel, "both", (8, 2 * W, 128), [VM] * 2)(half, lax.ppermute(half, "yh", SWAP))
+    rel = exchange(rel, "z")
+    rel = exchange(call(copies_kernel, "copies", (4, 16 * W, 128), [VM])(rel), "x")
+    ent, sq = call(square_kernel, "square", [(2 * W, ROWS), (8, 1, ROWS + REL)], [VM] * 4)(rel, s0, got1, got23)
     sq = exchange(sq, DIM)
-    new_re, new_im, new_acc, rel = call(
-        update_kernel, "update", [(W, ROWS), (W, ROWS), (1, ROWS), (64, W + 1, 128)], [VM] * 8
-    )(sq, tot, ent, ent_re, ent_im, ent_acc.reshape(1, ROWS), piece, pacc)
-    rel = exchange(rel, DOM)
-    new_rel_re, new_rel_im, new_rel_acc = call(
-        unpack_kernel, "unpack", [(W, REL), (W, REL), (32, 128)], [VM]
-    )(rel)
+    new_re, new_im, new_acc, new_rel_re, new_rel_im, new_rel_acc = call(
+        update_kernel, "update", [(W, ROWS), (W, ROWS), (1, ROWS), (W, REL), (W, REL), (1, REL)], [VM] * 9
+    )(sq, rel, ent, ent_re, ent_im, ent_acc.reshape(1, ROWS), rel_re, rel_im, rel_acc.reshape(1, REL))
     return new_re, new_im, new_acc.reshape(ROWS), new_rel_re, new_rel_im, new_rel_acc.reshape(REL)
 
 

time: 170 us -> 164 us (0.965)
  the two profiles are of different devices: /device:TPU:14 before, /device:TPU:1 now
where the time goes in v2:
time: 164 us; the launch traced here: 163 us
  blocking collectives  57.2 us (35%)
  starting transfers between devices  57 us (35%)
  waiting for transfers between devices  34.3 us (21%)
  Pallas kernels  9.12 us (6%)
  local copies, waits for them, and re-layouts  3.61 us (2%)
    all_to_all x5, blocking collectives, exchange(): return lax.all_to_all(pieces, axes, 0, 0)  57.2 us
    ppermute x5, starting transfers between devices, shift(): lax.ppermute(block, DOM, [(i, (i + distance) % 64) for i in range(64)])  35.4 us
    ppermute x5, waiting for transfers between devices, shift(): lax.ppermute(block, DOM, [(i, (i + distance) % 64) for i in range(64)])  19.2 us
    all_to_all x2, starting transfers between devices, exchange(): return lax.all_to_all(pieces, axes, 0, 0)  9.85 us
    all_to_all x2, waiting for transfers between devices, exchange(): return lax.all_to_all(pieces, axes, 0, 0)  7.27 us
    ppermute x1, starting transfers between devices, per_device(): w_other = lax.ppermute(w_mine, 'core', SWAP)  5.66 us
    ppermute x1, waiting for transfers between devices, per_device(): lax.ppermute(half, 'yh', SWAP)  5.53 us
    unnamed x26, local copies, waits for them, and re-layouts  3.44 us
  transfers between devices with their start and end apart: 10, of which 9 were waited for; matrix products, arithmetic and copies ran while one was open for 0% of the time, Pallas kernels for 1%

profile of v2, /device:TPU:1, one launch (start us, length us, event | category | flops | bytes accessed | tf_op | source)
XLA Modules:
  0.0 163.1 jit_solution(6343634133940012467)
XLA Ops:
  0.6 0.0 copy-start
  0.6 0.0 copy-start.5
  0.7 0.0 copy-start.6
  0.7 0.9 pad_maximum_fusion.b0
  1.6 0.0 copy-start.12
  1.6 8.4 %collective-permute-start.2 = (f32[50,512]{1,0:T(8,128)S(1)}, f32[50,512]{1,0:T(8,128)S(1)}, u32[]{:S(2)}, u32[]{:S(2)}) collective-permute-start(f32[50,512]{1,0:T(8,128)S(1)} %pad_maximum_fusion.b0), channel_id=1, source_target_pairs={{0,24},{8,32},{16,40},{24,48},{32,56},{40,64},{48,72},{56,80},{64,... | collective-permute-start | bytes 307208 | tf_op jit(solution)/shard_map/ppermute | solution.py:243
  10.1 6.1 %collective-permute-start.1 = (f32[50,512]{1,0:T(8,128)S(1)}, f32[50,512]{1,0:T(8,128)S(1)}, u32[]{:S(2)}, u32[]{:S(2)}) collective-permute-start(f32[50,512]{1,0:T(8,128)S(1)} %pad_maximum_fusion.b0), channel_id=1, source_target_pairs={{0,16},{8,24},{16,32},{24,40},{32,48},{40,56},{48,64},{56,72},{64,... | collective-permute-start | bytes 307208 | tf_op jit(solution)/shard_map/ppermute | solution.py:243
  16.2 3.1 %collective-permute-start = (f32[50,512]{1,0:T(8,128)S(1)}, f32[50,512]{1,0:T(8,128)S(1)}, u32[]{:S(2)}, u32[]{:S(2)}) collective-permute-start(f32[50,512]{1,0:T(8,128)S(1)} %pad_maximum_fusion.b0), channel_id=1, source_target_pairs={{0,8},{8,16},{16,24},{24,32},{32,40},{40,48},{48,56},{56,64},{64,7... | collective-permute-start | bytes 307208 | tf_op jit(solution)/shard_map/ppermute | solution.py:243
  19.3 0.0 copy-done.12
  19.3 0.0 copy-start.9
  19.3 0.0 copy-start.10
  19.3 0.0 copy-done.5
  19.4 0.0 copy-done.6
  19.4 0.6 copy-done.9
  20.0 0.0 copy-done.10
  20.0 0.0 copy-start.1
  20.0 1.0 copy-done.1
  21.0 0.0 copy-start.3
  21.1 1.0 copy-done.3
  22.1 1.1 query.1
  23.2 0.1 pad_add_fusion.info
  23.3 0.0 copy-start.8
  23.3 1.3 collective-permute-done.2.b3
  24.6 10.5 %collective-permute-done.1.b2 = f32[50,512]{1,0:T(8,128)S(1)} collective-permute-done((f32[50,512]{1,0:T(8,128)S(1)}, f32[50,512]{1,0:T(8,128)S(1)}, u32[]{:S(2)}, u32[]{:S(2)}) %collective-permute-start.1) | collective-permute-done | bytes 102432 | tf_op jit(solution)/shard_map/ppermute | solution.py:243
  35.1 0.8 collective-permute-done.b1
  36.0 0.0 copy-done.8
  36.0 1.2 score.1
  37.2 3.1 %collective-permute-start.3 = (f32[4,32,512]{2,1,0:T(8,128)S(1)}, f32[4,32,512]{2,1,0:T(8,128)S(1)}, u32[]{:S(2)}, u32[]{:S(2)}) collective-permute-start(f32[4,32,512]{2,1,0:T(8,128)S(1)} %get-tuple-element.28), channel_id=1, source_target_pairs={{0,1},{1,0},{2,3},{3,2},{4,5},{5,4},{6,7},{7,6},{8,9},{9,8},{10,11... | collective-permute-start | bytes 786440 | tf_op jit(solution)/shard_map/ppermute | solution.py:263
  40.3 1.1 collective-permute-done.3.b
  41.4 0.7 add.18
  42.2 6.4 %all-to-all-start = ((f32[4,32,512]{2,1,0:T(8,128)}), f32[4,32,512]{2,1,0:T(8,128)S(1)}, u32[]{:S(2)}, u32[]{:S(2)}) async-start(f32[4,32,512]{2,1,0:T(8,128)} %add.18), calls=%async_computation | async-start | bytes 524288 | tf_op jit(solution)/shard_map/all_to_all | solution.py:247
  48.5 0.0 copy-done
  48.5 0.1 dynamic-slice_bitcast_fusion
  48.6 0.1 copy.17.rhs
  48.7 7.3 %all-to-all-done.parts = f32[4,32,512]{2,1,0:T(8,128)S(1)} async-done(((f32[4,32,512]{2,1,0:T(8,128)}), f32[4,32,512]{2,1,0:T(8,128)S(1)}, u32[]{:S(2)}, u32[]{:S(2)}) %all-to-all-start) | async-done | bytes 262176 | tf_op jit(solution)/shard_map/all_to_all | solution.py:247
  55.9 0.8 weight.1
  56.8 9.3 %all_to_all.35.w_mine = f32[4,32,512]{2,1,0:T(8,128)S(1)} all-to-all(f32[4,32,512]{2,1,0:T(8,128)S(1)} %weight.1), channel_id=1, replica_groups=mesh['yh'=2,'x'=4,'z'=8,'yl'=4,'core'=2] {'yl'}, dimensions={0} | all-to-all | bytes 524288 | tf_op jit(solution)/shard_map/all_to_all | solution.py:247
  66.1 5.7 %collective-permute-start.4 = (f32[4,32,512]{2,1,0:T(8,128)S(1)}, f32[4,32,512]{2,1,0:T(8,128)S(1)}, u32[]{:S(2)}, u32[]{:S(2)}) collective-permute-start(f32[4,32,512]{2,1,0:T(8,128)S(1)} %all_to_all.35.w_mine), channel_id=1, source_target_pairs={{0,1},{1,0},{2,3},{3,2},{4,5},{5,4},{6,7},{7,6},{8,9},{9,8},{10,11... | collective-permute-start | bytes 786440 | tf_op jit(solution)/shard_map/ppermute | solution.py:267
  71.7 1.1 collective-permute-done.4.w_other
  72.9 1.6 %grad.1 = (f32[50,512]{1,0:T(8,128)S(1)}, f32[50,512]{1,0:T(8,128)S(1)}, f32[100,512]{1,0:T(8,128)S(1)}, f32[4,51,256]{2,1,0:T(8,128)S(1)}) custom-call(s32[2]{0:T(128)S(1)} %pad_add_fusion.info, s32[2]{0:T(128)S(1)} %copy-done.8, f32[64,256]{1,0:T(8,128)S(1)} %get-tuple-element.24.q_r, f32[64,256]{1,0:T(8,128)S(1)} %get-tuple-element.25.head_r, ...), custom_call_target="tpu_custom_call" | custom-call | tf_op jit(solution)/shard_map/grad/pallas_call | solution.py:268
  74.5 8.4 %all_to_all.36.gr = f32[4,51,256]{2,1,0:T(8,128)S(1)} all-to-all(f32[4,51,256]{2,1,0:T(8,128)S(1)} %get-tuple-element.30), channel_id=1, replica_groups=mesh['yh'=2,'x'=4,'z'=8,'yl'=4,'core'=2] {'x'}, dimensions={0} | all-to-all | bytes 417792 | tf_op jit(solution)/shard_map/all_to_all | solution.py:247
  82.9 1.4 place.1
  84.3 11.8 %all_to_all.37.parts = f32[8,50,128]{2,1,0:T(8,128)S(1)} all-to-all(f32[8,50,128]{2,1,0:T(8,128)S(1)} %place.1), channel_id=1, replica_groups=mesh['yh'=2,'x'=4,'z'=8,'yl'=4,'core'=2] {'z'}, dimensions={0} | all-to-all | bytes 409600 | tf_op jit(solution)/shard_map/all_to_all | solution.py:247
  96.2 3.0 %collective-permute-start.5 = (f32[50,128]{1,0:T(8,128)S(1)}, f32[50,128]{1,0:T(8,128)S(1)}, u32[]{:S(2)}, u32[]{:S(2)}) collective-permute-start(f32[50,128]{1,0:T(8,128)S(1)} %fold.1.a), channel_id=1, source_target_pairs={{0,256},{256,0},{1,257},{257,1},{2,258},{258,2},{3,259},{259,3},{4... | collective-permute-start | bytes 76808 | tf_op jit(solution)/shard_map/ppermute | solution.py:278
  99.2 5.5 %collective-permute-done.5.b = f32[50,128]{1,0:T(8,128)S(1)} collective-permute-done((f32[50,128]{1,0:T(8,128)S(1)}, f32[50,128]{1,0:T(8,128)S(1)}, u32[]{:S(2)}, u32[]{:S(2)}) %collective-permute-start.5) | collective-permute-done | bytes 25632 | tf_op jit(solution)/shard_map/ppermute | solution.py:278
  104.7 11.6 %all_to_all.38.a = f32[8,50,128]{2,1,0:T(8,128)S(1)} all-to-all(f32[8,50,128]{2,1,0:T(8,128)S(1)} %both.1), channel_id=1, replica_groups=mesh['yh'=2,'x'=4,'z'=8,'yl'=4,'core'=2] {'z'}, dimensions={0} | all-to-all | bytes 409600 | tf_op jit(solution)/shard_map/all_to_all | solution.py:247
  116.3 1.0 copies.1
  117.3 3.5 %all-to-all-start.5 = ((f32[4,400,128]{2,1,0:T(8,128)}), f32[4,400,128]{2,1,0:T(8,128)S(1)}, u32[]{:S(2)}, u32[]{:S(2)}) async-start(f32[4,400,128]{2,1,0:T(8,128)} %copies.1), calls=%async_computation.5 | async-start | bytes 1638400 | tf_op jit(solution)/shard_map/all_to_all | solution.py:247
  120.8 5.1 %collective-permute-start.6 = (f32[100,512]{1,0:T(8,128)S(1)}, f32[100,512]{1,0:T(8,128)S(1)}, u32[]{:S(2)}, u32[]{:S(2)}) collective-permute-start(f32[100,512]{1,0:T(8,128)S(1)} %get-tuple-element.33), channel_id=1, source_target_pairs={{0,496},{8,504},{16,0},{24,8},{32,16},{40,24},{48,32},{56,40},{64,... | collective-permute-start | bytes 614408 | tf_op jit(solution)/shard_map/ppermute | solution.py:243
  125.8 4.8 %collective-permute-done.6.got23 = f32[100,512]{1,0:T(8,128)S(1)} collective-permute-done((f32[100,512]{1,0:T(8,128)S(1)}, f32[100,512]{1,0:T(8,128)S(1)}, u32[]{:S(2)}, u32[]{:S(2)}) %collective-permute-start.6) | collective-permute-done | bytes 204832 | tf_op jit(solution)/shard_map/ppermute | solution.py:243
  130.6 12.6 %collective-permute-start.7 = (f32[50,512]{1,0:T(8,128)S(1)}, f32[50,512]{1,0:T(8,128)S(1)}, u32[]{:S(2)}, u32[]{:S(2)}) collective-permute-start(f32[50,512]{1,0:T(8,128)S(1)} %slice_add_fusion), channel_id=1, source_target_pairs={{0,504},{8,0},{16,8},{24,16},{32,24},{40,32},{48,40},{56,48},{64,5... | collective-permute-start | bytes 307208 | tf_op jit(solution)/shard_map/ppermute | solution.py:243
  143.3 1.8 %collective-permute-done.7.got1 = f32[50,512]{1,0:T(8,128)S(1)} collective-permute-done((f32[50,512]{1,0:T(8,128)S(1)}, f32[50,512]{1,0:T(8,128)S(1)}, u32[]{:S(2)}, u32[]{:S(2)}) %collective-permute-start.7) | collective-permute-done | bytes 102432 | tf_op jit(solution)/shard_map/ppermute | solution.py:243
  145.0 0.0 all-to-all-done.5.rel
  145.0 0.0 copy-start.2
  145.0 0.0 copy-start.4
  145.0 0.1 square.1
  145.2 0.0 copy-start.7
  145.2 16.1 %all_to_all.39.sq = f32[8,1,4608]{2,1,0:T(1,128)S(1)} all-to-all(f32[8,1,4608]{2,1,0:T(1,128)S(1)} %get-tuple-element.34), channel_id=1, replica_groups=mesh['yh'=2,'x'=4,'z'=8,'yl'=4,'core'=2] {'yl','core'}, dimensions={0} | all-to-all | bytes 294912 | tf_op jit(solution)/shard_map/all_to_all | solution.py:247
  161.3 0.0 copy-start.11
  161.3 0.0 copy-done.2
  161.3 0.0 copy-done.4
  161.3 0.0 copy-done.7
  161.3 0.7 copy-done.11
  162.0 1.1 update.1
  (4 shorter events, 0.1 us)
Async XLA Ops:
  0.6 47.9 %copy-start = (s32[2,128]{1,0:T(2,128)S(1)}, s32[2,128]{1,0:T(2,128)}, u32[]{:S(2)}) copy-start(s32[2,128]{1,0:T(2,128)} %param.18) | copy-start | bytes 3076
  0.6 18.7 %copy-start.5 = (f32[25,512]{1,0:T(8,128)S(1)}, f32[25,512]{1,0:T(8,128)}, u32[]{:S(2)}) copy-start(f32[25,512]{1,0:T(8,128)} %ent_re.3) | copy-start | bytes 153604
  0.7 18.7 %copy-start.6 = (f32[25,512]{1,0:T(8,128)S(1)}, f32[25,512]{1,0:T(8,128)}, u32[]{:S(2)}) copy-start(f32[25,512]{1,0:T(8,128)} %ent_im.3) | copy-start | bytes 153604
  1.6 17.7 %copy-start.12 = (s32[2,1000]{1,0:T(2,128)S(1)}, s32[2,1000]{1,0:T(2,128)}, u32[]{:S(2)}) copy-start(s32[2,1000]{1,0:T(2,128)} %param.20) | copy-start | bytes 24004
  1.6 23.0 %collective-permute-start.2 = (f32[50,512]{1,0:T(8,128)S(1)}, f32[50,512]{1,0:T(8,128)S(1)}, u32[]{:S(2)}, u32[]{:S(2)}) collective-permute-start(f32[50,512]{1,0:T(8,128)S(1)} %pad_maximum_fusion.b0), channel_id=1, source_target_pairs={{0,24},{8,32},{16,40},{24,48},{32,56},{40,64},{48,72},{56,80},{64,... | collective-permute-start | bytes 307208 | tf_op jit(solution)/shard_map/ppermute | solution.py:243
  10.1 25.1 %collective-permute-start.1 = (f32[50,512]{1,0:T(8,128)S(1)}, f32[50,512]{1,0:T(8,128)S(1)}, u32[]{:S(2)}, u32[]{:S(2)}) collective-permute-start(f32[50,512]{1,0:T(8,128)S(1)} %pad_maximum_fusion.b0), channel_id=1, source_target_pairs={{0,16},{8,24},{16,32},{24,40},{32,48},{40,56},{48,64},{56,72},{64,... | collective-permute-start | bytes 307208 | tf_op jit(solution)/shard_map/ppermute | solution.py:243
  16.2 19.8 %collective-permute-start = (f32[50,512]{1,0:T(8,128)S(1)}, f32[50,512]{1,0:T(8,128)S(1)}, u32[]{:S(2)}, u32[]{:S(2)}) collective-permute-start(f32[50,512]{1,0:T(8,128)S(1)} %pad_maximum_fusion.b0), channel_id=1, source_target_pairs={{0,8},{8,16},{16,24},{24,32},{32,40},{40,48},{48,56},{56,64},{64,7... | collective-permute-start | bytes 307208 | tf_op jit(solution)/shard_map/ppermute | solution.py:243
  19.3 0.7 copy-start.9
  19.3 0.7 copy-start.10
  20.0 1.0 copy-start.1
  21.0 1.0 copy-start.3
  23.3 12.7 %copy-start.8 = (s32[2]{0:T(128)S(1)}, s32[2]{0:T(128)}, u32[]{:S(2)}) copy-start(s32[2]{0:T(128)} %bucket.5) | copy-start | bytes 28
  37.2 4.3 %collective-permute-start.3 = (f32[4,32,512]{2,1,0:T(8,128)S(1)}, f32[4,32,512]{2,1,0:T(8,128)S(1)}, u32[]{:S(2)}, u32[]{:S(2)}) collective-permute-start(f32[4,32,512]{2,1,0:T(8,128)S(1)} %get-tuple-element.28), channel_id=1, source_target_pairs={{0,1},{1,0},{2,3},{3,2},{4,5},{5,4},{6,7},{7,6},{8,9},{9,8},{10,11... | collective-permute-start | bytes 786440 | tf_op jit(solution)/shard_map/ppermute | solution.py:263
  42.2 13.8 %all-to-all-start = ((f32[4,32,512]{2,1,0:T(8,128)}), f32[4,32,512]{2,1,0:T(8,128)S(1)}, u32[]{:S(2)}, u32[]{:S(2)}) async-start(f32[4,32,512]{2,1,0:T(8,128)} %add.18), calls=%async_computation | async-start | bytes 524288 | tf_op jit(solution)/shard_map/all_to_all | solution.py:247
  66.1 6.8 %collective-permute-start.4 = (f32[4,32,512]{2,1,0:T(8,128)S(1)}, f32[4,32,512]{2,1,0:T(8,128)S(1)}, u32[]{:S(2)}, u32[]{:S(2)}) collective-permute-start(f32[4,32,512]{2,1,0:T(8,128)S(1)} %all_to_all.35.w_mine), channel_id=1, source_target_pairs={{0,1},{1,0},{2,3},{3,2},{4,5},{5,4},{6,7},{7,6},{8,9},{9,8},{10,11... | collective-permute-start | bytes 786440 | tf_op jit(solution)/shard_map/ppermute | solution.py:267
  96.2 8.5 %collective-permute-start.5 = (f32[50,128]{1,0:T(8,128)S(1)}, f32[50,128]{1,0:T(8,128)S(1)}, u32[]{:S(2)}, u32[]{:S(2)}) collective-permute-start(f32[50,128]{1,0:T(8,128)S(1)} %fold.1.a), channel_id=1, source_target_pairs={{0,256},{256,0},{1,257},{257,1},{2,258},{258,2},{3,259},{259,3},{4... | collective-permute-start | bytes 76808 | tf_op jit(solution)/shard_map/ppermute | solution.py:278
  117.3 27.8 %all-to-all-start.5 = ((f32[4,400,128]{2,1,0:T(8,128)}), f32[4,400,128]{2,1,0:T(8,128)S(1)}, u32[]{:S(2)}, u32[]{:S(2)}) async-start(f32[4,400,128]{2,1,0:T(8,128)} %copies.1), calls=%async_computation.5 | async-start | bytes 1638400 | tf_op jit(solution)/shard_map/all_to_all | solution.py:247
  120.8 9.8 %collective-permute-start.6 = (f32[100,512]{1,0:T(8,128)S(1)}, f32[100,512]{1,0:T(8,128)S(1)}, u32[]{:S(2)}, u32[]{:S(2)}) collective-permute-start(f32[100,512]{1,0:T(8,128)S(1)} %get-tuple-element.33), channel_id=1, source_target_pairs={{0,496},{8,504},{16,0},{24,8},{32,16},{40,24},{48,32},{56,40},{64,... | collective-permute-start | bytes 614408 | tf_op jit(solution)/shard_map/ppermute | solution.py:243
  130.6 14.4 %collective-permute-start.7 = (f32[50,512]{1,0:T(8,128)S(1)}, f32[50,512]{1,0:T(8,128)S(1)}, u32[]{:S(2)}, u32[]{:S(2)}) collective-permute-start(f32[50,512]{1,0:T(8,128)S(1)} %slice_add_fusion), channel_id=1, source_target_pairs={{0,504},{8,0},{16,8},{24,16},{32,24},{40,32},{48,40},{56,48},{64,5... | collective-permute-start | bytes 307208 | tf_op jit(solution)/shard_map/ppermute | solution.py:243
  145.0 16.3 %copy-start.2 = (f32[25,4096]{1,0:T(8,128)S(1)}, f32[25,4096]{1,0:T(8,128)}, u32[]{:S(2)}) copy-start(f32[25,4096]{1,0:T(8,128)} %rel_re.3) | copy-start | bytes 1228804
  145.0 16.3 %copy-start.4 = (f32[25,4096]{1,0:T(8,128)S(1)}, f32[25,4096]{1,0:T(8,128)}, u32[]{:S(2)}) copy-start(f32[25,4096]{1,0:T(8,128)} %rel_im.3) | copy-start | bytes 1228804
  145.2 16.1 %copy-start.7 = (f32[4096]{0:T(1024)S(1)}, f32[4096]{0:T(1024)}, u32[]{:S(2)}) copy-start(f32[4096]{0:T(1024)} %param.16) | copy-start | bytes 49156
  161.3 0.7 copy-start.11

commit v3 on v2

--- a/solution.py
+++ b/solution.py
@@ -77,7 +77,7 @@
     return jnp.concatenate([ref[0:1, :], ref[1:2, :]], 1)
 
 
-def query_kernel(ent_re, ent_im, rel_re, rel_im, lhs, rel_ids, neg, head_o, relc_o, q_o, m_o):
+def query_kernel(info, ent_re, ent_im, rel_re, rel_im, lhs, rhs, rel_ids, neg, head_o, relc_o, q_o, m_o, hit_o):
     own = jnp.concatenate([pad32(ent_re[...]), pad32(ent_im[...])], 0)
     head = join3(nn(split3(own), onehot_rows(edge_ids(lhs), ROWS)))
     ids = edge_ids(rel_ids)
@@ -92,9 +92,11 @@
     h_re, h_im = head[:32], head[32:]
     r_re, r_im = relc[:32], relc[32:]
     q_o[...] = jnp.concatenate([h_re * r_re - h_im * r_im, h_re * r_im + h_im * r_re], 0)
+    first = info[0] == 0
     ones = jnp.ones((16, neg.shape[1]), BF16)
-    for c in range(2):
-        m_o[8 * c : 8 * c + 8, :] = nt(ones, onehot_rows(neg[c : c + 1, :], ROWS))[:8]
+    m_o[...] = nt(ones, onehot_rows(jnp.where(first, neg[0:1, :], neg[1:2, :]), ROWS))[:8]
+    ids = jnp.where(first, rhs[0:1, :], rhs[1:2, :])
+    hit_o[...] = jnp.transpose(jnp.where(iota((ROWS, CH), 0) == ids, 1.0, 0.0))
 
 
 def choose(step, blocks):
@@ -121,14 +123,13 @@
     o[...] = a[...] + b[...]
 
 
-def weight_kernel(info, bucket, parts, m_r, rhs, w_o):
+def weight_kernel(info, bucket, parts, m_r, hit_r, w_o):
     s = parts[0]
     for i in range(1, 4):
         s = s + parts[i]
-    core = info[0]
-    m = jnp.where(core == 0, m_r[0:1, :], m_r[8:9, :])
-    live = jnp.where(jnp.where(core == 0, bucket[0], bucket[1]) < STEPS, 1.0, 0.0)
-    hit = iota(s.shape, 1) == rhs[...]
+    m = m_r[0:1, :]
+    live = jnp.where(jnp.where(info[0] == 0, bucket[0], bucket[1]) < STEPS, 1.0, 0.0)
+    hit = hit_r[pl.ds(pl.multiple_of(info[2] * 32, 32), 32), :] > 0.5
     pos = jnp.sum(jnp.where(hit, s, 0.0), 1, keepdims=True)
     masked = jnp.where(m > 0.0, s, -1e30)
     top = jnp.maximum(jnp.max(masked, 1, keepdims=True), pos)
@@ -141,7 +142,7 @@
         w_o[i] = w
 
 
-def grad_kernel(info, bucket, q_r, head_r, relc_r, w_mine, w_other, b0, b1, b2, b3, lhs, rel_ids, s0_o, s1_o, s23_o, gr_o):
+def grad_kernel(info, bucket, q_r, head_r, relc_r, w_mine, w_other, b0, b1, b2, b3, lhs, rel_ids, s0_o, s1_o, s2_o, s3_o, gr_o):
     core = info[0]
     mine = w_mine[...].reshape(CH, ROWS)
     other = w_other[...].reshape(CH, ROWS)
@@ -169,9 +170,9 @@
         gr_o[i, 0:W, :] = gr_re
         gr_o[i, W : 2 * W, :] = gr_im
         gr_o[i, 2 * W : 2 * W + 1, :] = ids
-    for ref, at, slot in ((s0_o, 0, 0), (s1_o, 0, 1), (s23_o, 0, 3), (s23_o, 2 * W, 2)):
-        ref[at : at + W, :] = slots[slot][:W]
-        ref[at + W : at + 2 * W, :] = slots[slot][32 : 32 + W]
+    for ref, slot in zip((s0_o, s1_o, s2_o, s3_o), slots):
+        ref[0:W, :] = slot[:W]
+        ref[W : 2 * W, :] = slot[32 : 32 + W]
 
 
 def place_kernel(info, gr, out):
@@ -197,24 +198,18 @@
 
 def both_kernel(a, b, out):
     tot = a[...] + b[...]
-    for z in range(8):
-        out[z] = tot
-
-
-def copies_kernel(a, out):
-    for x in range(4):
-        for z in range(8):
-            out[x, 2 * W * z : 2 * W * z + 2 * W, :] = a[z]
-
-
-def square_kernel(rel, s0, got1, got23, ent_o, sq_o):
-    ent = s0[...] + (got1[...] + got23[2 * W : 4 * W, :])
+    for i in range(32):
+        out[i] = tot
+
+
+def square_kernel(rel, s0, got1, got2, got3, ent_o, sq_o):
+    ent = s0[...] + (got1[...] + (got2[...] + got3[...]))
     ent_o[...] = ent
     es = jnp.sum(ent * ent, 0, keepdims=True)
     for i in range(8):
         sq_o[i, :, 0:ROWS] = es
     for t in range(32):
-        tot = rel[t // 8, 2 * W * (t % 8) : 2 * W * (t % 8) + 2 * W, :]
+        tot = rel[t]
         rs = jnp.sum(tot * tot, 0, keepdims=True)
         for i in range(8):
             sq_o[i, :, ROWS + 128 * t : ROWS + 128 * t + 128] = rs
@@ -234,7 +229,7 @@
     scale = LEARN_RATE / jnp.sqrt(acc)
     for t in range(32):
         at = slice(128 * t, 128 * t + 128)
-        tot = rel[t // 8, 2 * W * (t % 8) : 2 * W * (t % 8) + 2 * W, :]
+        tot = rel[t]
         rre_o[:, at] = rel_re[:, at] - scale[:, at] * tot[:W]
         rim_o[:, at] = rel_im[:, at] - scale[:, at] * tot[W:]
 
@@ -248,37 +243,32 @@
 
 
 def per_device(ent_re, ent_im, ent_acc, rel_re, rel_im, rel_acc, lhs_rows, rhs_rows, rel_ids, neg_rows, bucket_step):
-    core = lax.axis_index("core")
-    yl = lax.axis_index("yl")
-    info = jnp.stack([core, lax.axis_index("x")]).astype(I32)
+    info = jnp.stack([lax.axis_index("core"), lax.axis_index("x"), lax.axis_index("yl")]).astype(I32)
     own = jnp.concatenate([ent_re, ent_im], 0)
     b1, b2, b3 = [shift(own, d) for d in (1, 2, 3)]
     neg = jnp.pad(neg_rows, ((0, 0), (0, 24)), constant_values=-1)
-    rhs = lax.dynamic_slice(rhs_rows, (core, 32 * yl), (1, 32)).reshape(32, 1)
-    head, relc, q, m = call(
-        query_kernel, "query", [(64, 256), (64, 256), (64, 256), (16, ROWS)], [VM] * 7,
-    )(ent_re, ent_im, rel_re, rel_im, lhs_rows, rel_ids, neg)
+    head, relc, q, m, hit = call(
+        query_kernel, "query", [(64, 256), (64, 256), (64, 256), (8, ROWS), (CH, ROWS)], [SM] + [VM] * 8,
+    )(info, ent_re, ent_im, rel_re, rel_im, lhs_rows, rhs_rows, rel_ids, neg)
     quarter = (4, 32, ROWS)
+    block = (2 * W, ROWS)
     keep, send = call(score_kernel, "score", [quarter, quarter], [SM, SM] + [VM] * 5)(info, bucket_step, q, own, b1, b2, b3)
     s = call(add_kernel, "add", quarter, [VM] * 2)(keep, lax.ppermute(send, "core", SWAP))
     s = exchange(s, "yl")
-    w = call(weight_kernel, "weight", quarter, [SM, SM] + [VM] * 3)(info, bucket_step, s, m, rhs)
+    w = call(weight_kernel, "weight", quarter, [SM, SM] + [VM] * 3)(info, bucket_step, s, m, hit)
     w_mine = exchange(w, "yl")
     w_other = lax.ppermute(w_mine, "core", SWAP)
-    s0, s1, s23, gr = call(
-        grad_kernel, "grad",
-        [(2 * W, ROWS), (2 * W, ROWS), (4 * W, ROWS), (4, 2 * W + 1, 256)], [SM, SM] + [VM] * 11,
+    s0, s1, s2, s3, gr = call(
+        grad_kernel, "grad", [block, block, block, block, (4, 2 * W + 1, 256)], [SM, SM] + [VM] * 11,
     )(info, bucket_step, q, head, relc, w_mine, w_other, own, b1, b2, b3, lhs_rows, rel_ids)
-    got23 = shift(s23, -2)
+    got = [shift(s1, -1), shift(s2, -2), shift(s3, -3)]
     gr = exchange(gr, "x")
     pieces = call(place_kernel, "place", (8, 2 * W, 128), [SM, VM])(info, gr)
-    got1 = shift(s1 + got23[: 2 * W], -1)
-    pieces = exchange(pieces, "z")
-    half = call(fold_kernel, "fold", (2 * W, 128), [VM])(pieces)
-    rel = call(both_kernel, "both", (8, 2 * W, 128), [VM] * 2)(half, lax.ppermute(half, "yh", SWAP))
-    rel = exchange(rel, "z")
-    rel = exchange(call(copies_kernel, "copies", (4, 16 * W, 128), [VM])(rel), "x")
-    ent, sq = call(square_kernel, "square", [(2 * W, ROWS), (8, 1, ROWS + REL)], [VM] * 4)(rel, s0, got1, got23)
+    half = call(fold_kernel, "fold", (2 * W, 128), [VM])(exchange(pieces, "z"))
+    twin, got = lax.optimization_barrier((lax.ppermute(half, "yh", SWAP), got))
+    rel = call(both_kernel, "both", (32, 2 * W, 128), [VM] * 2)(half, twin)
+    rel = exchange(rel, ("x", "z"))
+    ent, sq = call(square_kernel, "square", [block, (8, 1, ROWS + REL)], [VM] * 5)(rel, s0, *got)
     sq = exchange(sq, DIM)
     new_re, new_im, new_acc, new_rel_re, new_rel_im, new_rel_acc = call(
         update_kernel, "update", [(W, ROWS), (W, ROWS), (1, ROWS), (W, REL), (W, REL), (1, REL)], [VM] * 9

time: 164 us -> 163 us (level)
  blocking collectives: 57.2 us -> 78.8 us
  waiting for transfers between devices: 34.3 us -> 20.2 us
  starting transfers between devices: 57 us -> 49 us
    all_to_all x5, blocking collectives: 57.2 us -> 78.8 us  [exchange(): return lax.all_to_all(pieces, axes, 0, 0)]
    all_to_all x2 -> x1, waiting for transfers between devices: 7.27 us -> 0.01 us  [exchange(): return lax.all_to_all(pieces, axes, 0, 0)]
    all_to_all x2 -> x1, starting transfers between devices: 9.85 us -> 3.4 us  [exchange(): return lax.all_to_all(pieces, axes, 0, 0)]
    ppermute x5 -> x6, starting transfers between devices: 35.4 us -> 30.6 us  [shift(): lax.ppermute(block, DOM, [(i, (i + distance) % 64) for i in range(64)])]
    ppermute x1, waiting for transfers between devices: 5.53 us -> 1.65 us  [per_device(): twin, got = lax.optimization_barrier((lax.ppermute(half, 'yh', SWAP), got))]
    ppermute x1, starting transfers between devices: 2.98 us -> 6.21 us  [per_device(): twin, got = lax.optimization_barrier((lax.ppermute(half, 'yh', SWAP), got))]
    ppermute x5 -> x6, waiting for transfers between devices: 19.2 us -> 16.2 us  [shift(): lax.ppermute(block, DOM, [(i, (i + distance) % 64) for i in range(64)])]
    pallas_call x6 -> x5, Pallas kernels: 3.89 us -> 3.35 us  [the longest x1 1.61 us: per_device(): call(grad_kernel, 'grad', [block, block, block, block, (4, 2 * W + 1, 256...]
  transfers between devices with their start and end apart: 10 -> 10, of which waited for: 9 -> 7; matrix products, arithmetic and copies ran while one was open for 0% -> 0% of each run, Pallas kernels for 1% -> 1%
where the time goes in v3:
time: 163 us; the launch traced here: 162 us
  blocking collectives  78.8 us (48%)
  starting transfers between devices  49 us (30%)
  waiting for transfers between devices  20.2 us (12%)
  Pallas kernels  8.52 us (5%)
  local copies, waits for them, and re-layouts  4.08 us (3%)
    all_to_all x5, blocking collectives, exchange(): return lax.all_to_all(pieces, axes, 0, 0)  78.8 us
    ppermute x6, starting transfers between devices, shift(): lax.ppermute(block, DOM, [(i, (i + distance) % 64) for i in range(64)])  30.6 us
    ppermute x6, waiting for transfers between devices, shift(): lax.ppermute(block, DOM, [(i, (i + distance) % 64) for i in range(64)])  16.2 us
    ppermute x1, starting transfers between devices, per_device(): twin, got = lax.optimization_barrier((lax.ppermute(half, 'yh', SWAP), got))  6.21 us
    ppermute x1, starting transfers between devices, per_device(): w_other = lax.ppermute(w_mine, 'core', SWAP)  5.66 us
    unnamed x26, local copies, waits for them, and re-layouts  4.08 us
    all_to_all x1, starting transfers between devices, exchange(): return lax.all_to_all(pieces, axes, 0, 0)  3.4 us
  transfers between devices with their start and end apart: 10, of which 7 were waited for; matrix products, arithmetic and copies ran while one was open for 0% of the time, Pallas kernels for 1%

profile of v3, /device:TPU:1, one launch (start us, length us, event | category | flops | bytes accessed | tf_op | source)
XLA Modules:
  0.0 162.4 jit_solution(6884117510403796111)
XLA Ops:
  0.6 0.0 copy-start.4
  0.6 0.0 copy-start.5
  0.7 0.9 pad_maximum_fusion.b0
  1.6 8.4 %collective-permute-start.2 = (f32[50,512]{1,0:T(8,128)S(1)}, f32[50,512]{1,0:T(8,128)S(1)}, u32[]{:S(2)}, u32[]{:S(2)}) collective-permute-start(f32[50,512]{1,0:T(8,128)S(1)} %pad_maximum_fusion.b0), channel_id=1, source_target_pairs={{0,24},{8,32},{16,40},{24,48},{32,56},{40,64},{48,72},{56,80},{64,... | collective-permute-start | bytes 307208 | tf_op jit(solution)/shard_map/ppermute | solution.py:238
  10.0 6.1 %collective-permute-start.1 = (f32[50,512]{1,0:T(8,128)S(1)}, f32[50,512]{1,0:T(8,128)S(1)}, u32[]{:S(2)}, u32[]{:S(2)}) collective-permute-start(f32[50,512]{1,0:T(8,128)S(1)} %pad_maximum_fusion.b0), channel_id=1, source_target_pairs={{0,16},{8,24},{16,32},{24,40},{32,48},{40,56},{48,64},{56,72},{64,... | collective-permute-start | bytes 307208 | tf_op jit(solution)/shard_map/ppermute | solution.py:238
  16.2 3.1 %collective-permute-start = (f32[50,512]{1,0:T(8,128)S(1)}, f32[50,512]{1,0:T(8,128)S(1)}, u32[]{:S(2)}, u32[]{:S(2)}) collective-permute-start(f32[50,512]{1,0:T(8,128)S(1)} %pad_maximum_fusion.b0), channel_id=1, source_target_pairs={{0,8},{8,16},{16,24},{24,32},{32,40},{40,48},{48,56},{56,64},{64,7... | collective-permute-start | bytes 307208 | tf_op jit(solution)/shard_map/ppermute | solution.py:238
  19.3 0.0 copy-start.12
  19.3 0.7 copy-done.12
  20.0 0.0 copy-start.11
  20.0 0.0 copy-start.8
  20.0 0.0 copy-start.9
  20.0 0.1 pad_add_fusion.info
  20.1 0.0 copy-done.4
  20.1 0.0 copy-done.5
  20.1 0.6 copy-done.11
  20.7 0.0 copy-done.8
  20.7 0.0 copy-done.9
  20.7 0.0 copy-start
  20.7 1.0 copy-done
  21.7 0.0 copy-start.2
  21.7 1.0 copy-done.2
  22.8 1.5 query.1
  24.3 0.0 copy-start.7
  24.3 0.3 collective-permute-done.2.b3
  24.6 10.5 %collective-permute-done.1.b2 = f32[50,512]{1,0:T(8,128)S(1)} collective-permute-done((f32[50,512]{1,0:T(8,128)S(1)}, f32[50,512]{1,0:T(8,128)S(1)}, u32[]{:S(2)}, u32[]{:S(2)}) %collective-permute-start.1) | collective-permute-done | bytes 102432 | tf_op jit(solution)/shard_map/ppermute | solution.py:238
  35.1 0.8 collective-permute-done.b1
  35.9 0.0 copy-done.7
  36.0 1.2 score.1
  37.1 3.1 %collective-permute-start.3 = (f32[4,32,512]{2,1,0:T(8,128)S(1)}, f32[4,32,512]{2,1,0:T(8,128)S(1)}, u32[]{:S(2)}, u32[]{:S(2)}) collective-permute-start(f32[4,32,512]{2,1,0:T(8,128)S(1)} %get-tuple-element.34), channel_id=1, source_target_pairs={{0,1},{1,0},{2,3},{3,2},{4,5},{5,4},{6,7},{7,6},{8,9},{9,8},{10,11... | collective-permute-start | bytes 786440 | tf_op jit(solution)/shard_map/ppermute | solution.py:256
  40.3 1.1 collective-permute-done.3.b
  41.4 13.2 %all_to_all.30.parts = f32[4,32,512]{2,1,0:T(8,128)S(1)} all-to-all(f32[4,32,512]{2,1,0:T(8,128)S(1)} %add.7), channel_id=1, replica_groups=mesh['yh'=2,'x'=4,'z'=8,'yl'=4,'core'=2] {'yl'}, dimensions={0} | all-to-all | bytes 524288 | tf_op jit(solution)/shard_map/all_to_all | solution.py:242
  54.6 0.8 weight.1
  55.4 10.0 %all_to_all.31.w_mine = f32[4,32,512]{2,1,0:T(8,128)S(1)} all-to-all(f32[4,32,512]{2,1,0:T(8,128)S(1)} %weight.1), channel_id=1, replica_groups=mesh['yh'=2,'x'=4,'z'=8,'yl'=4,'core'=2] {'yl'}, dimensions={0} | all-to-all | bytes 524288 | tf_op jit(solution)/shard_map/all_to_all | solution.py:242
  65.4 5.7 %collective-permute-start.4 = (f32[4,32,512]{2,1,0:T(8,128)S(1)}, f32[4,32,512]{2,1,0:T(8,128)S(1)}, u32[]{:S(2)}, u32[]{:S(2)}) collective-permute-start(f32[4,32,512]{2,1,0:T(8,128)S(1)} %all_to_all.31.w_mine), channel_id=1, source_target_pairs={{0,1},{1,0},{2,3},{3,2},{4,5},{5,4},{6,7},{7,6},{8,9},{9,8},{10,11... | collective-permute-start | bytes 786440 | tf_op jit(solution)/shard_map/ppermute | solution.py:260
  71.0 1.1 collective-permute-done.4.w_other
  72.2 1.6 grad.1
  73.8 8.4 %all_to_all.32.gr = f32[4,51,256]{2,1,0:T(8,128)S(1)} all-to-all(f32[4,51,256]{2,1,0:T(8,128)S(1)} %get-tuple-element.37), channel_id=1, replica_groups=mesh['yh'=2,'x'=4,'z'=8,'yl'=4,'core'=2] {'x'}, dimensions={0} | all-to-all | bytes 417792 | tf_op jit(solution)/shard_map/all_to_all | solution.py:242
  82.2 2.1 %place.1 = f32[8,50,128]{2,1,0:T(8,128)} custom-call(s32[3]{0:T(128)S(1)} %pad_add_fusion.info, f32[4,51,256]{2,1,0:T(8,128)S(1)} %all_to_all.32.gr), custom_call_target="tpu_custom_call" | custom-call | tf_op jit(solution)/shard_map/place/pallas_call | solution.py:266
  84.3 3.4 %all-to-all-start.3 = ((f32[8,50,128]{2,1,0:T(8,128)}), f32[8,50,128]{2,1,0:T(8,128)S(1)}, u32[]{:S(2)}, u32[]{:S(2)}) async-start(f32[8,50,128]{2,1,0:T(8,128)} %place.1), calls=%async_computation.3 | async-start | bytes 458752 | tf_op jit(solution)/shard_map/all_to_all | solution.py:242
  87.7 5.9 %collective-permute-start.6 = (f32[50,512]{1,0:T(8,128)S(1)}, f32[50,512]{1,0:T(8,128)S(1)}, u32[]{:S(2)}, u32[]{:S(2)}) collective-permute-start(f32[50,512]{1,0:T(8,128)S(1)} %get-tuple-element.38), channel_id=1, source_target_pairs={{0,504},{8,0},{16,8},{24,16},{32,24},{40,32},{48,40},{56,48},{64,5... | collective-permute-start | bytes 307208 | tf_op jit(solution)/shard_map/ppermute | solution.py:238
  93.6 4.0 %collective-permute-start.7 = (f32[50,512]{1,0:T(8,128)S(1)}, f32[50,512]{1,0:T(8,128)S(1)}, u32[]{:S(2)}, u32[]{:S(2)}) collective-permute-start(f32[50,512]{1,0:T(8,128)S(1)} %get-tuple-element.39), channel_id=1, source_target_pairs={{0,496},{8,504},{16,0},{24,8},{32,16},{40,24},{48,32},{56,40},{64,... | collective-permute-start | bytes 307208 | tf_op jit(solution)/shard_map/ppermute | solution.py:238
  97.6 3.1 %collective-permute-start.8 = (f32[50,512]{1,0:T(8,128)S(1)}, f32[50,512]{1,0:T(8,128)S(1)}, u32[]{:S(2)}, u32[]{:S(2)}) collective-permute-start(f32[50,512]{1,0:T(8,128)S(1)} %get-tuple-element.40), channel_id=1, source_target_pairs={{0,488},{8,496},{16,504},{24,0},{32,8},{40,16},{48,24},{56,32},{64... | collective-permute-start | bytes 307208 | tf_op jit(solution)/shard_map/ppermute | solution.py:238
  100.7 0.0 all-to-all-done.3.parts
  100.7 6.2 %collective-permute-start.5 = (f32[50,128]{1,0:T(8,128)S(1)}, f32[50,128]{1,0:T(8,128)S(1)}, u32[]{:S(2)}, u32[]{:S(2)}) collective-permute-start(f32[50,128]{1,0:T(8,128)S(1)} %fold.1.a), channel_id=1, source_target_pairs={{0,256},{256,0},{1,257},{257,1},{2,258},{258,2},{3,259},{259,3},{4... | collective-permute-start | bytes 76808 | tf_op jit(solution)/shard_map/ppermute | solution.py:268
  107.0 0.0 collective-permute-done.6.got1
  107.0 0.0 collective-permute-done.7.got2
  107.0 4.6 %collective-permute-done.8.got3 = f32[50,512]{1,0:T(8,128)S(1)} collective-permute-done((f32[50,512]{1,0:T(8,128)S(1)}, f32[50,512]{1,0:T(8,128)S(1)}, u32[]{:S(2)}, u32[]{:S(2)}) %collective-permute-start.8) | collective-permute-done | bytes 102432 | tf_op jit(solution)/shard_map/ppermute | solution.py:238
  111.6 1.7 %collective-permute-done.5.b = f32[50,128]{1,0:T(8,128)S(1)} collective-permute-done((f32[50,128]{1,0:T(8,128)S(1)}, f32[50,128]{1,0:T(8,128)S(1)}, u32[]{:S(2)}, u32[]{:S(2)}) %collective-permute-start.5) | collective-permute-done | bytes 25632 | tf_op jit(solution)/shard_map/ppermute | solution.py:268
  113.2 0.1 both.1
  113.3 28.0 %all_to_all.33.rel = f32[32,50,128]{2,1,0:T(8,128)S(1)} all-to-all(f32[32,50,128]{2,1,0:T(8,128)S(1)} %both.1), channel_id=1, replica_groups=mesh['yh'=2,'x'=4,'z'=8,'yl'=4,'core'=2] {'x','z'}, dimensions={0} | all-to-all | bytes 1638400 | tf_op jit(solution)/shard_map/all_to_all | solution.py:242
  141.3 0.0 copy-start.1
  141.3 0.0 copy-start.3
  141.3 0.1 square.1
  141.4 0.0 copy-start.6
  141.4 19.2 %all_to_all.34.sq = f32[8,1,4608]{2,1,0:T(1,128)S(1)} all-to-all(f32[8,1,4608]{2,1,0:T(1,128)S(1)} %get-tuple-element.46), channel_id=1, replica_groups=mesh['yh'=2,'x'=4,'z'=8,'yl'=4,'core'=2] {'yl','core'}, dimensions={0} | all-to-all | bytes 294912 | tf_op jit(solution)/shard_map/all_to_all | solution.py:242
  160.6 0.0 copy-start.10
  160.6 0.0 copy-done.1
  160.6 0.0 copy-done.3
  160.6 0.0 copy-done.6
  160.6 0.7 copy-done.10
  161.3 1.1 update.1
  (3 shorter events, 0.1 us)
Async XLA Ops:
  0.6 19.5 %copy-start.4 = (f32[25,512]{1,0:T(8,128)S(1)}, f32[25,512]{1,0:T(8,128)}, u32[]{:S(2)}) copy-start(f32[25,512]{1,0:T(8,128)} %ent_re.3) | copy-start | bytes 153604
  0.6 19.4 %copy-start.5 = (f32[25,512]{1,0:T(8,128)S(1)}, f32[25,512]{1,0:T(8,128)}, u32[]{:S(2)}) copy-start(f32[25,512]{1,0:T(8,128)} %ent_im.3) | copy-start | bytes 153604
  1.6 23.0 %collective-permute-start.2 = (f32[50,512]{1,0:T(8,128)S(1)}, f32[50,512]{1,0:T(8,128)S(1)}, u32[]{:S(2)}, u32[]{:S(2)}) collective-permute-start(f32[50,512]{1,0:T(8,128)S(1)} %pad_maximum_fusion.b0), channel_id=1, source_target_pairs={{0,24},{8,32},{16,40},{24,48},{32,56},{40,64},{48,72},{56,80},{64,... | collective-permute-start | bytes 307208 | tf_op jit(solution)/shard_map/ppermute | solution.py:238
  10.0 25.1 %collective-permute-start.1 = (f32[50,512]{1,0:T(8,128)S(1)}, f32[50,512]{1,0:T(8,128)S(1)}, u32[]{:S(2)}, u32[]{:S(2)}) collective-permute-start(f32[50,512]{1,0:T(8,128)S(1)} %pad_maximum_fusion.b0), channel_id=1, source_target_pairs={{0,16},{8,24},{16,32},{24,40},{32,48},{40,56},{48,64},{56,72},{64,... | collective-permute-start | bytes 307208 | tf_op jit(solution)/shard_map/ppermute | solution.py:238
  16.2 19.8 %collective-permute-start = (f32[50,512]{1,0:T(8,128)S(1)}, f32[50,512]{1,0:T(8,128)S(1)}, u32[]{:S(2)}, u32[]{:S(2)}) collective-permute-start(f32[50,512]{1,0:T(8,128)S(1)} %pad_maximum_fusion.b0), channel_id=1, source_target_pairs={{0,8},{8,16},{16,24},{24,32},{32,40},{40,48},{48,56},{56,64},{64,7... | collective-permute-start | bytes 307208 | tf_op jit(solution)/shard_map/ppermute | solution.py:238
  19.3 0.7 copy-start.12
  20.0 0.7 copy-start.11
  20.0 0.7 copy-start.8
  20.0 0.7 copy-start.9
  20.7 1.0 copy-start
  21.7 1.0 copy-start.2
  24.3 11.6 %copy-start.7 = (s32[2]{0:T(128)S(1)}, s32[2]{0:T(128)}, u32[]{:S(2)}) copy-start(s32[2]{0:T(128)} %bucket.5) | copy-start | bytes 28
  37.1 4.3 %collective-permute-start.3 = (f32[4,32,512]{2,1,0:T(8,128)S(1)}, f32[4,32,512]{2,1,0:T(8,128)S(1)}, u32[]{:S(2)}, u32[]{:S(2)}) collective-permute-start(f32[4,32,512]{2,1,0:T(8,128)S(1)} %get-tuple-element.34), channel_id=1, source_target_pairs={{0,1},{1,0},{2,3},{3,2},{4,5},{5,4},{6,7},{7,6},{8,9},{9,8},{10,11... | collective-permute-start | bytes 786440 | tf_op jit(solution)/shard_map/ppermute | solution.py:256
  65.4 6.8 %collective-permute-start.4 = (f32[4,32,512]{2,1,0:T(8,128)S(1)}, f32[4,32,512]{2,1,0:T(8,128)S(1)}, u32[]{:S(2)}, u32[]{:S(2)}) collective-permute-start(f32[4,32,512]{2,1,0:T(8,128)S(1)} %all_to_all.31.w_mine), channel_id=1, source_target_pairs={{0,1},{1,0},{2,3},{3,2},{4,5},{5,4},{6,7},{7,6},{8,9},{9,8},{10,11... | collective-permute-start | bytes 786440 | tf_op jit(solution)/shard_map/ppermute | solution.py:260
  84.3 16.4 %all-to-all-start.3 = ((f32[8,50,128]{2,1,0:T(8,128)}), f32[8,50,128]{2,1,0:T(8,128)S(1)}, u32[]{:S(2)}, u32[]{:S(2)}) async-start(f32[8,50,128]{2,1,0:T(8,128)} %place.1), calls=%async_computation.3 | async-start | bytes 458752 | tf_op jit(solution)/shard_map/all_to_all | solution.py:242
  87.7 19.2 %collective-permute-start.6 = (f32[50,512]{1,0:T(8,128)S(1)}, f32[50,512]{1,0:T(8,128)S(1)}, u32[]{:S(2)}, u32[]{:S(2)}) collective-permute-start(f32[50,512]{1,0:T(8,128)S(1)} %get-tuple-element.38), channel_id=1, source_target_pairs={{0,504},{8,0},{16,8},{24,16},{32,24},{40,32},{48,40},{56,48},{64,5... | collective-permute-start | bytes 307208 | tf_op jit(solution)/shard_map/ppermute | solution.py:238
  93.6 13.3 %collective-permute-start.7 = (f32[50,512]{1,0:T(8,128)S(1)}, f32[50,512]{1,0:T(8,128)S(1)}, u32[]{:S(2)}, u32[]{:S(2)}) collective-permute-start(f32[50,512]{1,0:T(8,128)S(1)} %get-tuple-element.39), channel_id=1, source_target_pairs={{0,496},{8,504},{16,0},{24,8},{32,16},{40,24},{48,32},{56,40},{64,... | collective-permute-start | bytes 307208 | tf_op jit(solution)/shard_map/ppermute | solution.py:238
  97.6 14.0 %collective-permute-start.8 = (f32[50,512]{1,0:T(8,128)S(1)}, f32[50,512]{1,0:T(8,128)S(1)}, u32[]{:S(2)}, u32[]{:S(2)}) collective-permute-start(f32[50,512]{1,0:T(8,128)S(1)} %get-tuple-element.40), channel_id=1, source_target_pairs={{0,488},{8,496},{16,504},{24,0},{32,8},{40,16},{48,24},{56,32},{64... | collective-permute-start | bytes 307208 | tf_op jit(solution)/shard_map/ppermute | solution.py:238
  100.7 12.5 %collective-permute-start.5 = (f32[50,128]{1,0:T(8,128)S(1)}, f32[50,128]{1,0:T(8,128)S(1)}, u32[]{:S(2)}, u32[]{:S(2)}) collective-permute-start(f32[50,128]{1,0:T(8,128)S(1)} %fold.1.a), channel_id=1, source_target_pairs={{0,256},{256,0},{1,257},{257,1},{2,258},{258,2},{3,259},{259,3},{4... | collective-permute-start | bytes 76808 | tf_op jit(solution)/shard_map/ppermute | solution.py:268
  141.3 19.3 %copy-start.1 = (f32[25,4096]{1,0:T(8,128)S(1)}, f32[25,4096]{1,0:T(8,128)}, u32[]{:S(2)}) copy-start(f32[25,4096]{1,0:T(8,128)} %rel_re.3) | copy-start | bytes 1228804
  141.3 19.3 %copy-start.3 = (f32[25,4096]{1,0:T(8,128)S(1)}, f32[25,4096]{1,0:T(8,128)}, u32[]{:S(2)}) copy-start(f32[25,4096]{1,0:T(8,128)} %rel_im.3) | copy-start | bytes 1228804
  141.4 19.2 %copy-start.6 = (f32[4096]{0:T(1024)S(1)}, f32[4096]{0:T(1024)}, u32[]{:S(2)}) copy-start(f32[4096]{0:T(1024)} %param.16) | copy-start | bytes 49156
  160.6 0.7 copy-start.10

commit v4 on v3

--- a/solution.py
+++ b/solution.py
@@ -196,42 +196,42 @@
     out[...] = tot
 
 
-def both_kernel(a, b, out):
+def both_kernel(a, b, s0, got1, got2, got3, out, ent_o, sq_o):
     tot = a[...] + b[...]
     for i in range(32):
         out[i] = tot
-
-
-def square_kernel(rel, s0, got1, got2, got3, ent_o, sq_o):
     ent = s0[...] + (got1[...] + (got2[...] + got3[...]))
     ent_o[...] = ent
     es = jnp.sum(ent * ent, 0, keepdims=True)
+    rs = jnp.sum(tot * tot, 0, keepdims=True)
     for i in range(8):
         sq_o[i, :, 0:ROWS] = es
-    for t in range(32):
-        tot = rel[t]
-        rs = jnp.sum(tot * tot, 0, keepdims=True)
-        for i in range(8):
-            sq_o[i, :, ROWS + 128 * t : ROWS + 128 * t + 128] = rs
-
-
-def update_kernel(sq, rel, ent, ent_re, ent_im, eacc, rel_re, rel_im, racc, re_o, im_o, acc_o, rre_o, rim_o, racc_o):
+        sq_o[i, :, ROWS : ROWS + 128] = rs
+
+
+def entity_kernel(info, sq, ent, ent_re, ent_im, eacc, racc, re_o, im_o, acc_o, racc_o):
     s = sq[0]
     for i in range(1, 8):
         s = s + sq[i]
+    acc = racc[pl.ds(info[1] * 8 + info[3], 1), :] + s[:, ROWS:] / D
+    for i in range(32):
+        racc_o[i] = acc
     acc = eacc[...] + s[:, :ROWS] / D
     acc_o[...] = acc
     scale = LEARN_RATE / jnp.sqrt(acc)
     re_o[...] = ent_re[...] - scale * ent[0:W, :]
     im_o[...] = ent_im[...] - scale * ent[W : 2 * W, :]
-    acc = racc[...] + s[:, ROWS:] / D
-    racc_o[...] = acc
-    scale = LEARN_RATE / jnp.sqrt(acc)
+
+
+def relation_kernel(rel, racc, rel_re, rel_im, re_o, im_o, acc_o):
     for t in range(32):
         at = slice(128 * t, 128 * t + 128)
+        acc = racc[t]
+        acc_o[t : t + 1, :] = acc
+        scale = LEARN_RATE / jnp.sqrt(acc)
         tot = rel[t]
-        rre_o[:, at] = rel_re[:, at] - scale[:, at] * tot[:W]
-        rim_o[:, at] = rel_im[:, at] - scale[:, at] * tot[W:]
+        re_o[:, at] = rel_re[:, at] - scale * tot[:W]
+        im_o[:, at] = rel_im[:, at] - scale * tot[W:]
 
 
 def shift(block, distance):
@@ -243,7 +243,7 @@
 
 
 def per_device(ent_re, ent_im, ent_acc, rel_re, rel_im, rel_acc, lhs_rows, rhs_rows, rel_ids, neg_rows, bucket_step):
-    info = jnp.stack([lax.axis_index("core"), lax.axis_index("x"), lax.axis_index("yl")]).astype(I32)
+    info = jnp.stack([lax.axis_index("core"), lax.axis_index("x"), lax.axis_index("yl"), lax.axis_index("z")]).astype(I32)
     own = jnp.concatenate([ent_re, ent_im], 0)
     b1, b2, b3 = [shift(own, d) for d in (1, 2, 3)]
     neg = jnp.pad(neg_rows, ((0, 0), (0, 24)), constant_values=-1)
@@ -266,13 +266,14 @@
     pieces = call(place_kernel, "place", (8, 2 * W, 128), [SM, VM])(info, gr)
     half = call(fold_kernel, "fold", (2 * W, 128), [VM])(exchange(pieces, "z"))
     twin, got = lax.optimization_barrier((lax.ppermute(half, "yh", SWAP), got))
-    rel = call(both_kernel, "both", (32, 2 * W, 128), [VM] * 2)(half, twin)
+    rel, ent, sq = call(both_kernel, "both", [(32, 2 * W, 128), block, (8, 1, ROWS + 128)], [VM] * 6)(half, twin, s0, *got)
     rel = exchange(rel, ("x", "z"))
-    ent, sq = call(square_kernel, "square", [block, (8, 1, ROWS + REL)], [VM] * 5)(rel, s0, *got)
-    sq = exchange(sq, DIM)
-    new_re, new_im, new_acc, new_rel_re, new_rel_im, new_rel_acc = call(
-        update_kernel, "update", [(W, ROWS), (W, ROWS), (1, ROWS), (W, REL), (W, REL), (1, REL)], [VM] * 9
-    )(sq, rel, ent, ent_re, ent_im, ent_acc.reshape(1, ROWS), rel_re, rel_im, rel_acc.reshape(1, REL))
+    new_re, new_im, new_acc, racc = call(
+        entity_kernel, "entity", [(W, ROWS), (W, ROWS), (1, ROWS), (32, 1, 128)], [SM] + [VM] * 6
+    )(info, exchange(sq, DIM), ent, ent_re, ent_im, ent_acc.reshape(1, ROWS), rel_acc.reshape(32, 128))
+    new_rel_re, new_rel_im, new_rel_acc = call(
+        relation_kernel, "relation", [(W, REL), (W, REL), (32, 128)], [VM] * 4
+    )(rel, exchange(racc, ("x", "z")), rel_re, rel_im)
     return new_re, new_im, new_acc.reshape(ROWS), new_rel_re, new_rel_im, new_rel_acc.reshape(REL)
 
 

time: 163 us -> 174 us (1.067)
  the two profiles are of different devices: /device:TPU:1 before, /device:TPU:64 now
where the time goes in v4:
time: 174 us; the launch traced here: 173 us
  blocking collectives  95.4 us (55%)
  starting transfers between devices  46.3 us (27%)
  waiting for transfers between devices  16.1 us (9%)
  Pallas kernels  9.62 us (6%)
  local copies, waits for them, and re-layouts  4.09 us (2%)
    all_to_all x6, blocking collectives, exchange(): return lax.all_to_all(pieces, axes, 0, 0)  95.4 us
    ppermute x6, starting transfers between devices, shift(): lax.ppermute(block, DOM, [(i, (i + distance) % 64) for i in range(64)])  30.4 us
    ppermute x6, waiting for transfers between devices, shift(): lax.ppermute(block, DOM, [(i, (i + distance) % 64) for i in range(64)])  9.45 us
    ppermute x1, starting transfers between devices, per_device(): twin, got = lax.optimization_barrier((lax.ppermute(half, 'yh', SWAP), got))  6.49 us
    all_to_all x1, starting transfers between devices, exchange(): return lax.all_to_all(pieces, axes, 0, 0)  5.58 us
    unnamed x26, local copies, waits for them, and re-layouts  4.08 us
    ppermute x1, waiting for transfers between devices, per_device(): twin, got = lax.optimization_barrier((lax.ppermute(half, 'yh', SWAP), got))  3.63 us
  transfers between devices with their start and end apart: 10, of which 6 were waited for; matrix products, arithmetic and copies ran while one was open for 0% of the time, Pallas kernels for 1%

profile of v4, /device:TPU:64, one launch (start us, length us, event | category | flops | bytes accessed | tf_op | source)
XLA Modules:
  0.0 173.4 jit_solution(7779914363363669058)
XLA Ops:
  0.6 0.0 copy-start.4
  0.6 0.0 copy-start.5
  0.7 0.9 pad_maximum_fusion.b0
  1.6 9.1 %collective-permute-start.2 = (f32[50,512]{1,0:T(8,128)S(1)}, f32[50,512]{1,0:T(8,128)S(1)}, u32[]{:S(2)}, u32[]{:S(2)}) collective-permute-start(f32[50,512]{1,0:T(8,128)S(1)} %pad_maximum_fusion.b0), channel_id=1, source_target_pairs={{0,24},{8,32},{16,40},{24,48},{32,56},{40,64},{48,72},{56,80},{64,... | collective-permute-start | bytes 307208 | tf_op jit(solution)/shard_map/ppermute | solution.py:238
  10.7 4.3 %collective-permute-start.1 = (f32[50,512]{1,0:T(8,128)S(1)}, f32[50,512]{1,0:T(8,128)S(1)}, u32[]{:S(2)}, u32[]{:S(2)}) collective-permute-start(f32[50,512]{1,0:T(8,128)S(1)} %pad_maximum_fusion.b0), channel_id=1, source_target_pairs={{0,16},{8,24},{16,32},{24,40},{32,48},{40,56},{48,64},{56,72},{64,... | collective-permute-start | bytes 307208 | tf_op jit(solution)/shard_map/ppermute | solution.py:238
  15.0 3.4 %collective-permute-start = (f32[50,512]{1,0:T(8,128)S(1)}, f32[50,512]{1,0:T(8,128)S(1)}, u32[]{:S(2)}, u32[]{:S(2)}) collective-permute-start(f32[50,512]{1,0:T(8,128)S(1)} %pad_maximum_fusion.b0), channel_id=1, source_target_pairs={{0,8},{8,16},{16,24},{24,32},{32,40},{40,48},{48,56},{56,64},{64,7... | collective-permute-start | bytes 307208 | tf_op jit(solution)/shard_map/ppermute | solution.py:238
  18.4 0.0 copy-start.12
  18.4 0.7 copy-done.12
  19.1 0.0 copy-start.11
  19.1 0.0 copy-start.8
  19.1 0.0 copy-start.9
  19.1 0.1 pad_add_fusion.info
  19.2 0.0 copy-done.4
  19.2 0.0 copy-done.5
  19.2 0.6 copy-done.11
  19.8 0.0 copy-done.8
  19.8 0.0 copy-done.9
  19.8 0.0 copy-start
  19.8 1.0 copy-done
  20.8 0.0 copy-start.2
  20.8 1.0 copy-done.2
  21.9 1.5 query.1
  23.4 0.0 copy-start.7
  23.4 4.7 %collective-permute-done.2.b3 = f32[50,512]{1,0:T(8,128)S(1)} collective-permute-done((f32[50,512]{1,0:T(8,128)S(1)}, f32[50,512]{1,0:T(8,128)S(1)}, u32[]{:S(2)}, u32[]{:S(2)}) %collective-permute-start.2) | collective-permute-done | bytes 102432 | tf_op jit(solution)/shard_map/ppermute | solution.py:238
  28.1 4.2 %collective-permute-done.1.b2 = f32[50,512]{1,0:T(8,128)S(1)} collective-permute-done((f32[50,512]{1,0:T(8,128)S(1)}, f32[50,512]{1,0:T(8,128)S(1)}, u32[]{:S(2)}, u32[]{:S(2)}) %collective-permute-start.1) | collective-permute-done | bytes 102432 | tf_op jit(solution)/shard_map/ppermute | solution.py:238
  32.3 0.0 collective-permute-done.b1
  32.3 0.0 copy-done.7
  32.3 1.2 score.1
  33.5 1.9 %collective-permute-start.3 = (f32[4,32,512]{2,1,0:T(8,128)S(1)}, f32[4,32,512]{2,1,0:T(8,128)S(1)}, u32[]{:S(2)}, u32[]{:S(2)}) collective-permute-start(f32[4,32,512]{2,1,0:T(8,128)S(1)} %get-tuple-element.36), channel_id=1, source_target_pairs={{0,1},{1,0},{2,3},{3,2},{4,5},{5,4},{6,7},{7,6},{8,9},{9,8},{10,11... | collective-permute-start | bytes 786440 | tf_op jit(solution)/shard_map/ppermute | solution.py:256
  35.4 1.5 collective-permute-done.3.b
  37.0 16.3 %all_to_all.35.parts = f32[4,32,512]{2,1,0:T(8,128)S(1)} all-to-all(f32[4,32,512]{2,1,0:T(8,128)S(1)} %add.9), channel_id=1, replica_groups=mesh['yh'=2,'x'=4,'z'=8,'yl'=4,'core'=2] {'yl'}, dimensions={0} | all-to-all | bytes 524288 | tf_op jit(solution)/shard_map/all_to_all | solution.py:242
  53.3 0.8 weight.1
  54.0 11.0 %all_to_all.36.w_mine = f32[4,32,512]{2,1,0:T(8,128)S(1)} all-to-all(f32[4,32,512]{2,1,0:T(8,128)S(1)} %weight.1), channel_id=1, replica_groups=mesh['yh'=2,'x'=4,'z'=8,'yl'=4,'core'=2] {'yl'}, dimensions={0} | all-to-all | bytes 524288 | tf_op jit(solution)/shard_map/all_to_all | solution.py:242
  65.0 1.9 %collective-permute-start.4 = (f32[4,32,512]{2,1,0:T(8,128)S(1)}, f32[4,32,512]{2,1,0:T(8,128)S(1)}, u32[]{:S(2)}, u32[]{:S(2)}) collective-permute-start(f32[4,32,512]{2,1,0:T(8,128)S(1)} %all_to_all.36.w_mine), channel_id=1, source_target_pairs={{0,1},{1,0},{2,3},{3,2},{4,5},{5,4},{6,7},{7,6},{8,9},{9,8},{10,11... | collective-permute-start | bytes 786440 | tf_op jit(solution)/shard_map/ppermute | solution.py:260
  66.9 1.5 collective-permute-done.4.w_other
  68.4 1.6 grad.1
  70.0 9.3 %all_to_all.37.gr = f32[4,51,256]{2,1,0:T(8,128)S(1)} all-to-all(f32[4,51,256]{2,1,0:T(8,128)S(1)} %get-tuple-element.39), channel_id=1, replica_groups=mesh['yh'=2,'x'=4,'z'=8,'yl'=4,'core'=2] {'x'}, dimensions={0} | all-to-all | bytes 417792 | tf_op jit(solution)/shard_map/all_to_all | solution.py:242
  79.3 2.1 %place.1 = f32[8,50,128]{2,1,0:T(8,128)} custom-call(s32[4]{0:T(128)S(1)} %pad_add_fusion.info, f32[4,51,256]{2,1,0:T(8,128)S(1)} %all_to_all.37.gr), custom_call_target="tpu_custom_call" | custom-call | tf_op jit(solution)/shard_map/place/pallas_call | solution.py:266
  81.4 5.6 %all-to-all-start.3 = ((f32[8,50,128]{2,1,0:T(8,128)}), f32[8,50,128]{2,1,0:T(8,128)S(1)}, u32[]{:S(2)}, u32[]{:S(2)}) async-start(f32[8,50,128]{2,1,0:T(8,128)} %place.1), calls=%async_computation.3 | async-start | bytes 458752 | tf_op jit(solution)/shard_map/all_to_all | solution.py:242
  87.0 2.0 %collective-permute-start.6 = (f32[50,512]{1,0:T(8,128)S(1)}, f32[50,512]{1,0:T(8,128)S(1)}, u32[]{:S(2)}, u32[]{:S(2)}) collective-permute-start(f32[50,512]{1,0:T(8,128)S(1)} %get-tuple-element.40), channel_id=1, source_target_pairs={{0,504},{8,0},{16,8},{24,16},{32,24},{40,32},{48,40},{56,48},{64,5... | collective-permute-start | bytes 307208 | tf_op jit(solution)/shard_map/ppermute | solution.py:238
  89.0 7.4 %collective-permute-start.7 = (f32[50,512]{1,0:T(8,128)S(1)}, f32[50,512]{1,0:T(8,128)S(1)}, u32[]{:S(2)}, u32[]{:S(2)}) collective-permute-start(f32[50,512]{1,0:T(8,128)S(1)} %get-tuple-element.41), channel_id=1, source_target_pairs={{0,496},{8,504},{16,0},{24,8},{32,16},{40,24},{48,32},{56,40},{64,... | collective-permute-start | bytes 307208 | tf_op jit(solution)/shard_map/ppermute | solution.py:238
  96.4 4.2 %collective-permute-start.8 = (f32[50,512]{1,0:T(8,128)S(1)}, f32[50,512]{1,0:T(8,128)S(1)}, u32[]{:S(2)}, u32[]{:S(2)}) collective-permute-start(f32[50,512]{1,0:T(8,128)S(1)} %get-tuple-element.42), channel_id=1, source_target_pairs={{0,488},{8,496},{16,504},{24,0},{32,8},{40,16},{48,24},{56,32},{64... | collective-permute-start | bytes 307208 | tf_op jit(solution)/shard_map/ppermute | solution.py:238
  100.6 0.0 all-to-all-done.3.parts
  100.7 6.5 %collective-permute-start.5 = (f32[50,128]{1,0:T(8,128)S(1)}, f32[50,128]{1,0:T(8,128)S(1)}, u32[]{:S(2)}, u32[]{:S(2)}) collective-permute-start(f32[50,128]{1,0:T(8,128)S(1)} %fold.1.a), channel_id=1, source_target_pairs={{0,256},{256,0},{1,257},{257,1},{2,258},{258,2},{3,259},{259,3},{4... | collective-permute-start | bytes 76808 | tf_op jit(solution)/shard_map/ppermute | solution.py:268
  107.2 0.0 collective-permute-done.6.got1
  107.2 0.0 collective-permute-done.7.got2
  107.2 0.6 collective-permute-done.8.got3
  107.7 3.6 %collective-permute-done.5.b = f32[50,128]{1,0:T(8,128)S(1)} collective-permute-done((f32[50,128]{1,0:T(8,128)S(1)}, f32[50,128]{1,0:T(8,128)S(1)}, u32[]{:S(2)}, u32[]{:S(2)}) %collective-permute-start.5) | collective-permute-done | bytes 25632 | tf_op jit(solution)/shard_map/ppermute | solution.py:268
  111.4 0.1 both.1
  111.5 0.0 copy-start.6
  111.5 9.7 %all_to_all.38.sq = f32[8,1,640]{2,1,0:T(1,128)S(1)} all-to-all(f32[8,1,640]{2,1,0:T(1,128)S(1)} %get-tuple-element.48), channel_id=1, replica_groups=mesh['yh'=2,'x'=4,'z'=8,'yl'=4,'core'=2] {'yl','core'}, dimensions={0} | all-to-all | bytes 40960 | tf_op jit(solution)/shard_map/all_to_all | solution.py:242
  121.1 0.0 copy-start.10
  121.1 0.0 copy-done.6
  121.1 0.7 copy-done.10
  121.8 1.2 entity.1
  123.1 20.3 %all_to_all.39.racc = f32[32,1,128]{2,1,0:T(1,128)S(1)} all-to-all(f32[32,1,128]{2,1,0:T(1,128)S(1)} %get-tuple-element.54), channel_id=1, replica_groups=mesh['yh'=2,'x'=4,'z'=8,'yl'=4,'core'=2] {'x','z'}, dimensions={0} | all-to-all | bytes 32768 | tf_op jit(solution)/shard_map/all_to_all | solution.py:242
  143.3 0.0 copy-start.1
  143.3 0.0 copy-start.3
  143.3 28.9 %all_to_all.40.rel = f32[32,50,128]{2,1,0:T(8,128)S(1)} all-to-all(f32[32,50,128]{2,1,0:T(8,128)S(1)} %get-tuple-element.53), channel_id=1, replica_groups=mesh['yh'=2,'x'=4,'z'=8,'yl'=4,'core'=2] {'x','z'}, dimensions={0} | all-to-all | bytes 1638400 | tf_op jit(solution)/shard_map/all_to_all | solution.py:242
  172.3 0.0 copy-done.1
  172.3 0.0 copy-done.3
  172.3 1.1 relation.1
  (3 shorter events, 0.1 us)
Async XLA Ops:
  0.6 18.6 %copy-start.4 = (f32[25,512]{1,0:T(8,128)S(1)}, f32[25,512]{1,0:T(8,128)}, u32[]{:S(2)}) copy-start(f32[25,512]{1,0:T(8,128)} %ent_re.3) | copy-start | bytes 153604
  0.6 18.6 %copy-start.5 = (f32[25,512]{1,0:T(8,128)S(1)}, f32[25,512]{1,0:T(8,128)}, u32[]{:S(2)}) copy-start(f32[25,512]{1,0:T(8,128)} %ent_im.3) | copy-start | bytes 153604
  1.6 26.5 %collective-permute-start.2 = (f32[50,512]{1,0:T(8,128)S(1)}, f32[50,512]{1,0:T(8,128)S(1)}, u32[]{:S(2)}, u32[]{:S(2)}) collective-permute-start(f32[50,512]{1,0:T(8,128)S(1)} %pad_maximum_fusion.b0), channel_id=1, source_target_pairs={{0,24},{8,32},{16,40},{24,48},{32,56},{40,64},{48,72},{56,80},{64,... | collective-permute-start | bytes 307208 | tf_op jit(solution)/shard_map/ppermute | solution.py:238
  10.7 21.6 %collective-permute-start.1 = (f32[50,512]{1,0:T(8,128)S(1)}, f32[50,512]{1,0:T(8,128)S(1)}, u32[]{:S(2)}, u32[]{:S(2)}) collective-permute-start(f32[50,512]{1,0:T(8,128)S(1)} %pad_maximum_fusion.b0), channel_id=1, source_target_pairs={{0,16},{8,24},{16,32},{24,40},{32,48},{40,56},{48,64},{56,72},{64,... | collective-permute-start | bytes 307208 | tf_op jit(solution)/shard_map/ppermute | solution.py:238
  15.0 17.3 %collective-permute-start = (f32[50,512]{1,0:T(8,128)S(1)}, f32[50,512]{1,0:T(8,128)S(1)}, u32[]{:S(2)}, u32[]{:S(2)}) collective-permute-start(f32[50,512]{1,0:T(8,128)S(1)} %pad_maximum_fusion.b0), channel_id=1, source_target_pairs={{0,8},{8,16},{16,24},{24,32},{32,40},{40,48},{48,56},{56,64},{64,7... | collective-permute-start | bytes 307208 | tf_op jit(solution)/shard_map/ppermute | solution.py:238
  18.4 0.7 copy-start.12
  19.1 0.7 copy-start.11
  19.1 0.7 copy-start.8
  19.1 0.7 copy-start.9
  19.8 1.0 copy-start
  20.8 1.0 copy-start.2
  23.4 8.9 %copy-start.7 = (s32[2]{0:T(128)S(1)}, s32[2]{0:T(128)}, u32[]{:S(2)}) copy-start(s32[2]{0:T(128)} %bucket.5) | copy-start | bytes 28
  33.5 3.4 %collective-permute-start.3 = (f32[4,32,512]{2,1,0:T(8,128)S(1)}, f32[4,32,512]{2,1,0:T(8,128)S(1)}, u32[]{:S(2)}, u32[]{:S(2)}) collective-permute-start(f32[4,32,512]{2,1,0:T(8,128)S(1)} %get-tuple-element.36), channel_id=1, source_target_pairs={{0,1},{1,0},{2,3},{3,2},{4,5},{5,4},{6,7},{7,6},{8,9},{9,8},{10,11... | collective-permute-start | bytes 786440 | tf_op jit(solution)/shard_map/ppermute | solution.py:256
  65.0 3.4 %collective-permute-start.4 = (f32[4,32,512]{2,1,0:T(8,128)S(1)}, f32[4,32,512]{2,1,0:T(8,128)S(1)}, u32[]{:S(2)}, u32[]{:S(2)}) collective-permute-start(f32[4,32,512]{2,1,0:T(8,128)S(1)} %all_to_all.36.w_mine), channel_id=1, source_target_pairs={{0,1},{1,0},{2,3},{3,2},{4,5},{5,4},{6,7},{7,6},{8,9},{9,8},{10,11... | collective-permute-start | bytes 786440 | tf_op jit(solution)/shard_map/ppermute | solution.py:260
  81.4 19.2 %all-to-all-start.3 = ((f32[8,50,128]{2,1,0:T(8,128)}), f32[8,50,128]{2,1,0:T(8,128)S(1)}, u32[]{:S(2)}, u32[]{:S(2)}) async-start(f32[8,50,128]{2,1,0:T(8,128)} %place.1), calls=%async_computation.3 | async-start | bytes 458752 | tf_op jit(solution)/shard_map/all_to_all | solution.py:242
  87.0 20.2 %collective-permute-start.6 = (f32[50,512]{1,0:T(8,128)S(1)}, f32[50,512]{1,0:T(8,128)S(1)}, u32[]{:S(2)}, u32[]{:S(2)}) collective-permute-start(f32[50,512]{1,0:T(8,128)S(1)} %get-tuple-element.40), channel_id=1, source_target_pairs={{0,504},{8,0},{16,8},{24,16},{32,24},{40,32},{48,40},{56,48},{64,5... | collective-permute-start | bytes 307208 | tf_op jit(solution)/shard_map/ppermute | solution.py:238
  89.0 18.2 %collective-permute-start.7 = (f32[50,512]{1,0:T(8,128)S(1)}, f32[50,512]{1,0:T(8,128)S(1)}, u32[]{:S(2)}, u32[]{:S(2)}) collective-permute-start(f32[50,512]{1,0:T(8,128)S(1)} %get-tuple-element.41), channel_id=1, source_target_pairs={{0,496},{8,504},{16,0},{24,8},{32,16},{40,24},{48,32},{56,40},{64,... | collective-permute-start | bytes 307208 | tf_op jit(solution)/shard_map/ppermute | solution.py:238
  96.4 11.4 %collective-permute-start.8 = (f32[50,512]{1,0:T(8,128)S(1)}, f32[50,512]{1,0:T(8,128)S(1)}, u32[]{:S(2)}, u32[]{:S(2)}) collective-permute-start(f32[50,512]{1,0:T(8,128)S(1)} %get-tuple-element.42), channel_id=1, source_target_pairs={{0,488},{8,496},{16,504},{24,0},{32,8},{40,16},{48,24},{56,32},{64... | collective-permute-start | bytes 307208 | tf_op jit(solution)/shard_map/ppermute | solution.py:238
  100.7 10.7 %collective-permute-start.5 = (f32[50,128]{1,0:T(8,128)S(1)}, f32[50,128]{1,0:T(8,128)S(1)}, u32[]{:S(2)}, u32[]{:S(2)}) collective-permute-start(f32[50,128]{1,0:T(8,128)S(1)} %fold.1.a), channel_id=1, source_target_pairs={{0,256},{256,0},{1,257},{257,1},{2,258},{258,2},{3,259},{259,3},{4... | collective-permute-start | bytes 76808 | tf_op jit(solution)/shard_map/ppermute | solution.py:268
  111.5 9.7 %copy-start.6 = (f32[4096]{0:T(1024)S(1)}, f32[4096]{0:T(1024)}, u32[]{:S(2)}) copy-start(f32[4096]{0:T(1024)} %param.16) | copy-start | bytes 49156
  121.1 0.7 copy-start.10
  143.3 28.9 %copy-start.1 = (f32[25,4096]{1,0:T(8,128)S(1)}, f32[25,4096]{1,0:T(8,128)}, u32[]{:S(2)}) copy-start(f32[25,4096]{1,0:T(8,128)} %rel_re.3) | copy-start | bytes 1228804
  143.3 28.9 %copy-start.3 = (f32[25,4096]{1,0:T(8,128)S(1)}, f32[25,4096]{1,0:T(8,128)}, u32[]{:S(2)}) copy-start(f32[25,4096]{1,0:T(8,128)} %rel_im.3) | copy-start | bytes 1228804

commit v5 on v4

--- a/solution.py
+++ b/solution.py
@@ -166,7 +166,7 @@
     gr_re = (g_re * h_re + g_im * h_im)[:W]
     gr_im = (g_im * h_re - g_re * h_im)[:W]
     ids = edge_ids(rel_ids).astype(F32)
-    for i in range(4):
+    for i in range(8):
         gr_o[i, 0:W, :] = gr_re
         gr_o[i, W : 2 * W, :] = gr_im
         gr_o[i, 2 * W : 2 * W + 1, :] = ids
@@ -179,7 +179,7 @@
     x = info[1]
     vals = []
     cols = []
-    for i in range(4):
+    for i in range(8):
         vals.append(split3(pack(gr[i, 0 : 2 * W, :])))
         ids = gr[i, 2 * W : 2 * W + 1, :].astype(I32)
         cols.append(jnp.where(jnp.right_shift(ids, 10) == x, jnp.bitwise_and(ids, 1023), -1))
@@ -189,17 +189,11 @@
         out[z, W : 2 * W, :] = total[32 : 32 + W, 128 * z : 128 * z + 128]
 
 
-def fold_kernel(parts, out):
+def square_kernel(parts, s0, got1, got2, got3, tot_o, ent_o, sq_o):
     tot = parts[0]
     for i in range(1, 8):
         tot = tot + parts[i]
-    out[...] = tot
-
-
-def both_kernel(a, b, s0, got1, got2, got3, out, ent_o, sq_o):
-    tot = a[...] + b[...]
-    for i in range(32):
-        out[i] = tot
+    tot_o[...] = tot
     ent = s0[...] + (got1[...] + (got2[...] + got3[...]))
     ent_o[...] = ent
     es = jnp.sum(ent * ent, 0, keepdims=True)
@@ -209,13 +203,20 @@
         sq_o[i, :, ROWS : ROWS + 128] = rs
 
 
-def entity_kernel(info, sq, ent, ent_re, ent_im, eacc, racc, re_o, im_o, acc_o, racc_o):
+def update_kernel(info, sq, tot, ent, ent_re, ent_im, eacc, rel_re, rel_im, racc, re_o, im_o, acc_o, rel_o):
     s = sq[0]
     for i in range(1, 8):
         s = s + sq[i]
-    acc = racc[pl.ds(info[1] * 8 + info[3], 1), :] + s[:, ROWS:] / D
+    tile = info[1] * 8 + info[3]
+    lane = pl.ds(pl.multiple_of(tile * 128, 128), 128)
+    acc = racc[pl.ds(tile, 1), :] + s[:, ROWS:] / D
+    scale = LEARN_RATE / jnp.sqrt(acc)
+    new_re = rel_re[:, lane] - scale * tot[0:W, :]
+    new_im = rel_im[:, lane] - scale * tot[W : 2 * W, :]
     for i in range(32):
-        racc_o[i] = acc
+        rel_o[i, 0:W, :] = new_re
+        rel_o[i, W : 2 * W, :] = new_im
+        rel_o[i, 2 * W : 2 * W + 1, :] = acc
     acc = eacc[...] + s[:, :ROWS] / D
     acc_o[...] = acc
     scale = LEARN_RATE / jnp.sqrt(acc)
@@ -223,15 +224,12 @@
     im_o[...] = ent_im[...] - scale * ent[W : 2 * W, :]
 
 
-def relation_kernel(rel, racc, rel_re, rel_im, re_o, im_o, acc_o):
+def spread_kernel(rel, re_o, im_o, acc_o):
     for t in range(32):
         at = slice(128 * t, 128 * t + 128)
-        acc = racc[t]
-        acc_o[t : t + 1, :] = acc
-        scale = LEARN_RATE / jnp.sqrt(acc)
-        tot = rel[t]
-        re_o[:, at] = rel_re[:, at] - scale * tot[:W]
-        im_o[:, at] = rel_im[:, at] - scale * tot[W:]
+        re_o[:, at] = rel[t, 0:W, :]
+        im_o[:, at] = rel[t, W : 2 * W, :]
+        acc_o[t : t + 1, :] = rel[t, 2 * W : 2 * W + 1, :]
 
 
 def shift(block, distance):
@@ -259,21 +257,20 @@
     w_mine = exchange(w, "yl")
     w_other = lax.ppermute(w_mine, "core", SWAP)
     s0, s1, s2, s3, gr = call(
-        grad_kernel, "grad", [block, block, block, block, (4, 2 * W + 1, 256)], [SM, SM] + [VM] * 11,
+        grad_kernel, "grad", [block, block, block, block, (8, 2 * W + 1, 256)], [SM, SM] + [VM] * 11,
     )(info, bucket_step, q, head, relc, w_mine, w_other, own, b1, b2, b3, lhs_rows, rel_ids)
-    got = [shift(s1, -1), shift(s2, -2), shift(s3, -3)]
-    gr = exchange(gr, "x")
+    got1, got2, got3 = shift(s1, -1), shift(s2, -2), shift(s3, -3)
+    gr = exchange(gr, ("yh", "x"))
     pieces = call(place_kernel, "place", (8, 2 * W, 128), [SM, VM])(info, gr)
-    half = call(fold_kernel, "fold", (2 * W, 128), [VM])(exchange(pieces, "z"))
-    twin, got = lax.optimization_barrier((lax.ppermute(half, "yh", SWAP), got))
-    rel, ent, sq = call(both_kernel, "both", [(32, 2 * W, 128), block, (8, 1, ROWS + 128)], [VM] * 6)(half, twin, s0, *got)
+    pieces, got1, got2 = lax.optimization_barrier((pieces, got1, got2))
+    pieces = exchange(pieces, "z")
+    tot, ent, sq = call(square_kernel, "square", [(2 * W, 128), block, (8, 1, ROWS + 128)], [VM] * 5)(pieces, s0, got1, got2, got3)
+    sq = exchange(sq, DIM)
+    new_re, new_im, new_acc, rel = call(
+        update_kernel, "update", [(W, ROWS), (W, ROWS), (1, ROWS), (32, 2 * W + 1, 128)], [SM] + [VM] * 9
+    )(info, sq, tot, ent, ent_re, ent_im, ent_acc.reshape(1, ROWS), rel_re, rel_im, rel_acc.reshape(32, 128))
     rel = exchange(rel, ("x", "z"))
-    new_re, new_im, new_acc, racc = call(
-        entity_kernel, "entity", [(W, ROWS), (W, ROWS), (1, ROWS), (32, 1, 128)], [SM] + [VM] * 6
-    )(info, exchange(sq, DIM), ent, ent_re, ent_im, ent_acc.reshape(1, ROWS), rel_acc.reshape(32, 128))
-    new_rel_re, new_rel_im, new_rel_acc = call(
-        relation_kernel, "relation", [(W, REL), (W, REL), (32, 128)], [VM] * 4
-    )(rel, exchange(racc, ("x", "z")), rel_re, rel_im)
+    new_rel_re, new_rel_im, new_rel_acc = call(spread_kernel, "spread", [(W, REL), (W, REL), (32, 128)], [VM])(rel)
     return new_re, new_im, new_acc.reshape(ROWS), new_rel_re, new_rel_im, new_rel_acc.reshape(REL)
 
 

time: 174 us -> 173 us (level)
  blocking collectives: 95.4 us -> 81.1 us
  starting transfers between devices: 46.3 us -> 57.7 us
    all_to_all x6 -> x4, blocking collectives: 95.4 us -> 81.1 us  [exchange(): return lax.all_to_all(pieces, axes, 0, 0)]
    ppermute x6, starting transfers between devices: 30.4 us -> 44.7 us  [shift(): lax.ppermute(block, DOM, [(i, (i + distance) % 64) for i in range(64)])]
    ppermute x1 -> x0, starting transfers between devices: 6.49 us -> none  [per_device(): twin, got = lax.optimization_barrier((lax.ppermute(half, 'yh', SWAP), got))]
    ppermute x1 -> x0, waiting for transfers between devices: 3.63 us -> none  [per_device(): twin, got = lax.optimization_barrier((lax.ppermute(half, 'yh', SWAP), got))]
    all_to_all x1 -> x2, starting transfers between devices: 5.58 us -> 9.2 us  [exchange(): return lax.all_to_all(pieces, axes, 0, 0)]
    all_to_all x1 -> x2, waiting for transfers between devices: 0.01 us -> 2.23 us  [exchange(): return lax.all_to_all(pieces, axes, 0, 0)]
    ppermute x6, waiting for transfers between devices: 9.45 us -> 11.2 us  [shift(): lax.ppermute(block, DOM, [(i, (i + distance) % 64) for i in range(64)])]
    pallas_call x5 -> x4, Pallas kernels: 4.05 us -> 4.56 us  [the longest x1 2.23 us: per_device(): call(grad_kernel, 'grad', [block, block, block, block, (8, 2 * W + 1, 256...]
  transfers between devices with their start and end apart: 10 -> 10, of which waited for: 6 -> 6; matrix products, arithmetic and copies ran while one was open for 0% -> 0% of each run, Pallas kernels for 1% -> 3%
where the time goes in v5:
time: 173 us; the launch traced here: 172 us
  blocking collectives  81.1 us (47%)
  starting transfers between devices  57.7 us (33%)
  waiting for transfers between devices  16.5 us (10%)
  Pallas kernels  10.8 us (6%)
  local copies, waits for them, and re-layouts  4.08 us (2%)
    all_to_all x4, blocking collectives, exchange(): return lax.all_to_all(pieces, axes, 0, 0)  81.1 us
    ppermute x6, starting transfers between devices, shift(): lax.ppermute(block, DOM, [(i, (i + distance) % 64) for i in range(64)])  44.7 us
    ppermute x6, waiting for transfers between devices, shift(): lax.ppermute(block, DOM, [(i, (i + distance) % 64) for i in range(64)])  11.2 us
    all_to_all x2, starting transfers between devices, exchange(): return lax.all_to_all(pieces, axes, 0, 0)  9.2 us
    unnamed x26, local copies, waits for them, and re-layouts  4.07 us
  transfers between devices with their start and end apart: 10, of which 6 were waited for; matrix products, arithmetic and copies ran while one was open for 0% of the time, Pallas kernels for 3%

profile of v5, /device:TPU:64, one launch (start us, length us, event | category | flops | bytes accessed | tf_op | source)
XLA Modules:
  0.0 172.0 jit_solution(2536370683324563499)
XLA Ops:
  0.6 0.0 copy-start.4
  0.6 0.0 copy-start.5
  0.7 0.9 pad_maximum_fusion.b0
  1.6 9.1 %collective-permute-start.2 = (f32[50,512]{1,0:T(8,128)S(1)}, f32[50,512]{1,0:T(8,128)S(1)}, u32[]{:S(2)}, u32[]{:S(2)}) collective-permute-start(f32[50,512]{1,0:T(8,128)S(1)} %pad_maximum_fusion.b0), channel_id=1, source_target_pairs={{0,24},{8,32},{16,40},{24,48},{32,56},{40,64},{48,72},{56,80},{64,... | collective-permute-start | bytes 307208 | tf_op jit(solution)/shard_map/ppermute | solution.py:236
  10.7 4.3 %collective-permute-start.1 = (f32[50,512]{1,0:T(8,128)S(1)}, f32[50,512]{1,0:T(8,128)S(1)}, u32[]{:S(2)}, u32[]{:S(2)}) collective-permute-start(f32[50,512]{1,0:T(8,128)S(1)} %pad_maximum_fusion.b0), channel_id=1, source_target_pairs={{0,16},{8,24},{16,32},{24,40},{32,48},{40,56},{48,64},{56,72},{64,... | collective-permute-start | bytes 307208 | tf_op jit(solution)/shard_map/ppermute | solution.py:236
  15.0 3.4 %collective-permute-start = (f32[50,512]{1,0:T(8,128)S(1)}, f32[50,512]{1,0:T(8,128)S(1)}, u32[]{:S(2)}, u32[]{:S(2)}) collective-permute-start(f32[50,512]{1,0:T(8,128)S(1)} %pad_maximum_fusion.b0), channel_id=1, source_target_pairs={{0,8},{8,16},{16,24},{24,32},{32,40},{40,48},{48,56},{56,64},{64,7... | collective-permute-start | bytes 307208 | tf_op jit(solution)/shard_map/ppermute | solution.py:236
  18.4 0.0 copy-start.12
  18.4 0.7 copy-done.12
  19.1 0.0 copy-start.11
  19.1 0.0 copy-start.8
  19.1 0.0 copy-start.9
  19.1 0.1 pad_add_fusion.info
  19.2 0.0 copy-done.4
  19.2 0.0 copy-done.5
  19.2 0.6 copy-done.11
  19.8 0.0 copy-done.8
  19.8 0.0 copy-done.9
  19.8 0.0 copy-start
  19.8 1.0 copy-done
  20.8 0.0 copy-start.2
  20.8 1.0 copy-done.2
  21.9 1.5 query.1
  23.4 0.0 copy-start.7
  23.4 4.7 %collective-permute-done.2.b3 = f32[50,512]{1,0:T(8,128)S(1)} collective-permute-done((f32[50,512]{1,0:T(8,128)S(1)}, f32[50,512]{1,0:T(8,128)S(1)}, u32[]{:S(2)}, u32[]{:S(2)}) %collective-permute-start.2) | collective-permute-done | bytes 102432 | tf_op jit(solution)/shard_map/ppermute | solution.py:236
  28.1 4.2 %collective-permute-done.1.b2 = f32[50,512]{1,0:T(8,128)S(1)} collective-permute-done((f32[50,512]{1,0:T(8,128)S(1)}, f32[50,512]{1,0:T(8,128)S(1)}, u32[]{:S(2)}, u32[]{:S(2)}) %collective-permute-start.1) | collective-permute-done | bytes 102432 | tf_op jit(solution)/shard_map/ppermute | solution.py:236
  32.3 0.0 collective-permute-done.b1
  32.3 0.0 copy-done.7
  32.3 1.2 score.1
  33.5 1.9 %collective-permute-start.3 = (f32[4,32,512]{2,1,0:T(8,128)S(1)}, f32[4,32,512]{2,1,0:T(8,128)S(1)}, u32[]{:S(2)}, u32[]{:S(2)}) collective-permute-start(f32[4,32,512]{2,1,0:T(8,128)S(1)} %get-tuple-element.35), channel_id=1, source_target_pairs={{0,1},{1,0},{2,3},{3,2},{4,5},{5,4},{6,7},{7,6},{8,9},{9,8},{10,11... | collective-permute-start | bytes 786440 | tf_op jit(solution)/shard_map/ppermute | solution.py:254
  35.4 1.5 collective-permute-done.3.b
  37.0 16.3 %all_to_all.30.parts = f32[4,32,512]{2,1,0:T(8,128)S(1)} all-to-all(f32[4,32,512]{2,1,0:T(8,128)S(1)} %add.9), channel_id=1, replica_groups=mesh['yh'=2,'x'=4,'z'=8,'yl'=4,'core'=2] {'yl'}, dimensions={0} | all-to-all | bytes 524288 | tf_op jit(solution)/shard_map/all_to_all | solution.py:240
  53.3 0.8 weight.1
  54.0 11.0 %all_to_all.31.w_mine = f32[4,32,512]{2,1,0:T(8,128)S(1)} all-to-all(f32[4,32,512]{2,1,0:T(8,128)S(1)} %weight.1), channel_id=1, replica_groups=mesh['yh'=2,'x'=4,'z'=8,'yl'=4,'core'=2] {'yl'}, dimensions={0} | all-to-all | bytes 524288 | tf_op jit(solution)/shard_map/all_to_all | solution.py:240
  65.0 1.9 %collective-permute-start.4 = (f32[4,32,512]{2,1,0:T(8,128)S(1)}, f32[4,32,512]{2,1,0:T(8,128)S(1)}, u32[]{:S(2)}, u32[]{:S(2)}) collective-permute-start(f32[4,32,512]{2,1,0:T(8,128)S(1)} %all_to_all.31.w_mine), channel_id=1, source_target_pairs={{0,1},{1,0},{2,3},{3,2},{4,5},{5,4},{6,7},{7,6},{8,9},{9,8},{10,11... | collective-permute-start | bytes 786440 | tf_op jit(solution)/shard_map/ppermute | solution.py:258
  66.9 1.5 collective-permute-done.4.w_other
  68.4 2.2 %grad.1 = (f32[50,512]{1,0:T(8,128)S(1)}, f32[50,512]{1,0:T(8,128)S(1)}, f32[50,512]{1,0:T(8,128)S(1)}, f32[50,512]{1,0:T(8,128)S(1)}, f32[8,51,256]{2,1,0:T(8,128)}) custom-call(s32[4]{0:T(128)S(1)} %pad_add_fusion.info, s32[2]{0:T(128)S(1)} %copy-done.7, f32[64,256]{1,0:T(8,128)S(1)} %get-tuple-element.31.q_r, f32[64,256]{1,0:T(8,128)S(1)} %get-tuple-element.32.head_r, ...), custom_call_target="tpu_custom_call" | custom-call | tf_op jit(solution)/shard_map/grad/pallas_call | solution.py:259
  70.7 3.5 %all-to-all-start.2 = ((f32[8,51,256]{2,1,0:T(8,128)}), f32[8,51,256]{2,1,0:T(8,128)S(1)}, u32[]{:S(2)}, u32[]{:S(2)}) async-start(f32[8,51,256]{2,1,0:T(8,128)} %get-tuple-element.38), calls=%async_computation.2 | async-start | bytes 917504 | tf_op jit(solution)/shard_map/all_to_all | solution.py:240
  74.1 4.2 %collective-permute-start.5 = (f32[50,512]{1,0:T(8,128)S(1)}, f32[50,512]{1,0:T(8,128)S(1)}, u32[]{:S(2)}, u32[]{:S(2)}) collective-permute-start(f32[50,512]{1,0:T(8,128)S(1)} %get-tuple-element.39), channel_id=1, source_target_pairs={{0,504},{8,0},{16,8},{24,16},{32,24},{40,32},{48,40},{56,48},{64,5... | collective-permute-start | bytes 307208 | tf_op jit(solution)/shard_map/ppermute | solution.py:236
  78.3 9.4 %collective-permute-start.6 = (f32[50,512]{1,0:T(8,128)S(1)}, f32[50,512]{1,0:T(8,128)S(1)}, u32[]{:S(2)}, u32[]{:S(2)}) collective-permute-start(f32[50,512]{1,0:T(8,128)S(1)} %get-tuple-element.40), channel_id=1, source_target_pairs={{0,496},{8,504},{16,0},{24,8},{32,16},{40,24},{48,32},{56,40},{64,... | collective-permute-start | bytes 307208 | tf_op jit(solution)/shard_map/ppermute | solution.py:236
  87.8 2.2 %all-to-all-done.2.gr = f32[8,51,256]{2,1,0:T(8,128)S(1)} async-done(((f32[8,51,256]{2,1,0:T(8,128)}), f32[8,51,256]{2,1,0:T(8,128)S(1)}, u32[]{:S(2)}, u32[]{:S(2)}) %all-to-all-start.2) | async-done | bytes 417824 | tf_op jit(solution)/shard_map/all_to_all | solution.py:240
  90.0 2.8 %place.1 = f32[8,50,128]{2,1,0:T(8,128)} custom-call(s32[4]{0:T(128)S(1)} %pad_add_fusion.info, f32[8,51,256]{2,1,0:T(8,128)S(1)} %all-to-all-done.2.gr), custom_call_target="tpu_custom_call" | custom-call | tf_op jit(solution)/shard_map/place/pallas_call | solution.py:264
  92.8 0.0 copy-start.1
  92.8 0.0 copy-start.3
  92.8 0.0 collective-permute-done.5.got1
  92.8 0.0 collective-permute-done.6.got2
  92.8 5.7 %all-to-all-start.3 = ((f32[8,50,128]{2,1,0:T(8,128)}), f32[8,50,128]{2,1,0:T(8,128)S(1)}, u32[]{:S(2)}, u32[]{:S(2)}) async-start(f32[8,50,128]{2,1,0:T(8,128)} %place.1), calls=%async_computation.3 | async-start | bytes 458752 | tf_op jit(solution)/shard_map/all_to_all | solution.py:240
  98.5 14.3 %collective-permute-start.7 = (f32[50,512]{1,0:T(8,128)S(1)}, f32[50,512]{1,0:T(8,128)S(1)}, u32[]{:S(2)}, u32[]{:S(2)}) collective-permute-start(f32[50,512]{1,0:T(8,128)S(1)} %get-tuple-element.45), channel_id=1, source_target_pairs={{0,488},{8,496},{16,504},{24,0},{32,8},{40,16},{48,24},{56,32},{64... | collective-permute-start | bytes 307208 | tf_op jit(solution)/shard_map/ppermute | solution.py:236
  112.8 2.3 %collective-permute-done.7.got3 = f32[50,512]{1,0:T(8,128)S(1)} collective-permute-done((f32[50,512]{1,0:T(8,128)S(1)}, f32[50,512]{1,0:T(8,128)S(1)}, u32[]{:S(2)}, u32[]{:S(2)}) %collective-permute-start.7) | collective-permute-done | bytes 102432 | tf_op jit(solution)/shard_map/ppermute | solution.py:236
  115.2 0.0 all-to-all-done.3.parts
  115.2 0.1 square.1
  115.2 0.0 copy-start.6
  115.2 10.3 %all_to_all.32.sq = f32[8,1,640]{2,1,0:T(1,128)S(1)} all-to-all(f32[8,1,640]{2,1,0:T(1,128)S(1)} %get-tuple-element.46), channel_id=1, replica_groups=mesh['yh'=2,'x'=4,'z'=8,'yl'=4,'core'=2] {'yl','core'}, dimensions={0} | all-to-all | bytes 40960 | tf_op jit(solution)/shard_map/all_to_all | solution.py:240
  125.5 0.0 copy-start.10
  125.5 0.0 copy-done.1
  125.5 0.0 copy-done.3
  125.5 0.0 copy-done.6
  125.5 0.7 copy-done.10
  126.2 1.2 update.1
  127.4 43.5 %all_to_all.33.rel = f32[32,51,128]{2,1,0:T(8,128)S(1)} all-to-all(f32[32,51,128]{2,1,0:T(8,128)S(1)} %get-tuple-element.52), channel_id=1, replica_groups=mesh['yh'=2,'x'=4,'z'=8,'yl'=4,'core'=2] {'x','z'}, dimensions={0} | all-to-all | bytes 1671168 | tf_op jit(solution)/shard_map/all_to_all | solution.py:240
  170.9 1.0 spread.1
  (2 shorter events, 0.0 us)
Async XLA Ops:
  0.6 18.6 %copy-start.4 = (f32[25,512]{1,0:T(8,128)S(1)}, f32[25,512]{1,0:T(8,128)}, u32[]{:S(2)}) copy-start(f32[25,512]{1,0:T(8,128)} %ent_re.3) | copy-start | bytes 153604
  0.6 18.6 %copy-start.5 = (f32[25,512]{1,0:T(8,128)S(1)}, f32[25,512]{1,0:T(8,128)}, u32[]{:S(2)}) copy-start(f32[25,512]{1,0:T(8,128)} %ent_im.3) | copy-start | bytes 153604
  1.6 26.5 %collective-permute-start.2 = (f32[50,512]{1,0:T(8,128)S(1)}, f32[50,512]{1,0:T(8,128)S(1)}, u32[]{:S(2)}, u32[]{:S(2)}) collective-permute-start(f32[50,512]{1,0:T(8,128)S(1)} %pad_maximum_fusion.b0), channel_id=1, source_target_pairs={{0,24},{8,32},{16,40},{24,48},{32,56},{40,64},{48,72},{56,80},{64,... | collective-permute-start | bytes 307208 | tf_op jit(solution)/shard_map/ppermute | solution.py:236
  10.7 21.6 %collective-permute-start.1 = (f32[50,512]{1,0:T(8,128)S(1)}, f32[50,512]{1,0:T(8,128)S(1)}, u32[]{:S(2)}, u32[]{:S(2)}) collective-permute-start(f32[50,512]{1,0:T(8,128)S(1)} %pad_maximum_fusion.b0), channel_id=1, source_target_pairs={{0,16},{8,24},{16,32},{24,40},{32,48},{40,56},{48,64},{56,72},{64,... | collective-permute-start | bytes 307208 | tf_op jit(solution)/shard_map/ppermute | solution.py:236
  15.0 17.3 %collective-permute-start = (f32[50,512]{1,0:T(8,128)S(1)}, f32[50,512]{1,0:T(8,128)S(1)}, u32[]{:S(2)}, u32[]{:S(2)}) collective-permute-start(f32[50,512]{1,0:T(8,128)S(1)} %pad_maximum_fusion.b0), channel_id=1, source_target_pairs={{0,8},{8,16},{16,24},{24,32},{32,40},{40,48},{48,56},{56,64},{64,7... | collective-permute-start | bytes 307208 | tf_op jit(solution)/shard_map/ppermute | solution.py:236
  18.4 0.7 copy-start.12
  19.1 0.7 copy-start.11
  19.1 0.7 copy-start.8
  19.1 0.7 copy-start.9
  19.8 1.0 copy-start
  20.8 1.0 copy-start.2
  23.4 8.9 %copy-start.7 = (s32[2]{0:T(128)S(1)}, s32[2]{0:T(128)}, u32[]{:S(2)}) copy-start(s32[2]{0:T(128)} %bucket.5) | copy-start | bytes 28
  33.5 3.4 %collective-permute-start.3 = (f32[4,32,512]{2,1,0:T(8,128)S(1)}, f32[4,32,512]{2,1,0:T(8,128)S(1)}, u32[]{:S(2)}, u32[]{:S(2)}) collective-permute-start(f32[4,32,512]{2,1,0:T(8,128)S(1)} %get-tuple-element.35), channel_id=1, source_target_pairs={{0,1},{1,0},{2,3},{3,2},{4,5},{5,4},{6,7},{7,6},{8,9},{9,8},{10,11... | collective-permute-start | bytes 786440 | tf_op jit(solution)/shard_map/ppermute | solution.py:254
  65.0 3.4 %collective-permute-start.4 = (f32[4,32,512]{2,1,0:T(8,128)S(1)}, f32[4,32,512]{2,1,0:T(8,128)S(1)}, u32[]{:S(2)}, u32[]{:S(2)}) collective-permute-start(f32[4,32,512]{2,1,0:T(8,128)S(1)} %all_to_all.31.w_mine), channel_id=1, source_target_pairs={{0,1},{1,0},{2,3},{3,2},{4,5},{5,4},{6,7},{7,6},{8,9},{9,8},{10,11... | collective-permute-start | bytes 786440 | tf_op jit(solution)/shard_map/ppermute | solution.py:258
  70.7 19.3 %all-to-all-start.2 = ((f32[8,51,256]{2,1,0:T(8,128)}), f32[8,51,256]{2,1,0:T(8,128)S(1)}, u32[]{:S(2)}, u32[]{:S(2)}) async-start(f32[8,51,256]{2,1,0:T(8,128)} %get-tuple-element.38), calls=%async_computation.2 | async-start | bytes 917504 | tf_op jit(solution)/shard_map/all_to_all | solution.py:240
  74.1 18.6 %collective-permute-start.5 = (f32[50,512]{1,0:T(8,128)S(1)}, f32[50,512]{1,0:T(8,128)S(1)}, u32[]{:S(2)}, u32[]{:S(2)}) collective-permute-start(f32[50,512]{1,0:T(8,128)S(1)} %get-tuple-element.39), channel_id=1, source_target_pairs={{0,504},{8,0},{16,8},{24,16},{32,24},{40,32},{48,40},{56,48},{64,5... | collective-permute-start | bytes 307208 | tf_op jit(solution)/shard_map/ppermute | solution.py:236
  78.3 14.4 %collective-permute-start.6 = (f32[50,512]{1,0:T(8,128)S(1)}, f32[50,512]{1,0:T(8,128)S(1)}, u32[]{:S(2)}, u32[]{:S(2)}) collective-permute-start(f32[50,512]{1,0:T(8,128)S(1)} %get-tuple-element.40), channel_id=1, source_target_pairs={{0,496},{8,504},{16,0},{24,8},{32,16},{40,24},{48,32},{56,40},{64,... | collective-permute-start | bytes 307208 | tf_op jit(solution)/shard_map/ppermute | solution.py:236
  92.8 32.8 %copy-start.1 = (f32[25,4096]{1,0:T(8,128)S(1)}, f32[25,4096]{1,0:T(8,128)}, u32[]{:S(2)}) copy-start(f32[25,4096]{1,0:T(8,128)} %rel_re.3) | copy-start | bytes 1228804
  92.8 32.8 %copy-start.3 = (f32[25,4096]{1,0:T(8,128)S(1)}, f32[25,4096]{1,0:T(8,128)}, u32[]{:S(2)}) copy-start(f32[25,4096]{1,0:T(8,128)} %rel_im.3) | copy-start | bytes 1228804
  92.8 22.4 %all-to-all-start.3 = ((f32[8,50,128]{2,1,0:T(8,128)}), f32[8,50,128]{2,1,0:T(8,128)S(1)}, u32[]{:S(2)}, u32[]{:S(2)}) async-start(f32[8,50,128]{2,1,0:T(8,128)} %place.1), calls=%async_computation.3 | async-start | bytes 458752 | tf_op jit(solution)/shard_map/all_to_all | solution.py:240
  98.5 16.7 %collective-permute-start.7 = (f32[50,512]{1,0:T(8,128)S(1)}, f32[50,512]{1,0:T(8,128)S(1)}, u32[]{:S(2)}, u32[]{:S(2)}) collective-permute-start(f32[50,512]{1,0:T(8,128)S(1)} %get-tuple-element.45), channel_id=1, source_target_pairs={{0,488},{8,496},{16,504},{24,0},{32,8},{40,16},{48,24},{56,32},{64... | collective-permute-start | bytes 307208 | tf_op jit(solution)/shard_map/ppermute | solution.py:236
  115.2 10.3 %copy-start.6 = (f32[4096]{0:T(1024)S(1)}, f32[4096]{0:T(1024)}, u32[]{:S(2)}) copy-start(f32[4096]{0:T(1024)} %param.16) | copy-start | bytes 49156
  125.5 0.7 copy-start.10

commit v6 on v3

--- a/solution.py
+++ b/solution.py
@@ -142,7 +142,7 @@
         w_o[i] = w
 
 
-def grad_kernel(info, bucket, q_r, head_r, relc_r, w_mine, w_other, b0, b1, b2, b3, lhs, rel_ids, s0_o, s1_o, s2_o, s3_o, gr_o):
+def grad_kernel(info, bucket, q_r, head_r, relc_r, w_mine, w_other, b0, b1, b2, b3, lhs, rel_ids, s0_o, s1_o, s23_o, gr_o):
     core = info[0]
     mine = w_mine[...].reshape(CH, ROWS)
     other = w_other[...].reshape(CH, ROWS)
@@ -166,20 +166,20 @@
     gr_re = (g_re * h_re + g_im * h_im)[:W]
     gr_im = (g_im * h_re - g_re * h_im)[:W]
     ids = edge_ids(rel_ids).astype(F32)
-    for i in range(4):
+    for i in range(8):
         gr_o[i, 0:W, :] = gr_re
         gr_o[i, W : 2 * W, :] = gr_im
         gr_o[i, 2 * W : 2 * W + 1, :] = ids
-    for ref, slot in zip((s0_o, s1_o, s2_o, s3_o), slots):
-        ref[0:W, :] = slot[:W]
-        ref[W : 2 * W, :] = slot[32 : 32 + W]
+    for ref, at, slot in ((s0_o, 0, 0), (s1_o, 0, 1), (s23_o, 0, 3), (s23_o, 2 * W, 2)):
+        ref[at : at + W, :] = slots[slot][:W]
+        ref[at + W : at + 2 * W, :] = slots[slot][32 : 32 + W]
 
 
 def place_kernel(info, gr, out):
     x = info[1]
     vals = []
     cols = []
-    for i in range(4):
+    for i in range(8):
         vals.append(split3(pack(gr[i, 0 : 2 * W, :])))
         ids = gr[i, 2 * W : 2 * W + 1, :].astype(I32)
         cols.append(jnp.where(jnp.right_shift(ids, 10) == x, jnp.bitwise_and(ids, 1023), -1))
@@ -189,21 +189,16 @@
         out[z, W : 2 * W, :] = total[32 : 32 + W, 128 * z : 128 * z + 128]
 
 
-def fold_kernel(parts, out):
+def total_kernel(parts, out):
     tot = parts[0]
     for i in range(1, 8):
         tot = tot + parts[i]
-    out[...] = tot
-
-
-def both_kernel(a, b, out):
-    tot = a[...] + b[...]
     for i in range(32):
         out[i] = tot
 
 
-def square_kernel(rel, s0, got1, got2, got3, ent_o, sq_o):
-    ent = s0[...] + (got1[...] + (got2[...] + got3[...]))
+def square_kernel(rel, s0, got1, got23, ent_o, sq_o):
+    ent = s0[...] + (got1[...] + got23[2 * W : 4 * W, :])
     ent_o[...] = ent
     es = jnp.sum(ent * ent, 0, keepdims=True)
     for i in range(8):
@@ -258,17 +253,17 @@
     w = call(weight_kernel, "weight", quarter, [SM, SM] + [VM] * 3)(info, bucket_step, s, m, hit)
     w_mine = exchange(w, "yl")
     w_other = lax.ppermute(w_mine, "core", SWAP)
-    s0, s1, s2, s3, gr = call(
-        grad_kernel, "grad", [block, block, block, block, (4, 2 * W + 1, 256)], [SM, SM] + [VM] * 11,
+    s0, s1, s23, gr = call(
+        grad_kernel, "grad", [block, block, (4 * W, ROWS), (8, 2 * W + 1, 256)], [SM, SM] + [VM] * 11,
     )(info, bucket_step, q, head, relc, w_mine, w_other, own, b1, b2, b3, lhs_rows, rel_ids)
-    got = [shift(s1, -1), shift(s2, -2), shift(s3, -3)]
-    gr = exchange(gr, "x")
+    got23 = shift(s23, -2)
+    gr = exchange(gr, ("yh", "x"))
     pieces = call(place_kernel, "place", (8, 2 * W, 128), [SM, VM])(info, gr)
-    half = call(fold_kernel, "fold", (2 * W, 128), [VM])(exchange(pieces, "z"))
-    twin, got = lax.optimization_barrier((lax.ppermute(half, "yh", SWAP), got))
-    rel = call(both_kernel, "both", (32, 2 * W, 128), [VM] * 2)(half, twin)
+    pieces, got23 = lax.optimization_barrier((pieces, got23))
+    got1 = shift(s1 + got23[: 2 * W], -1)
+    rel = call(total_kernel, "total", (32, 2 * W, 128), [VM])(exchange(pieces, "z"))
     rel = exchange(rel, ("x", "z"))
-    ent, sq = call(square_kernel, "square", [block, (8, 1, ROWS + REL)], [VM] * 5)(rel, s0, *got)
+    ent, sq = call(square_kernel, "square", [block, (8, 1, ROWS + REL)], [VM] * 4)(rel, s0, got1, got23)
     sq = exchange(sq, DIM)
     new_re, new_im, new_acc, new_rel_re, new_rel_im, new_rel_acc = call(
         update_kernel, "update", [(W, ROWS), (W, ROWS), (1, ROWS), (W, REL), (W, REL), (1, REL)], [VM] * 9

time: 163 us -> 162 us (level)
  blocking collectives: 78.8 us -> 53.2 us
  waiting for transfers between devices: 20.2 us -> 34 us
  starting transfers between devices: 49 us -> 57.4 us
    all_to_all x5 -> x4, blocking collectives: 78.8 us -> 53.2 us  [exchange(): return lax.all_to_all(pieces, axes, 0, 0)]
    ppermute x6 -> x5, waiting for transfers between devices: 16.2 us -> 26 us  [shift(): lax.ppermute(block, DOM, [(i, (i + distance) % 64) for i in range(64)])]
    ppermute x6 -> x5, starting transfers between devices: 30.6 us -> 39.5 us  [shift(): lax.ppermute(block, DOM, [(i, (i + distance) % 64) for i in range(64)])]
    ppermute x1 -> x0, starting transfers between devices: 6.21 us -> none  [per_device(): twin, got = lax.optimization_barrier((lax.ppermute(half, 'yh', SWAP), got))]
    all_to_all x1 -> x2, starting transfers between devices: 3.4 us -> 9.18 us  [exchange(): return lax.all_to_all(pieces, axes, 0, 0)]
    all_to_all x1 -> x2, waiting for transfers between devices: 0.01 us -> 5.71 us  [exchange(): return lax.all_to_all(pieces, axes, 0, 0)]
    ppermute x1 -> x0, waiting for transfers between devices: 1.65 us -> none  [per_device(): twin, got = lax.optimization_barrier((lax.ppermute(half, 'yh', SWAP), got))]
    pallas_call x4 -> x3, Pallas kernels: 1.82 us -> 3.37 us  [the longest x1 2.23 us: per_device(): call(grad_kernel, 'grad', [block, block, (4 * W, ROWS), (8, 2 * W + 1, 25...]
  transfers between devices with their start and end apart: 10 -> 9, of which waited for: 7 -> 8; matrix products, arithmetic and copies ran while one was open for 0% -> 0% of each run, Pallas kernels for 1% -> 2%
where the time goes in v6:
time: 162 us; the launch traced here: 161 us
  starting transfers between devices  57.4 us (35%)
  blocking collectives  53.2 us (33%)
  waiting for transfers between devices  34 us (21%)
  Pallas kernels  10 us (6%)
  local copies, waits for them, and re-layouts  4.08 us (3%)
    all_to_all x4, blocking collectives, exchange(): return lax.all_to_all(pieces, axes, 0, 0)  53.2 us
    ppermute x5, starting transfers between devices, shift(): lax.ppermute(block, DOM, [(i, (i + distance) % 64) for i in range(64)])  39.5 us
    ppermute x5, waiting for transfers between devices, shift(): lax.ppermute(block, DOM, [(i, (i + distance) % 64) for i in range(64)])  26 us
    all_to_all x2, starting transfers between devices, exchange(): return lax.all_to_all(pieces, axes, 0, 0)  9.18 us
    all_to_all x2, waiting for transfers between devices, exchange(): return lax.all_to_all(pieces, axes, 0, 0)  5.71 us
    ppermute x1, starting transfers between devices, per_device(): w_other = lax.ppermute(w_mine, 'core', SWAP)  5.66 us
    unnamed x26, local copies, waits for them, and re-layouts  4.08 us
  transfers between devices with their start and end apart: 9, of which 8 were waited for; matrix products, arithmetic and copies ran while one was open for 0% of the time, Pallas kernels for 2%

profile of v6, /device:TPU:1, one launch (start us, length us, event | category | flops | bytes accessed | tf_op | source)
XLA Modules:
  0.0 160.6 jit_solution(16511658342303996825)
XLA Ops:
  0.6 0.0 copy-start.4
  0.6 0.0 copy-start.5
  0.7 0.9 pad_maximum_fusion.b0
  1.6 8.4 %collective-permute-start.2 = (f32[50,512]{1,0:T(8,128)S(1)}, f32[50,512]{1,0:T(8,128)S(1)}, u32[]{:S(2)}, u32[]{:S(2)}) collective-permute-start(f32[50,512]{1,0:T(8,128)S(1)} %pad_maximum_fusion.b0), channel_id=1, source_target_pairs={{0,24},{8,32},{16,40},{24,48},{32,56},{40,64},{48,72},{56,80},{64,... | collective-permute-start | bytes 307208 | tf_op jit(solution)/shard_map/ppermute | solution.py:233
  10.0 6.1 %collective-permute-start.1 = (f32[50,512]{1,0:T(8,128)S(1)}, f32[50,512]{1,0:T(8,128)S(1)}, u32[]{:S(2)}, u32[]{:S(2)}) collective-permute-start(f32[50,512]{1,0:T(8,128)S(1)} %pad_maximum_fusion.b0), channel_id=1, source_target_pairs={{0,16},{8,24},{16,32},{24,40},{32,48},{40,56},{48,64},{56,72},{64,... | collective-permute-start | bytes 307208 | tf_op jit(solution)/shard_map/ppermute | solution.py:233
  16.2 3.1 %collective-permute-start = (f32[50,512]{1,0:T(8,128)S(1)}, f32[50,512]{1,0:T(8,128)S(1)}, u32[]{:S(2)}, u32[]{:S(2)}) collective-permute-start(f32[50,512]{1,0:T(8,128)S(1)} %pad_maximum_fusion.b0), channel_id=1, source_target_pairs={{0,8},{8,16},{16,24},{24,32},{32,40},{40,48},{48,56},{56,64},{64,7... | collective-permute-start | bytes 307208 | tf_op jit(solution)/shard_map/ppermute | solution.py:233
  19.3 0.0 copy-start.12
  19.3 0.7 copy-done.12
  20.0 0.0 copy-start.11
  20.0 0.0 copy-start.8
  20.0 0.0 copy-start.9
  20.0 0.1 pad_add_fusion.info
  20.1 0.0 copy-done.4
  20.1 0.0 copy-done.5
  20.1 0.6 copy-done.11
  20.7 0.0 copy-done.8
  20.7 0.0 copy-done.9
  20.7 0.0 copy-start
  20.7 1.0 copy-done
  21.7 0.0 copy-start.2
  21.7 1.0 copy-done.2
  22.8 1.5 query.1
  24.3 0.0 copy-start.7
  24.3 0.3 collective-permute-done.2.b3
  24.6 10.5 %collective-permute-done.1.b2 = f32[50,512]{1,0:T(8,128)S(1)} collective-permute-done((f32[50,512]{1,0:T(8,128)S(1)}, f32[50,512]{1,0:T(8,128)S(1)}, u32[]{:S(2)}, u32[]{:S(2)}) %collective-permute-start.1) | collective-permute-done | bytes 102432 | tf_op jit(solution)/shard_map/ppermute | solution.py:233
  35.1 0.8 collective-permute-done.b1
  35.9 0.0 copy-done.7
  36.0 1.2 score.1
  37.1 3.1 %collective-permute-start.3 = (f32[4,32,512]{2,1,0:T(8,128)S(1)}, f32[4,32,512]{2,1,0:T(8,128)S(1)}, u32[]{:S(2)}, u32[]{:S(2)}) collective-permute-start(f32[4,32,512]{2,1,0:T(8,128)S(1)} %get-tuple-element.31), channel_id=1, source_target_pairs={{0,1},{1,0},{2,3},{3,2},{4,5},{5,4},{6,7},{7,6},{8,9},{9,8},{10,11... | collective-permute-start | bytes 786440 | tf_op jit(solution)/shard_map/ppermute | solution.py:251
  40.3 1.1 collective-permute-done.3.b
  41.4 13.2 %all_to_all.30.parts = f32[4,32,512]{2,1,0:T(8,128)S(1)} all-to-all(f32[4,32,512]{2,1,0:T(8,128)S(1)} %add.12), channel_id=1, replica_groups=mesh['yh'=2,'x'=4,'z'=8,'yl'=4,'core'=2] {'yl'}, dimensions={0} | all-to-all | bytes 524288 | tf_op jit(solution)/shard_map/all_to_all | solution.py:237
  54.6 0.8 weight.1
  55.4 10.0 %all_to_all.31.w_mine = f32[4,32,512]{2,1,0:T(8,128)S(1)} all-to-all(f32[4,32,512]{2,1,0:T(8,128)S(1)} %weight.1), channel_id=1, replica_groups=mesh['yh'=2,'x'=4,'z'=8,'yl'=4,'core'=2] {'yl'}, dimensions={0} | all-to-all | bytes 524288 | tf_op jit(solution)/shard_map/all_to_all | solution.py:237
  65.4 5.7 %collective-permute-start.4 = (f32[4,32,512]{2,1,0:T(8,128)S(1)}, f32[4,32,512]{2,1,0:T(8,128)S(1)}, u32[]{:S(2)}, u32[]{:S(2)}) collective-permute-start(f32[4,32,512]{2,1,0:T(8,128)S(1)} %all_to_all.31.w_mine), channel_id=1, source_target_pairs={{0,1},{1,0},{2,3},{3,2},{4,5},{5,4},{6,7},{7,6},{8,9},{9,8},{10,11... | collective-permute-start | bytes 786440 | tf_op jit(solution)/shard_map/ppermute | solution.py:255
  71.0 1.1 collective-permute-done.4.w_other
  72.2 2.2 %grad.1 = (f32[50,512]{1,0:T(8,128)S(1)}, f32[50,512]{1,0:T(8,128)S(1)}, f32[100,512]{1,0:T(8,128)S(1)}, f32[8,51,256]{2,1,0:T(8,128)}) custom-call(s32[3]{0:T(128)S(1)} %pad_add_fusion.info, s32[2]{0:T(128)S(1)} %copy-done.7, f32[64,256]{1,0:T(8,128)S(1)} %get-tuple-element.27.q_r, f32[64,256]{1,0:T(8,128)S(1)} %get-tuple-element.28.head_r, ...), custom_call_target="tpu_custom_call" | custom-call | tf_op jit(solution)/shard_map/grad/pallas_call | solution.py:256
  74.4 3.5 %all-to-all-start.2 = ((f32[8,51,256]{2,1,0:T(8,128)}), f32[8,51,256]{2,1,0:T(8,128)S(1)}, u32[]{:S(2)}, u32[]{:S(2)}) async-start(f32[8,51,256]{2,1,0:T(8,128)} %get-tuple-element.34), calls=%async_computation.2 | async-start | bytes 917504 | tf_op jit(solution)/shard_map/all_to_all | solution.py:237
  77.9 8.6 %collective-permute-start.5 = (f32[100,512]{1,0:T(8,128)S(1)}, f32[100,512]{1,0:T(8,128)S(1)}, u32[]{:S(2)}, u32[]{:S(2)}) collective-permute-start(f32[100,512]{1,0:T(8,128)S(1)} %get-tuple-element.35), channel_id=1, source_target_pairs={{0,496},{8,504},{16,0},{24,8},{32,16},{40,24},{48,32},{56,40},{64,... | collective-permute-start | bytes 614408 | tf_op jit(solution)/shard_map/ppermute | solution.py:233
  86.5 5.7 %all-to-all-done.2.gr = f32[8,51,256]{2,1,0:T(8,128)S(1)} async-done(((f32[8,51,256]{2,1,0:T(8,128)}), f32[8,51,256]{2,1,0:T(8,128)S(1)}, u32[]{:S(2)}, u32[]{:S(2)}) %all-to-all-start.2) | async-done | bytes 417824 | tf_op jit(solution)/shard_map/all_to_all | solution.py:237
  92.2 2.1 %place.1 = f32[8,50,128]{2,1,0:T(8,128)S(1)} custom-call(s32[3]{0:T(128)S(1)} %pad_add_fusion.info, f32[8,51,256]{2,1,0:T(8,128)S(1)} %all-to-all-done.2.gr), custom_call_target="tpu_custom_call" | custom-call | tf_op jit(solution)/shard_map/place/pallas_call | solution.py:261
  94.3 6.7 %collective-permute-done.5.got23 = f32[100,512]{1,0:T(8,128)S(1)} collective-permute-done((f32[100,512]{1,0:T(8,128)S(1)}, f32[100,512]{1,0:T(8,128)S(1)}, u32[]{:S(2)}, u32[]{:S(2)}) %collective-permute-start.5) | collective-permute-done | bytes 204832 | tf_op jit(solution)/shard_map/ppermute | solution.py:233
  101.0 13.5 %all_to_all.32.parts = f32[8,50,128]{2,1,0:T(8,128)S(1)} all-to-all(f32[8,50,128]{2,1,0:T(8,128)S(1)} %place.1), channel_id=1, replica_groups=mesh['yh'=2,'x'=4,'z'=8,'yl'=4,'core'=2] {'z'}, dimensions={0} | all-to-all | bytes 409600 | tf_op jit(solution)/shard_map/all_to_all | solution.py:237
  114.4 1.0 total.1
  115.4 5.7 %all-to-all-start.4 = ((f32[32,50,128]{2,1,0:T(8,128)}), f32[32,50,128]{2,1,0:T(8,128)S(1)}, u32[]{:S(2)}, u32[]{:S(2)}) async-start(f32[32,50,128]{2,1,0:T(8,128)} %total.1), calls=%async_computation.4 | async-start | bytes 1835008 | tf_op jit(solution)/shard_map/all_to_all | solution.py:237
  121.2 13.2 %collective-permute-start.6 = (f32[50,512]{1,0:T(8,128)S(1)}, f32[50,512]{1,0:T(8,128)S(1)}, u32[]{:S(2)}, u32[]{:S(2)}) collective-permute-start(f32[50,512]{1,0:T(8,128)S(1)} %slice_add_fusion), channel_id=1, source_target_pairs={{0,504},{8,0},{16,8},{24,16},{32,24},{40,32},{48,40},{56,48},{64,5... | collective-permute-start | bytes 307208 | tf_op jit(solution)/shard_map/ppermute | solution.py:233
  134.4 7.7 %collective-permute-done.6.got1 = f32[50,512]{1,0:T(8,128)S(1)} collective-permute-done((f32[50,512]{1,0:T(8,128)S(1)}, f32[50,512]{1,0:T(8,128)S(1)}, u32[]{:S(2)}, u32[]{:S(2)}) %collective-permute-start.6) | collective-permute-done | bytes 102432 | tf_op jit(solution)/shard_map/ppermute | solution.py:233
  142.1 0.0 all-to-all-done.4.rel
  142.1 0.0 copy-start.1
  142.1 0.0 copy-start.3
  142.1 0.1 square.1
  142.3 0.0 copy-start.6
  142.3 16.5 %all_to_all.33.sq = f32[8,1,4608]{2,1,0:T(1,128)S(1)} all-to-all(f32[8,1,4608]{2,1,0:T(1,128)S(1)} %get-tuple-element.40), channel_id=1, replica_groups=mesh['yh'=2,'x'=4,'z'=8,'yl'=4,'core'=2] {'yl','core'}, dimensions={0} | all-to-all | bytes 294912 | tf_op jit(solution)/shard_map/all_to_all | solution.py:237
  158.8 0.0 copy-start.10
  158.8 0.0 copy-done.1
  158.8 0.0 copy-done.3
  158.8 0.0 copy-done.6
  158.8 0.7 copy-done.10
  159.5 1.1 update.1
  (3 shorter events, 0.1 us)
Async XLA Ops:
  0.6 19.5 %copy-start.4 = (f32[25,512]{1,0:T(8,128)S(1)}, f32[25,512]{1,0:T(8,128)}, u32[]{:S(2)}) copy-start(f32[25,512]{1,0:T(8,128)} %ent_re.3) | copy-start | bytes 153604
  0.6 19.4 %copy-start.5 = (f32[25,512]{1,0:T(8,128)S(1)}, f32[25,512]{1,0:T(8,128)}, u32[]{:S(2)}) copy-start(f32[25,512]{1,0:T(8,128)} %ent_im.3) | copy-start | bytes 153604
  1.6 23.0 %collective-permute-start.2 = (f32[50,512]{1,0:T(8,128)S(1)}, f32[50,512]{1,0:T(8,128)S(1)}, u32[]{:S(2)}, u32[]{:S(2)}) collective-permute-start(f32[50,512]{1,0:T(8,128)S(1)} %pad_maximum_fusion.b0), channel_id=1, source_target_pairs={{0,24},{8,32},{16,40},{24,48},{32,56},{40,64},{48,72},{56,80},{64,... | collective-permute-start | bytes 307208 | tf_op jit(solution)/shard_map/ppermute | solution.py:233
  10.0 25.1 %collective-permute-start.1 = (f32[50,512]{1,0:T(8,128)S(1)}, f32[50,512]{1,0:T(8,128)S(1)}, u32[]{:S(2)}, u32[]{:S(2)}) collective-permute-start(f32[50,512]{1,0:T(8,128)S(1)} %pad_maximum_fusion.b0), channel_id=1, source_target_pairs={{0,16},{8,24},{16,32},{24,40},{32,48},{40,56},{48,64},{56,72},{64,... | collective-permute-start | bytes 307208 | tf_op jit(solution)/shard_map/ppermute | solution.py:233
  16.2 19.8 %collective-permute-start = (f32[50,512]{1,0:T(8,128)S(1)}, f32[50,512]{1,0:T(8,128)S(1)}, u32[]{:S(2)}, u32[]{:S(2)}) collective-permute-start(f32[50,512]{1,0:T(8,128)S(1)} %pad_maximum_fusion.b0), channel_id=1, source_target_pairs={{0,8},{8,16},{16,24},{24,32},{32,40},{40,48},{48,56},{56,64},{64,7... | collective-permute-start | bytes 307208 | tf_op jit(solution)/shard_map/ppermute | solution.py:233
  19.3 0.7 copy-start.12
  20.0 0.7 copy-start.11
  20.0 0.7 copy-start.8
  20.0 0.7 copy-start.9
  20.7 1.0 copy-start
  21.7 1.0 copy-start.2
  24.3 11.6 %copy-start.7 = (s32[2]{0:T(128)S(1)}, s32[2]{0:T(128)}, u32[]{:S(2)}) copy-start(s32[2]{0:T(128)} %bucket.5) | copy-start | bytes 28
  37.1 4.3 %collective-permute-start.3 = (f32[4,32,512]{2,1,0:T(8,128)S(1)}, f32[4,32,512]{2,1,0:T(8,128)S(1)}, u32[]{:S(2)}, u32[]{:S(2)}) collective-permute-start(f32[4,32,512]{2,1,0:T(8,128)S(1)} %get-tuple-element.31), channel_id=1, source_target_pairs={{0,1},{1,0},{2,3},{3,2},{4,5},{5,4},{6,7},{7,6},{8,9},{9,8},{10,11... | collective-permute-start | bytes 786440 | tf_op jit(solution)/shard_map/ppermute | solution.py:251
  65.4 6.8 %collective-permute-start.4 = (f32[4,32,512]{2,1,0:T(8,128)S(1)}, f32[4,32,512]{2,1,0:T(8,128)S(1)}, u32[]{:S(2)}, u32[]{:S(2)}) collective-permute-start(f32[4,32,512]{2,1,0:T(8,128)S(1)} %all_to_all.31.w_mine), channel_id=1, source_target_pairs={{0,1},{1,0},{2,3},{3,2},{4,5},{5,4},{6,7},{7,6},{8,9},{9,8},{10,11... | collective-permute-start | bytes 786440 | tf_op jit(solution)/shard_map/ppermute | solution.py:255
  74.4 17.8 %all-to-all-start.2 = ((f32[8,51,256]{2,1,0:T(8,128)}), f32[8,51,256]{2,1,0:T(8,128)S(1)}, u32[]{:S(2)}, u32[]{:S(2)}) async-start(f32[8,51,256]{2,1,0:T(8,128)} %get-tuple-element.34), calls=%async_computation.2 | async-start | bytes 917504 | tf_op jit(solution)/shard_map/all_to_all | solution.py:237
  77.9 23.1 %collective-permute-start.5 = (f32[100,512]{1,0:T(8,128)S(1)}, f32[100,512]{1,0:T(8,128)S(1)}, u32[]{:S(2)}, u32[]{:S(2)}) collective-permute-start(f32[100,512]{1,0:T(8,128)S(1)} %get-tuple-element.35), channel_id=1, source_target_pairs={{0,496},{8,504},{16,0},{24,8},{32,16},{40,24},{48,32},{56,40},{64,... | collective-permute-start | bytes 614408 | tf_op jit(solution)/shard_map/ppermute | solution.py:233
  115.4 26.7 %all-to-all-start.4 = ((f32[32,50,128]{2,1,0:T(8,128)}), f32[32,50,128]{2,1,0:T(8,128)S(1)}, u32[]{:S(2)}, u32[]{:S(2)}) async-start(f32[32,50,128]{2,1,0:T(8,128)} %total.1), calls=%async_computation.4 | async-start | bytes 1835008 | tf_op jit(solution)/shard_map/all_to_all | solution.py:237
  121.2 20.9 %collective-permute-start.6 = (f32[50,512]{1,0:T(8,128)S(1)}, f32[50,512]{1,0:T(8,128)S(1)}, u32[]{:S(2)}, u32[]{:S(2)}) collective-permute-start(f32[50,512]{1,0:T(8,128)S(1)} %slice_add_fusion), channel_id=1, source_target_pairs={{0,504},{8,0},{16,8},{24,16},{32,24},{40,32},{48,40},{56,48},{64,5... | collective-permute-start | bytes 307208 | tf_op jit(solution)/shard_map/ppermute | solution.py:233
  142.1 16.7 %copy-start.1 = (f32[25,4096]{1,0:T(8,128)S(1)}, f32[25,4096]{1,0:T(8,128)}, u32[]{:S(2)}) copy-start(f32[25,4096]{1,0:T(8,128)} %rel_re.3) | copy-start | bytes 1228804
  142.1 16.7 %copy-start.3 = (f32[25,4096]{1,0:T(8,128)S(1)}, f32[25,4096]{1,0:T(8,128)}, u32[]{:S(2)}) copy-start(f32[25,4096]{1,0:T(8,128)} %rel_im.3) | copy-start | bytes 1228804
  142.3 16.6 %copy-start.6 = (f32[4096]{0:T(1024)S(1)}, f32[4096]{0:T(1024)}, u32[]{:S(2)}) copy-start(f32[4096]{0:T(1024)} %param.16) | copy-start | bytes 49156
  158.8 0.7 copy-start.10

commit v7 on v3

--- a/solution.py
+++ b/solution.py
@@ -196,14 +196,22 @@
     out[...] = tot
 
 
-def both_kernel(a, b, out):
+def both_kernel(info, a, b, s0, got1, got2, got3, out, ring_o, wrap_o):
     tot = a[...] + b[...]
     for i in range(32):
         out[i] = tot
-
-
-def square_kernel(rel, s0, got1, got2, got3, ent_o, sq_o):
-    ent = s0[...] + (got1[...] + (got2[...] + got3[...]))
+    z = info[3]
+    ring = s0[...]
+    wrap = jnp.zeros_like(ring)
+    for s, got in ((1, got1), (2, got2), (3, got3)):
+        ring = ring + jnp.where(z + s < 8, got[...], 0.0)
+        wrap = wrap + jnp.where(z + s < 8, 0.0, got[...])
+    ring_o[...] = ring
+    wrap_o[...] = wrap
+
+
+def square_kernel(rel, ring, wrap, ent_o, sq_o):
+    ent = ring[...] + wrap[...]
     ent_o[...] = ent
     es = jnp.sum(ent * ent, 0, keepdims=True)
     for i in range(8):
@@ -243,7 +251,7 @@
 
 
 def per_device(ent_re, ent_im, ent_acc, rel_re, rel_im, rel_acc, lhs_rows, rhs_rows, rel_ids, neg_rows, bucket_step):
-    info = jnp.stack([lax.axis_index("core"), lax.axis_index("x"), lax.axis_index("yl")]).astype(I32)
+    info = jnp.stack([lax.axis_index("core"), lax.axis_index("x"), lax.axis_index("yl"), lax.axis_index("z")]).astype(I32)
     own = jnp.concatenate([ent_re, ent_im], 0)
     b1, b2, b3 = [shift(own, d) for d in (1, 2, 3)]
     neg = jnp.pad(neg_rows, ((0, 0), (0, 24)), constant_values=-1)
@@ -261,14 +269,15 @@
     s0, s1, s2, s3, gr = call(
         grad_kernel, "grad", [block, block, block, block, (4, 2 * W + 1, 256)], [SM, SM] + [VM] * 11,
     )(info, bucket_step, q, head, relc, w_mine, w_other, own, b1, b2, b3, lhs_rows, rel_ids)
-    got = [shift(s1, -1), shift(s2, -2), shift(s3, -3)]
+    got = [lax.ppermute(v, "z", [(i, (i - d) % 8) for i in range(8)]) for d, v in ((1, s1), (2, s2), (3, s3))]
     gr = exchange(gr, "x")
     pieces = call(place_kernel, "place", (8, 2 * W, 128), [SM, VM])(info, gr)
     half = call(fold_kernel, "fold", (2 * W, 128), [VM])(exchange(pieces, "z"))
     twin, got = lax.optimization_barrier((lax.ppermute(half, "yh", SWAP), got))
-    rel = call(both_kernel, "both", (32, 2 * W, 128), [VM] * 2)(half, twin)
+    rel, ring, wrap = call(both_kernel, "both", [(32, 2 * W, 128), block, block], [SM] + [VM] * 6)(info, half, twin, s0, *got)
+    wrap = lax.ppermute(wrap, DOM, [(i, (i - 8) % 64) for i in range(64) if i % 8 >= 5])
     rel = exchange(rel, ("x", "z"))
-    ent, sq = call(square_kernel, "square", [block, (8, 1, ROWS + REL)], [VM] * 5)(rel, s0, *got)
+    ent, sq = call(square_kernel, "square", [block, (8, 1, ROWS + REL)], [VM] * 3)(rel, ring, wrap)
     sq = exchange(sq, DIM)
     new_re, new_im, new_acc, new_rel_re, new_rel_im, new_rel_acc = call(
         update_kernel, "update", [(W, ROWS), (W, ROWS), (1, ROWS), (W, REL), (W, REL), (1, REL)], [VM] * 9

time: 163 us -> 156 us (0.957)
  blocking collectives: 78.8 us -> 45.3 us
  waiting for transfers between devices: 20.2 us -> 40.7 us
  starting transfers between devices: 49 us -> 53.1 us
    all_to_all x5 -> x4, blocking collectives: 78.8 us -> 45.3 us  [exchange(): return lax.all_to_all(pieces, axes, 0, 0)]
    all_to_all x1 -> x2, waiting for transfers between devices: 0.01 us -> 21.3 us  [exchange(): return lax.all_to_all(pieces, axes, 0, 0)]
    ppermute x6 -> x3, starting transfers between devices: 30.6 us -> 17.7 us  [shift(): lax.ppermute(block, DOM, [(i, (i + distance) % 64) for i in range(64)])]
    ppermute x0 -> x4, starting transfers between devices: none -> 12.2 us  [the longest x3 11.6 us: per_device(): lax.ppermute(v, 'z', [(i, (i - d) % 8) for i in range(8)])]
    all_to_all x1 -> x2, starting transfers between devices: 3.4 us -> 11.5 us  [exchange(): return lax.all_to_all(pieces, axes, 0, 0)]
    ppermute x0 -> x4, waiting for transfers between devices: none -> 5.36 us  [the longest x3 5.36 us: per_device(): lax.ppermute(v, 'z', [(i, (i - d) % 8) for i in range(8)])]
    ppermute x6 -> x3, waiting for transfers between devices: 16.2 us -> 11.6 us  [shift(): lax.ppermute(block, DOM, [(i, (i + distance) % 64) for i in range(64)])]
    ppermute x1, starting transfers between devices: 6.21 us -> 2.98 us  [per_device(): twin, got = lax.optimization_barrier((lax.ppermute(half, 'yh', SWAP), got))]
  transfers between devices with their start and end apart: 10 -> 12, of which waited for: 7 -> 9; matrix products, arithmetic and copies ran while one was open for 0% -> 0% of each run, Pallas kernels for 1% -> 1%
where the time goes in v7:
time: 156 us; the launch traced here: 155 us
  starting transfers between devices  53.1 us (34%)
  blocking collectives  45.3 us (29%)
  waiting for transfers between devices  40.7 us (26%)
  Pallas kernels  9.97 us (6%)
  local copies, waits for them, and re-layouts  4.08 us (3%)
    all_to_all x4, blocking collectives, exchange(): return lax.all_to_all(pieces, axes, 0, 0)  45.3 us
    all_to_all x2, waiting for transfers between devices, exchange(): return lax.all_to_all(pieces, axes, 0, 0)  21.3 us
    ppermute x3, starting transfers between devices, shift(): lax.ppermute(block, DOM, [(i, (i + distance) % 64) for i in range(64)])  17.7 us
    ppermute x3, waiting for transfers between devices, shift(): lax.ppermute(block, DOM, [(i, (i + distance) % 64) for i in range(64)])  11.6 us
    ppermute x3, starting transfers between devices, per_device(): lax.ppermute(v, 'z', [(i, (i - d) % 8) for i in range(8)])  11.6 us
    all_to_all x2, starting transfers between devices, exchange(): return lax.all_to_all(pieces, axes, 0, 0)  11.5 us
    ppermute x1, starting transfers between devices, per_device(): w_other = lax.ppermute(w_mine, 'core', SWAP)  5.66 us
    ppermute x3, waiting for transfers between devices, per_device(): lax.ppermute(v, 'z', [(i, (i - d) % 8) for i in range(8)])  5.36 us
  transfers between devices with their start and end apart: 12, of which 9 were waited for; matrix products, arithmetic and copies ran while one was open for 0% of the time, Pallas kernels for 1%

profile of v7, /device:TPU:1, one launch (start us, length us, event | category | flops | bytes accessed | tf_op | source)
XLA Modules:
  0.0 155.1 jit_solution(201822219595656954)
XLA Ops:
  0.6 0.0 copy-start.4
  0.6 0.0 copy-start.5
  0.7 0.9 pad_maximum_fusion.b0
  1.6 8.4 %collective-permute-start.2 = (f32[50,512]{1,0:T(8,128)S(1)}, f32[50,512]{1,0:T(8,128)S(1)}, u32[]{:S(2)}, u32[]{:S(2)}) collective-permute-start(f32[50,512]{1,0:T(8,128)S(1)} %pad_maximum_fusion.b0), channel_id=1, source_target_pairs={{0,24},{8,32},{16,40},{24,48},{32,56},{40,64},{48,72},{56,80},{64,... | collective-permute-start | bytes 307208 | tf_op jit(solution)/shard_map/ppermute | solution.py:246
  10.0 6.1 %collective-permute-start.1 = (f32[50,512]{1,0:T(8,128)S(1)}, f32[50,512]{1,0:T(8,128)S(1)}, u32[]{:S(2)}, u32[]{:S(2)}) collective-permute-start(f32[50,512]{1,0:T(8,128)S(1)} %pad_maximum_fusion.b0), channel_id=1, source_target_pairs={{0,16},{8,24},{16,32},{24,40},{32,48},{40,56},{48,64},{56,72},{64,... | collective-permute-start | bytes 307208 | tf_op jit(solution)/shard_map/ppermute | solution.py:246
  16.2 3.1 %collective-permute-start = (f32[50,512]{1,0:T(8,128)S(1)}, f32[50,512]{1,0:T(8,128)S(1)}, u32[]{:S(2)}, u32[]{:S(2)}) collective-permute-start(f32[50,512]{1,0:T(8,128)S(1)} %pad_maximum_fusion.b0), channel_id=1, source_target_pairs={{0,8},{8,16},{16,24},{24,32},{32,40},{40,48},{48,56},{56,64},{64,7... | collective-permute-start | bytes 307208 | tf_op jit(solution)/shard_map/ppermute | solution.py:246
  19.3 0.0 copy-start.12
  19.3 0.7 copy-done.12
  20.0 0.0 copy-start.11
  20.0 0.0 copy-start.8
  20.0 0.0 copy-start.9
  20.0 0.1 pad_add_fusion.info
  20.1 0.0 copy-done.4
  20.1 0.0 copy-done.5
  20.1 0.6 copy-done.11
  20.7 0.0 copy-done.8
  20.7 0.0 copy-done.9
  20.7 0.0 copy-start
  20.7 1.0 copy-done
  21.7 0.0 copy-start.2
  21.7 1.0 copy-done.2
  22.8 1.5 query.1
  24.3 0.0 copy-start.7
  24.3 0.3 collective-permute-done.2.b3
  24.6 10.5 %collective-permute-done.1.b2 = f32[50,512]{1,0:T(8,128)S(1)} collective-permute-done((f32[50,512]{1,0:T(8,128)S(1)}, f32[50,512]{1,0:T(8,128)S(1)}, u32[]{:S(2)}, u32[]{:S(2)}) %collective-permute-start.1) | collective-permute-done | bytes 102432 | tf_op jit(solution)/shard_map/ppermute | solution.py:246
  35.1 0.8 collective-permute-done.b1
  35.9 0.0 copy-done.7
  36.0 1.2 score.1
  37.1 3.1 %collective-permute-start.3 = (f32[4,32,512]{2,1,0:T(8,128)S(1)}, f32[4,32,512]{2,1,0:T(8,128)S(1)}, u32[]{:S(2)}, u32[]{:S(2)}) collective-permute-start(f32[4,32,512]{2,1,0:T(8,128)S(1)} %get-tuple-element.37), channel_id=1, source_target_pairs={{0,1},{1,0},{2,3},{3,2},{4,5},{5,4},{6,7},{7,6},{8,9},{9,8},{10,11... | collective-permute-start | bytes 786440 | tf_op jit(solution)/shard_map/ppermute | solution.py:264
  40.3 1.1 collective-permute-done.3.b
  41.4 13.2 %all_to_all.30.parts = f32[4,32,512]{2,1,0:T(8,128)S(1)} all-to-all(f32[4,32,512]{2,1,0:T(8,128)S(1)} %add.9), channel_id=1, replica_groups=mesh['yh'=2,'x'=4,'z'=8,'yl'=4,'core'=2] {'yl'}, dimensions={0} | all-to-all | bytes 524288 | tf_op jit(solution)/shard_map/all_to_all | solution.py:250
  54.6 0.8 weight.1
  55.4 10.0 %all_to_all.31.w_mine = f32[4,32,512]{2,1,0:T(8,128)S(1)} all-to-all(f32[4,32,512]{2,1,0:T(8,128)S(1)} %weight.1), channel_id=1, replica_groups=mesh['yh'=2,'x'=4,'z'=8,'yl'=4,'core'=2] {'yl'}, dimensions={0} | all-to-all | bytes 524288 | tf_op jit(solution)/shard_map/all_to_all | solution.py:250
  65.4 5.7 %collective-permute-start.4 = (f32[4,32,512]{2,1,0:T(8,128)S(1)}, f32[4,32,512]{2,1,0:T(8,128)S(1)}, u32[]{:S(2)}, u32[]{:S(2)}) collective-permute-start(f32[4,32,512]{2,1,0:T(8,128)S(1)} %all_to_all.31.w_mine), channel_id=1, source_target_pairs={{0,1},{1,0},{2,3},{3,2},{4,5},{5,4},{6,7},{7,6},{8,9},{9,8},{10,11... | collective-permute-start | bytes 786440 | tf_op jit(solution)/shard_map/ppermute | solution.py:268
  71.0 1.1 collective-permute-done.4.w_other
  72.2 1.6 %grad.1 = (f32[50,512]{1,0:T(8,128)S(1)}, f32[50,512]{1,0:T(8,128)S(1)}, f32[50,512]{1,0:T(8,128)S(1)}, f32[50,512]{1,0:T(8,128)S(1)}, f32[4,51,256]{2,1,0:T(8,128)S(1)}) custom-call(s32[4]{0:T(128)S(1)} %pad_add_fusion.info, s32[2]{0:T(128)S(1)} %copy-done.7, f32[64,256]{1,0:T(8,128)S(1)} %get-tuple-element.33.q_r, f32[64,256]{1,0:T(8,128)S(1)} %get-tuple-element.34.head_r, ...), custom_call_target="tpu_custom_call" | custom-call | tf_op jit(solution)/shard_map/grad/pallas_call | solution.py:269
  73.8 8.4 %all_to_all.32.gr = f32[4,51,256]{2,1,0:T(8,128)S(1)} all-to-all(f32[4,51,256]{2,1,0:T(8,128)S(1)} %get-tuple-element.40), channel_id=1, replica_groups=mesh['yh'=2,'x'=4,'z'=8,'yl'=4,'core'=2] {'x'}, dimensions={0} | all-to-all | bytes 417792 | tf_op jit(solution)/shard_map/all_to_all | solution.py:250
  82.2 2.1 %place.1 = f32[8,50,128]{2,1,0:T(8,128)} custom-call(s32[4]{0:T(128)S(1)} %pad_add_fusion.info, f32[4,51,256]{2,1,0:T(8,128)S(1)} %all_to_all.32.gr), custom_call_target="tpu_custom_call" | custom-call | tf_op jit(solution)/shard_map/place/pallas_call | solution.py:274
  84.3 3.4 %all-to-all-start.3 = ((f32[8,50,128]{2,1,0:T(8,128)}), f32[8,50,128]{2,1,0:T(8,128)S(1)}, u32[]{:S(2)}, u32[]{:S(2)}) async-start(f32[8,50,128]{2,1,0:T(8,128)} %place.1), calls=%async_computation.3 | async-start | bytes 458752 | tf_op jit(solution)/shard_map/all_to_all | solution.py:250
  87.7 4.5 %collective-permute-start.6 = (f32[50,512]{1,0:T(8,128)S(1)}, f32[50,512]{1,0:T(8,128)S(1)}, u32[]{:S(2)}, u32[]{:S(2)}) collective-permute-start(f32[50,512]{1,0:T(8,128)S(1)} %get-tuple-element.41), channel_id=1, source_target_pairs={{0,56},{8,0},{16,8},{24,16},{32,24},{40,32},{48,40},{56,48},{1,57}... | collective-permute-start | bytes 307208 | tf_op jit(solution)/shard_map/ppermute | solution.py:272
  92.3 4.0 %collective-permute-start.7 = (f32[50,512]{1,0:T(8,128)S(1)}, f32[50,512]{1,0:T(8,128)S(1)}, u32[]{:S(2)}, u32[]{:S(2)}) collective-permute-start(f32[50,512]{1,0:T(8,128)S(1)} %get-tuple-element.42), channel_id=1, source_target_pairs={{0,48},{8,56},{16,0},{24,8},{32,16},{40,24},{48,32},{56,40},{1,49}... | collective-permute-start | bytes 307208 | tf_op jit(solution)/shard_map/ppermute | solution.py:272
  96.2 3.1 %collective-permute-start.8 = (f32[50,512]{1,0:T(8,128)S(1)}, f32[50,512]{1,0:T(8,128)S(1)}, u32[]{:S(2)}, u32[]{:S(2)}) collective-permute-start(f32[50,512]{1,0:T(8,128)S(1)} %get-tuple-element.43), channel_id=1, source_target_pairs={{0,40},{8,48},{16,56},{24,0},{32,8},{40,16},{48,24},{56,32},{1,41}... | collective-permute-start | bytes 307208 | tf_op jit(solution)/shard_map/ppermute | solution.py:272
  99.3 0.0 all-to-all-done.3.parts
  99.3 3.0 %collective-permute-start.5 = (f32[50,128]{1,0:T(8,128)S(1)}, f32[50,128]{1,0:T(8,128)S(1)}, u32[]{:S(2)}, u32[]{:S(2)}) collective-permute-start(f32[50,128]{1,0:T(8,128)S(1)} %fold.1.a), channel_id=1, source_target_pairs={{0,256},{256,0},{1,257},{257,1},{2,258},{258,2},{3,259},{259,3},{4... | collective-permute-start | bytes 76808 | tf_op jit(solution)/shard_map/ppermute | solution.py:276
  102.3 0.0 collective-permute-done.6.got1
  102.3 1.1 collective-permute-done.7.got2
  103.5 4.2 %collective-permute-done.8.got3 = f32[50,512]{1,0:T(8,128)S(1)} collective-permute-done((f32[50,512]{1,0:T(8,128)S(1)}, f32[50,512]{1,0:T(8,128)S(1)}, u32[]{:S(2)}, u32[]{:S(2)}) %collective-permute-start.8) | collective-permute-done | bytes 102432 | tf_op jit(solution)/shard_map/ppermute | solution.py:272
  107.7 0.2 collective-permute-done.5.b
  107.9 1.6 %both.1 = (f32[32,50,128]{2,1,0:T(8,128)}, f32[50,512]{1,0:T(8,128)S(1)}, f32[50,512]{1,0:T(8,128)S(1)}) custom-call(s32[4]{0:T(128)S(1)} %pad_add_fusion.info, f32[50,128]{1,0:T(8,128)S(1)} %fold.1.a, f32[50,128]{1,0:T(8,128)S(1)} %collective-permute-done.5.b, f32[50,512]{1,0:T(8,128)S(1)} %get-tuple-element.45.s0, ...), custom_call_target="tpu_custom_call" | custom-call | tf_op jit(solution)/shard_map/both/pallas_call | solution.py:277
  109.4 8.1 %all-to-all-start.4 = ((f32[32,50,128]{2,1,0:T(8,128)}), f32[32,50,128]{2,1,0:T(8,128)S(1)}, u32[]{:S(2)}, u32[]{:S(2)}) async-start(f32[32,50,128]{2,1,0:T(8,128)} %get-tuple-element.49), calls=%async_computation.4 | async-start | bytes 1835008 | tf_op jit(solution)/shard_map/all_to_all | solution.py:250
  117.5 0.7 collective-permute-start.9
  118.2 0.0 collective-permute-done.9.wrap
  118.2 21.3 %all-to-all-done.4.rel = f32[32,50,128]{2,1,0:T(8,128)S(1)} async-done(((f32[32,50,128]{2,1,0:T(8,128)}), f32[32,50,128]{2,1,0:T(8,128)S(1)}, u32[]{:S(2)}, u32[]{:S(2)}) %all-to-all-start.4) | async-done | bytes 819232 | tf_op jit(solution)/shard_map/all_to_all | solution.py:250
  139.5 0.0 copy-start.1
  139.5 0.0 copy-start.3
  139.5 0.1 square.1
  139.6 0.0 copy-start.6
  139.6 13.7 %all_to_all.33.sq = f32[8,1,4608]{2,1,0:T(1,128)S(1)} all-to-all(f32[8,1,4608]{2,1,0:T(1,128)S(1)} %get-tuple-element.52), channel_id=1, replica_groups=mesh['yh'=2,'x'=4,'z'=8,'yl'=4,'core'=2] {'yl','core'}, dimensions={0} | all-to-all | bytes 294912 | tf_op jit(solution)/shard_map/all_to_all | solution.py:250
  153.3 0.0 copy-start.10
  153.3 0.0 copy-done.1
  153.3 0.0 copy-done.3
  153.3 0.0 copy-done.6
  153.3 0.7 copy-done.10
  154.0 1.1 update.1
  (3 shorter events, 0.1 us)
Async XLA Ops:
  0.6 19.5 %copy-start.4 = (f32[25,512]{1,0:T(8,128)S(1)}, f32[25,512]{1,0:T(8,128)}, u32[]{:S(2)}) copy-start(f32[25,512]{1,0:T(8,128)} %ent_re.3) | copy-start | bytes 153604
  0.6 19.4 %copy-start.5 = (f32[25,512]{1,0:T(8,128)S(1)}, f32[25,512]{1,0:T(8,128)}, u32[]{:S(2)}) copy-start(f32[25,512]{1,0:T(8,128)} %ent_im.3) | copy-start | bytes 153604
  1.6 23.0 %collective-permute-start.2 = (f32[50,512]{1,0:T(8,128)S(1)}, f32[50,512]{1,0:T(8,128)S(1)}, u32[]{:S(2)}, u32[]{:S(2)}) collective-permute-start(f32[50,512]{1,0:T(8,128)S(1)} %pad_maximum_fusion.b0), channel_id=1, source_target_pairs={{0,24},{8,32},{16,40},{24,48},{32,56},{40,64},{48,72},{56,80},{64,... | collective-permute-start | bytes 307208 | tf_op jit(solution)/shard_map/ppermute | solution.py:246
  10.0 25.1 %collective-permute-start.1 = (f32[50,512]{1,0:T(8,128)S(1)}, f32[50,512]{1,0:T(8,128)S(1)}, u32[]{:S(2)}, u32[]{:S(2)}) collective-permute-start(f32[50,512]{1,0:T(8,128)S(1)} %pad_maximum_fusion.b0), channel_id=1, source_target_pairs={{0,16},{8,24},{16,32},{24,40},{32,48},{40,56},{48,64},{56,72},{64,... | collective-permute-start | bytes 307208 | tf_op jit(solution)/shard_map/ppermute | solution.py:246
  16.2 19.8 %collective-permute-start = (f32[50,512]{1,0:T(8,128)S(1)}, f32[50,512]{1,0:T(8,128)S(1)}, u32[]{:S(2)}, u32[]{:S(2)}) collective-permute-start(f32[50,512]{1,0:T(8,128)S(1)} %pad_maximum_fusion.b0), channel_id=1, source_target_pairs={{0,8},{8,16},{16,24},{24,32},{32,40},{40,48},{48,56},{56,64},{64,7... | collective-permute-start | bytes 307208 | tf_op jit(solution)/shard_map/ppermute | solution.py:246
  19.3 0.7 copy-start.12
  20.0 0.7 copy-start.11
  20.0 0.7 copy-start.8
  20.0 0.7 copy-start.9
  20.7 1.0 copy-start
  21.7 1.0 copy-start.2
  24.3 11.6 %copy-start.7 = (s32[2]{0:T(128)S(1)}, s32[2]{0:T(128)}, u32[]{:S(2)}) copy-start(s32[2]{0:T(128)} %bucket.5) | copy-start | bytes 28
  37.1 4.3 %collective-permute-start.3 = (f32[4,32,512]{2,1,0:T(8,128)S(1)}, f32[4,32,512]{2,1,0:T(8,128)S(1)}, u32[]{:S(2)}, u32[]{:S(2)}) collective-permute-start(f32[4,32,512]{2,1,0:T(8,128)S(1)} %get-tuple-element.37), channel_id=1, source_target_pairs={{0,1},{1,0},{2,3},{3,2},{4,5},{5,4},{6,7},{7,6},{8,9},{9,8},{10,11... | collective-permute-start | bytes 786440 | tf_op jit(solution)/shard_map/ppermute | solution.py:264
  65.4 6.8 %collective-permute-start.4 = (f32[4,32,512]{2,1,0:T(8,128)S(1)}, f32[4,32,512]{2,1,0:T(8,128)S(1)}, u32[]{:S(2)}, u32[]{:S(2)}) collective-permute-start(f32[4,32,512]{2,1,0:T(8,128)S(1)} %all_to_all.31.w_mine), channel_id=1, source_target_pairs={{0,1},{1,0},{2,3},{3,2},{4,5},{5,4},{6,7},{7,6},{8,9},{9,8},{10,11... | collective-permute-start | bytes 786440 | tf_op jit(solution)/shard_map/ppermute | solution.py:268
  84.3 15.0 %all-to-all-start.3 = ((f32[8,50,128]{2,1,0:T(8,128)}), f32[8,50,128]{2,1,0:T(8,128)S(1)}, u32[]{:S(2)}, u32[]{:S(2)}) async-start(f32[8,50,128]{2,1,0:T(8,128)} %place.1), calls=%async_computation.3 | async-start | bytes 458752 | tf_op jit(solution)/shard_map/all_to_all | solution.py:250
  87.7 14.6 %collective-permute-start.6 = (f32[50,512]{1,0:T(8,128)S(1)}, f32[50,512]{1,0:T(8,128)S(1)}, u32[]{:S(2)}, u32[]{:S(2)}) collective-permute-start(f32[50,512]{1,0:T(8,128)S(1)} %get-tuple-element.41), channel_id=1, source_target_pairs={{0,56},{8,0},{16,8},{24,16},{32,24},{40,32},{48,40},{56,48},{1,57}... | collective-permute-start | bytes 307208 | tf_op jit(solution)/shard_map/ppermute | solution.py:272
  92.3 11.2 %collective-permute-start.7 = (f32[50,512]{1,0:T(8,128)S(1)}, f32[50,512]{1,0:T(8,128)S(1)}, u32[]{:S(2)}, u32[]{:S(2)}) collective-permute-start(f32[50,512]{1,0:T(8,128)S(1)} %get-tuple-element.42), channel_id=1, source_target_pairs={{0,48},{8,56},{16,0},{24,8},{32,16},{40,24},{48,32},{56,40},{1,49}... | collective-permute-start | bytes 307208 | tf_op jit(solution)/shard_map/ppermute | solution.py:272
  96.2 11.5 %collective-permute-start.8 = (f32[50,512]{1,0:T(8,128)S(1)}, f32[50,512]{1,0:T(8,128)S(1)}, u32[]{:S(2)}, u32[]{:S(2)}) collective-permute-start(f32[50,512]{1,0:T(8,128)S(1)} %get-tuple-element.43), channel_id=1, source_target_pairs={{0,40},{8,48},{16,56},{24,0},{32,8},{40,16},{48,24},{56,32},{1,41}... | collective-permute-start | bytes 307208 | tf_op jit(solution)/shard_map/ppermute | solution.py:272
  99.3 8.5 %collective-permute-start.5 = (f32[50,128]{1,0:T(8,128)S(1)}, f32[50,128]{1,0:T(8,128)S(1)}, u32[]{:S(2)}, u32[]{:S(2)}) collective-permute-start(f32[50,128]{1,0:T(8,128)S(1)} %fold.1.a), channel_id=1, source_target_pairs={{0,256},{256,0},{1,257},{257,1},{2,258},{258,2},{3,259},{259,3},{4... | collective-permute-start | bytes 76808 | tf_op jit(solution)/shard_map/ppermute | solution.py:276
  109.4 30.0 %all-to-all-start.4 = ((f32[32,50,128]{2,1,0:T(8,128)}), f32[32,50,128]{2,1,0:T(8,128)S(1)}, u32[]{:S(2)}, u32[]{:S(2)}) async-start(f32[32,50,128]{2,1,0:T(8,128)} %get-tuple-element.49), calls=%async_computation.4 | async-start | bytes 1835008 | tf_op jit(solution)/shard_map/all_to_all | solution.py:250
  117.5 0.7 collective-permute-start.9
  139.5 13.8 %copy-start.1 = (f32[25,4096]{1,0:T(8,128)S(1)}, f32[25,4096]{1,0:T(8,128)}, u32[]{:S(2)}) copy-start(f32[25,4096]{1,0:T(8,128)} %rel_re.3) | copy-start | bytes 1228804
  139.5 13.8 %copy-start.3 = (f32[25,4096]{1,0:T(8,128)S(1)}, f32[25,4096]{1,0:T(8,128)}, u32[]{:S(2)}) copy-start(f32[25,4096]{1,0:T(8,128)} %rel_im.3) | copy-start | bytes 1228804
  139.6 13.7 %copy-start.6 = (f32[4096]{0:T(1024)S(1)}, f32[4096]{0:T(1024)}, u32[]{:S(2)}) copy-start(f32[4096]{0:T(1024)} %param.16) | copy-start | bytes 49156
  153.3 0.7 copy-start.10

commit v8 on v7

--- a/solution.py
+++ b/solution.py
@@ -142,7 +142,7 @@
         w_o[i] = w
 
 
-def grad_kernel(info, bucket, q_r, head_r, relc_r, w_mine, w_other, b0, b1, b2, b3, lhs, rel_ids, s0_o, s1_o, s2_o, s3_o, gr_o):
+def grad_kernel(info, bucket, q_r, head_r, relc_r, w_mine, w_other, b0, b1, b2, b3, lhs, rel_ids, s0_o, s1_o, s23_o, gr_o):
     core = info[0]
     mine = w_mine[...].reshape(CH, ROWS)
     other = w_other[...].reshape(CH, ROWS)
@@ -170,9 +170,9 @@
         gr_o[i, 0:W, :] = gr_re
         gr_o[i, W : 2 * W, :] = gr_im
         gr_o[i, 2 * W : 2 * W + 1, :] = ids
-    for ref, slot in zip((s0_o, s1_o, s2_o, s3_o), slots):
-        ref[0:W, :] = slot[:W]
-        ref[W : 2 * W, :] = slot[32 : 32 + W]
+    for ref, at, slot in ((s0_o, 0, 0), (s1_o, 0, 1), (s23_o, 0, 3), (s23_o, 2 * W, 2)):
+        ref[at : at + W, :] = slots[slot][:W]
+        ref[at + W : at + 2 * W, :] = slots[slot][32 : 32 + W]
 
 
 def place_kernel(info, gr, out):
@@ -196,18 +196,29 @@
     out[...] = tot
 
 
-def both_kernel(info, a, b, s0, got1, got2, got3, out, ring_o, wrap_o):
+def carry_kernel(info, s1, got23, out):
+    z = info[3]
+    own = s1[...]
+    far = got23[0 : 2 * W, :]
+    wraps = (z >= 6) | (z == 0)
+    out[0 : 2 * W, :] = jnp.where(z == 0, 0.0, own) + jnp.where(wraps, 0.0, far)
+    out[2 * W : 4 * W, :] = jnp.where(z == 0, own, 0.0) + jnp.where(wraps, far, 0.0)
+
+
+def both_kernel(info, a, b, s0, got1, got23, out, ring_o, wrap_o):
     tot = a[...] + b[...]
-    for i in range(32):
+    for i in range(8):
         out[i] = tot
-    z = info[3]
-    ring = s0[...]
-    wrap = jnp.zeros_like(ring)
-    for s, got in ((1, got1), (2, got2), (3, got3)):
-        ring = ring + jnp.where(z + s < 8, got[...], 0.0)
-        wrap = wrap + jnp.where(z + s < 8, 0.0, got[...])
-    ring_o[...] = ring
-    wrap_o[...] = wrap
+    wraps = info[3] >= 6
+    second = got23[2 * W : 4 * W, :]
+    ring_o[...] = s0[...] + (got1[0 : 2 * W, :] + jnp.where(wraps, 0.0, second))
+    wrap_o[...] = got1[2 * W : 4 * W, :] + jnp.where(wraps, second, 0.0)
+
+
+def copies_kernel(a, out):
+    for x in range(4):
+        for z in range(8):
+            out[x, 2 * W * z : 2 * W * z + 2 * W, :] = a[z]
 
 
 def square_kernel(rel, ring, wrap, ent_o, sq_o):
@@ -217,7 +228,7 @@
     for i in range(8):
         sq_o[i, :, 0:ROWS] = es
     for t in range(32):
-        tot = rel[t]
+        tot = rel[t // 8, 2 * W * (t % 8) : 2 * W * (t % 8) + 2 * W, :]
         rs = jnp.sum(tot * tot, 0, keepdims=True)
         for i in range(8):
             sq_o[i, :, ROWS + 128 * t : ROWS + 128 * t + 128] = rs
@@ -237,7 +248,7 @@
     scale = LEARN_RATE / jnp.sqrt(acc)
     for t in range(32):
         at = slice(128 * t, 128 * t + 128)
-        tot = rel[t]
+        tot = rel[t // 8, 2 * W * (t % 8) : 2 * W * (t % 8) + 2 * W, :]
         rre_o[:, at] = rel_re[:, at] - scale[:, at] * tot[:W]
         rim_o[:, at] = rel_im[:, at] - scale[:, at] * tot[W:]
 
@@ -266,17 +277,21 @@
     w = call(weight_kernel, "weight", quarter, [SM, SM] + [VM] * 3)(info, bucket_step, s, m, hit)
     w_mine = exchange(w, "yl")
     w_other = lax.ppermute(w_mine, "core", SWAP)
-    s0, s1, s2, s3, gr = call(
-        grad_kernel, "grad", [block, block, block, block, (4, 2 * W + 1, 256)], [SM, SM] + [VM] * 11,
+    s0, s1, s23, gr = call(
+        grad_kernel, "grad", [block, block, (4 * W, ROWS), (4, 2 * W + 1, 256)], [SM, SM] + [VM] * 11,
     )(info, bucket_step, q, head, relc, w_mine, w_other, own, b1, b2, b3, lhs_rows, rel_ids)
-    got = [lax.ppermute(v, "z", [(i, (i - d) % 8) for i in range(8)]) for d, v in ((1, s1), (2, s2), (3, s3))]
+    got23 = lax.ppermute(s23, "z", [(i, (i - 2) % 8) for i in range(8)])
     gr = exchange(gr, "x")
     pieces = call(place_kernel, "place", (8, 2 * W, 128), [SM, VM])(info, gr)
+    pieces, got23 = lax.optimization_barrier((pieces, got23))
+    carry = call(carry_kernel, "carry", (4 * W, ROWS), [SM] + [VM] * 2)(info, s1, got23)
+    got1 = lax.ppermute(carry, "z", [(i, (i - 1) % 8) for i in range(8)])
     half = call(fold_kernel, "fold", (2 * W, 128), [VM])(exchange(pieces, "z"))
-    twin, got = lax.optimization_barrier((lax.ppermute(half, "yh", SWAP), got))
-    rel, ring, wrap = call(both_kernel, "both", [(32, 2 * W, 128), block, block], [SM] + [VM] * 6)(info, half, twin, s0, *got)
+    twin, got1 = lax.optimization_barrier((lax.ppermute(half, "yh", SWAP), got1))
+    rel, ring, wrap = call(both_kernel, "both", [(8, 2 * W, 128), block, block], [SM] + [VM] * 5)(info, half, twin, s0, got1, got23)
     wrap = lax.ppermute(wrap, DOM, [(i, (i - 8) % 64) for i in range(64) if i % 8 >= 5])
-    rel = exchange(rel, ("x", "z"))
+    rel, wrap = lax.optimization_barrier((exchange(rel, "z"), wrap))
+    rel = exchange(call(copies_kernel, "copies", (4, 16 * W, 128), [VM])(rel), "x")
     ent, sq = call(square_kernel, "square", [block, (8, 1, ROWS + REL)], [VM] * 3)(rel, ring, wrap)
     sq = exchange(sq, DIM)
     new_re, new_im, new_acc, new_rel_re, new_rel_im, new_rel_acc = call(

time: 156 us -> 151 us (0.968)
  blocking collectives: 45.3 us -> 57.2 us
  starting transfers between devices: 53.1 us -> 42.7 us
  waiting for transfers between devices: 40.7 us -> 33.9 us
    all_to_all x4 -> x5, blocking collectives: 45.3 us -> 57.2 us  [exchange(): return lax.all_to_all(pieces, axes, 0, 0)]
    all_to_all x2, waiting for transfers between devices: 21.3 us -> 12.4 us  [exchange(): return lax.all_to_all(pieces, axes, 0, 0)]
    ppermute x4 -> x3, starting transfers between devices: 14.5 us -> 8.73 us  [the longest x1 4.52 us: per_device(): got1 = lax.ppermute(carry, 'z', [(i, (i - 1) % 8) for i in range(8)])]
    all_to_all x2, starting transfers between devices: 11.5 us -> 6.81 us  [exchange(): return lax.all_to_all(pieces, axes, 0, 0)]
    ppermute x4 -> x3, waiting for transfers between devices: 5.53 us -> 7.55 us  [the longest x1 6.21 us: per_device(): lax.ppermute(half, 'yh', SWAP)]
    pallas_call x2 -> x4, Pallas kernels: 3.16 us -> 3.51 us  [the longest x1 1.61 us: per_device(): call(grad_kernel, 'grad', [block, block, (4 * W, ROWS), (4, 2 * W + 1, 25...]
  transfers between devices with their start and end apart: 12 -> 11, of which waited for: 9 -> 9; matrix products, arithmetic and copies ran while one was open for 0% -> 0% of each run, Pallas kernels for 1% -> 3%
where the time goes in v8:
time: 151 us; the launch traced here: 150 us
  blocking collectives  57.2 us (38%)
  starting transfers between devices  42.7 us (28%)
  waiting for transfers between devices  33.9 us (22%)
  Pallas kernels  10.3 us (7%)
  local copies, waits for them, and re-layouts  4.08 us (3%)
    all_to_all x5, blocking collectives, exchange(): return lax.all_to_all(pieces, axes, 0, 0)  57.2 us
    ppermute x3, starting transfers between devices, shift(): lax.ppermute(block, DOM, [(i, (i + distance) % 64) for i in range(64)])  17.7 us
    all_to_all x2, waiting for transfers between devices, exchange(): return lax.all_to_all(pieces, axes, 0, 0)  12.4 us
    ppermute x3, waiting for transfers between devices, shift(): lax.ppermute(block, DOM, [(i, (i + distance) % 64) for i in range(64)])  11.6 us
    all_to_all x2, starting transfers between devices, exchange(): return lax.all_to_all(pieces, axes, 0, 0)  6.81 us
    ppermute x1, waiting for transfers between devices, per_device(): lax.ppermute(half, 'yh', SWAP)  6.21 us
    ppermute x1, starting transfers between devices, per_device(): w_other = lax.ppermute(w_mine, 'core', SWAP)  5.66 us
    ppermute x1, starting transfers between devices, per_device(): got1 = lax.ppermute(carry, 'z', [(i, (i - 1) % 8) for i in range(8)])  4.52 us
  transfers between devices with their start and end apart: 11, of which 9 were waited for; matrix products, arithmetic and copies ran while one was open for 0% of the time, Pallas kernels for 3%

profile of v8, /device:TPU:1, one launch (start us, length us, event | category | flops | bytes accessed | tf_op | source)
XLA Modules:
  0.0 150.1 jit_solution(12259951785294906005)
XLA Ops:
  0.6 0.0 copy-start.4
  0.6 0.0 copy-start.5
  0.7 0.9 pad_maximum_fusion.b0
  1.6 8.4 %collective-permute-start.2 = (f32[50,512]{1,0:T(8,128)S(1)}, f32[50,512]{1,0:T(8,128)S(1)}, u32[]{:S(2)}, u32[]{:S(2)}) collective-permute-start(f32[50,512]{1,0:T(8,128)S(1)} %pad_maximum_fusion.b0), channel_id=1, source_target_pairs={{0,24},{8,32},{16,40},{24,48},{32,56},{40,64},{48,72},{56,80},{64,... | collective-permute-start | bytes 307208 | tf_op jit(solution)/shard_map/ppermute | solution.py:257
  10.0 6.1 %collective-permute-start.1 = (f32[50,512]{1,0:T(8,128)S(1)}, f32[50,512]{1,0:T(8,128)S(1)}, u32[]{:S(2)}, u32[]{:S(2)}) collective-permute-start(f32[50,512]{1,0:T(8,128)S(1)} %pad_maximum_fusion.b0), channel_id=1, source_target_pairs={{0,16},{8,24},{16,32},{24,40},{32,48},{40,56},{48,64},{56,72},{64,... | collective-permute-start | bytes 307208 | tf_op jit(solution)/shard_map/ppermute | solution.py:257
  16.2 3.1 %collective-permute-start = (f32[50,512]{1,0:T(8,128)S(1)}, f32[50,512]{1,0:T(8,128)S(1)}, u32[]{:S(2)}, u32[]{:S(2)}) collective-permute-start(f32[50,512]{1,0:T(8,128)S(1)} %pad_maximum_fusion.b0), channel_id=1, source_target_pairs={{0,8},{8,16},{16,24},{24,32},{32,40},{40,48},{48,56},{56,64},{64,7... | collective-permute-start | bytes 307208 | tf_op jit(solution)/shard_map/ppermute | solution.py:257
  19.3 0.0 copy-start.12
  19.3 0.7 copy-done.12
  20.0 0.0 copy-start.11
  20.0 0.0 copy-start.8
  20.0 0.0 copy-start.9
  20.0 0.1 pad_add_fusion.info
  20.1 0.0 copy-done.4
  20.1 0.0 copy-done.5
  20.1 0.6 copy-done.11
  20.7 0.0 copy-done.8
  20.7 0.0 copy-done.9
  20.7 0.0 copy-start
  20.7 1.0 copy-done
  21.7 0.0 copy-start.2
  21.7 1.0 copy-done.2
  22.8 1.5 %query.1 = (f32[64,256]{1,0:T(8,128)S(1)}, f32[64,256]{1,0:T(8,128)S(1)}, f32[64,256]{1,0:T(8,128)S(1)}, f32[8,512]{1,0:T(8,128)S(1)}, f32[128,512]{1,0:T(8,128)S(1)}) custom-call(s32[4]{0:T(128)S(1)} %pad_add_fusion.info, f32[25,512]{1,0:T(8,128)S(1)} %copy-done.4, f32[25,512]{1,0:T(8,128)S(1)} %copy-done.5, f32[25,4096]{1,0:T(8,128)S(1)} %copy-done, ...), custom_call_target="tpu_custom_call" | custom-call | tf_op jit(solution)/shard_map/query/pallas_call | solution.py:269
  24.3 0.0 copy-start.7
  24.3 0.3 collective-permute-done.2.b3
  24.6 10.5 %collective-permute-done.1.b2 = f32[50,512]{1,0:T(8,128)S(1)} collective-permute-done((f32[50,512]{1,0:T(8,128)S(1)}, f32[50,512]{1,0:T(8,128)S(1)}, u32[]{:S(2)}, u32[]{:S(2)}) %collective-permute-start.1) | collective-permute-done | bytes 102432 | tf_op jit(solution)/shard_map/ppermute | solution.py:257
  35.1 0.8 collective-permute-done.b1
  35.9 0.0 copy-done.7
  36.0 1.2 score.1
  37.1 3.1 %collective-permute-start.3 = (f32[4,32,512]{2,1,0:T(8,128)S(1)}, f32[4,32,512]{2,1,0:T(8,128)S(1)}, u32[]{:S(2)}, u32[]{:S(2)}) collective-permute-start(f32[4,32,512]{2,1,0:T(8,128)S(1)} %get-tuple-element.38), channel_id=1, source_target_pairs={{0,1},{1,0},{2,3},{3,2},{4,5},{5,4},{6,7},{7,6},{8,9},{9,8},{10,11... | collective-permute-start | bytes 786440 | tf_op jit(solution)/shard_map/ppermute | solution.py:275
  40.3 1.1 collective-permute-done.3.b
  41.4 13.2 %all_to_all.35.parts = f32[4,32,512]{2,1,0:T(8,128)S(1)} all-to-all(f32[4,32,512]{2,1,0:T(8,128)S(1)} %add.9), channel_id=1, replica_groups=mesh['yh'=2,'x'=4,'z'=8,'yl'=4,'core'=2] {'yl'}, dimensions={0} | all-to-all | bytes 524288 | tf_op jit(solution)/shard_map/all_to_all | solution.py:261
  54.6 0.8 weight.1
  55.4 10.0 %all_to_all.36.w_mine = f32[4,32,512]{2,1,0:T(8,128)S(1)} all-to-all(f32[4,32,512]{2,1,0:T(8,128)S(1)} %weight.1), channel_id=1, replica_groups=mesh['yh'=2,'x'=4,'z'=8,'yl'=4,'core'=2] {'yl'}, dimensions={0} | all-to-all | bytes 524288 | tf_op jit(solution)/shard_map/all_to_all | solution.py:261
  65.4 5.7 %collective-permute-start.4 = (f32[4,32,512]{2,1,0:T(8,128)S(1)}, f32[4,32,512]{2,1,0:T(8,128)S(1)}, u32[]{:S(2)}, u32[]{:S(2)}) collective-permute-start(f32[4,32,512]{2,1,0:T(8,128)S(1)} %all_to_all.36.w_mine), channel_id=1, source_target_pairs={{0,1},{1,0},{2,3},{3,2},{4,5},{5,4},{6,7},{7,6},{8,9},{9,8},{10,11... | collective-permute-start | bytes 786440 | tf_op jit(solution)/shard_map/ppermute | solution.py:279
  71.0 1.1 collective-permute-done.4.w_other
  72.2 1.6 %grad.1 = (f32[50,512]{1,0:T(8,128)S(1)}, f32[50,512]{1,0:T(8,128)S(1)}, f32[100,512]{1,0:T(8,128)S(1)}, f32[4,51,256]{2,1,0:T(8,128)S(1)}) custom-call(s32[4]{0:T(128)S(1)} %pad_add_fusion.info, s32[2]{0:T(128)S(1)} %copy-done.7, f32[64,256]{1,0:T(8,128)S(1)} %get-tuple-element.34.q_r, f32[64,256]{1,0:T(8,128)S(1)} %get-tuple-element.35.head_r, ...), custom_call_target="tpu_custom_call" | custom-call | tf_op jit(solution)/shard_map/grad/pallas_call | solution.py:280
  73.8 1.9 %collective-permute-start.5 = (f32[100,512]{1,0:T(8,128)S(1)}, f32[100,512]{1,0:T(8,128)S(1)}, u32[]{:S(2)}, u32[]{:S(2)}) collective-permute-start(f32[100,512]{1,0:T(8,128)S(1)} %get-tuple-element.42), channel_id=1, source_target_pairs={{0,48},{8,56},{16,0},{24,8},{32,16},{40,24},{48,32},{56,40},{1,49}... | collective-permute-start | bytes 614408 | tf_op jit(solution)/shard_map/ppermute | solution.py:283
  75.7 8.4 %all_to_all.37.gr = f32[4,51,256]{2,1,0:T(8,128)S(1)} all-to-all(f32[4,51,256]{2,1,0:T(8,128)S(1)} %get-tuple-element.41), channel_id=1, replica_groups=mesh['yh'=2,'x'=4,'z'=8,'yl'=4,'core'=2] {'x'}, dimensions={0} | all-to-all | bytes 417792 | tf_op jit(solution)/shard_map/all_to_all | solution.py:261
  84.2 2.1 %place.1 = f32[8,50,128]{2,1,0:T(8,128)} custom-call(s32[4]{0:T(128)S(1)} %pad_add_fusion.info, f32[4,51,256]{2,1,0:T(8,128)S(1)} %all_to_all.37.gr), custom_call_target="tpu_custom_call" | custom-call | tf_op jit(solution)/shard_map/place/pallas_call | solution.py:285
  86.3 1.3 collective-permute-done.5.got23
  87.6 3.4 %all-to-all-start.3 = ((f32[8,50,128]{2,1,0:T(8,128)}), f32[8,50,128]{2,1,0:T(8,128)S(1)}, u32[]{:S(2)}, u32[]{:S(2)}) async-start(f32[8,50,128]{2,1,0:T(8,128)} %place.1), calls=%async_computation.3 | async-start | bytes 458752 | tf_op jit(solution)/shard_map/all_to_all | solution.py:261
  91.0 0.6 carry.1
  91.6 4.5 %collective-permute-start.7 = (f32[100,512]{1,0:T(8,128)S(1)}, f32[100,512]{1,0:T(8,128)S(1)}, u32[]{:S(2)}, u32[]{:S(2)}) collective-permute-start(f32[100,512]{1,0:T(8,128)S(1)} %carry.1), channel_id=1, source_target_pairs={{0,56},{8,0},{16,8},{24,16},{32,24},{40,32},{48,40},{56,48},{1,57}... | collective-permute-start | bytes 614408 | tf_op jit(solution)/shard_map/ppermute | solution.py:288
  96.1 4.2 %all-to-all-done.3.parts = f32[8,50,128]{2,1,0:T(8,128)S(1)} async-done(((f32[8,50,128]{2,1,0:T(8,128)}), f32[8,50,128]{2,1,0:T(8,128)S(1)}, u32[]{:S(2)}, u32[]{:S(2)}) %all-to-all-start.3) | async-done | bytes 204832 | tf_op jit(solution)/shard_map/all_to_all | solution.py:261
  100.4 2.3 %collective-permute-start.6 = (f32[50,128]{1,0:T(8,128)S(1)}, f32[50,128]{1,0:T(8,128)S(1)}, u32[]{:S(2)}, u32[]{:S(2)}) collective-permute-start(f32[50,128]{1,0:T(8,128)S(1)} %fold.1.a), channel_id=1, source_target_pairs={{0,256},{256,0},{1,257},{257,1},{2,258},{258,2},{3,259},{259,3},{4... | collective-permute-start | bytes 76808 | tf_op jit(solution)/shard_map/ppermute | solution.py:290
  102.7 0.0 collective-permute-done.7.got1
  102.7 6.2 %collective-permute-done.6.b = f32[50,128]{1,0:T(8,128)S(1)} collective-permute-done((f32[50,128]{1,0:T(8,128)S(1)}, f32[50,128]{1,0:T(8,128)S(1)}, u32[]{:S(2)}, u32[]{:S(2)}) %collective-permute-start.6) | collective-permute-done | bytes 25632 | tf_op jit(solution)/shard_map/ppermute | solution.py:290
  108.9 1.3 both.1
  110.1 3.4 %all-to-all-start.4 = ((f32[8,50,128]{2,1,0:T(8,128)}), f32[8,50,128]{2,1,0:T(8,128)S(1)}, u32[]{:S(2)}, u32[]{:S(2)}) async-start(f32[8,50,128]{2,1,0:T(8,128)} %get-tuple-element.49), calls=%async_computation.4 | async-start | bytes 458752 | tf_op jit(solution)/shard_map/all_to_all | solution.py:261
  113.6 0.7 collective-permute-start.8
  114.2 0.0 collective-permute-done.8.wrap
  114.2 8.2 %all-to-all-done.4.a = f32[8,50,128]{2,1,0:T(8,128)S(1)} async-done(((f32[8,50,128]{2,1,0:T(8,128)}), f32[8,50,128]{2,1,0:T(8,128)S(1)}, u32[]{:S(2)}, u32[]{:S(2)}) %all-to-all-start.4) | async-done | bytes 204832 | tf_op jit(solution)/shard_map/all_to_all | solution.py:261
  122.5 0.1 copies.1
  122.5 10.9 %all_to_all.38.rel = f32[4,400,128]{2,1,0:T(8,128)S(1)} all-to-all(f32[4,400,128]{2,1,0:T(8,128)S(1)} %copies.1), channel_id=1, replica_groups=mesh['yh'=2,'x'=4,'z'=8,'yl'=4,'core'=2] {'x'}, dimensions={0} | all-to-all | bytes 1638400 | tf_op jit(solution)/shard_map/all_to_all | solution.py:261
  133.4 0.0 copy-start.1
  133.4 0.0 copy-start.3
  133.4 0.1 square.1
  133.5 0.0 copy-start.6
  133.6 14.7 %all_to_all.39.sq = f32[8,1,4608]{2,1,0:T(1,128)S(1)} all-to-all(f32[8,1,4608]{2,1,0:T(1,128)S(1)} %get-tuple-element.54), channel_id=1, replica_groups=mesh['yh'=2,'x'=4,'z'=8,'yl'=4,'core'=2] {'yl','core'}, dimensions={0} | all-to-all | bytes 294912 | tf_op jit(solution)/shard_map/all_to_all | solution.py:261
  148.2 0.0 copy-done.1
  148.2 0.0 copy-done.3
  148.3 0.0 copy-done.6
  148.3 0.7 copy-done.10
  148.9 1.1 update.1
  (4 shorter events, 0.1 us)
Async XLA Ops:
  0.6 19.5 %copy-start.4 = (f32[25,512]{1,0:T(8,128)S(1)}, f32[25,512]{1,0:T(8,128)}, u32[]{:S(2)}) copy-start(f32[25,512]{1,0:T(8,128)} %ent_re.3) | copy-start | bytes 153604
  0.6 19.4 %copy-start.5 = (f32[25,512]{1,0:T(8,128)S(1)}, f32[25,512]{1,0:T(8,128)}, u32[]{:S(2)}) copy-start(f32[25,512]{1,0:T(8,128)} %ent_im.3) | copy-start | bytes 153604
  1.6 23.0 %collective-permute-start.2 = (f32[50,512]{1,0:T(8,128)S(1)}, f32[50,512]{1,0:T(8,128)S(1)}, u32[]{:S(2)}, u32[]{:S(2)}) collective-permute-start(f32[50,512]{1,0:T(8,128)S(1)} %pad_maximum_fusion.b0), channel_id=1, source_target_pairs={{0,24},{8,32},{16,40},{24,48},{32,56},{40,64},{48,72},{56,80},{64,... | collective-permute-start | bytes 307208 | tf_op jit(solution)/shard_map/ppermute | solution.py:257
  10.0 25.1 %collective-permute-start.1 = (f32[50,512]{1,0:T(8,128)S(1)}, f32[50,512]{1,0:T(8,128)S(1)}, u32[]{:S(2)}, u32[]{:S(2)}) collective-permute-start(f32[50,512]{1,0:T(8,128)S(1)} %pad_maximum_fusion.b0), channel_id=1, source_target_pairs={{0,16},{8,24},{16,32},{24,40},{32,48},{40,56},{48,64},{56,72},{64,... | collective-permute-start | bytes 307208 | tf_op jit(solution)/shard_map/ppermute | solution.py:257
  16.2 19.8 %collective-permute-start = (f32[50,512]{1,0:T(8,128)S(1)}, f32[50,512]{1,0:T(8,128)S(1)}, u32[]{:S(2)}, u32[]{:S(2)}) collective-permute-start(f32[50,512]{1,0:T(8,128)S(1)} %pad_maximum_fusion.b0), channel_id=1, source_target_pairs={{0,8},{8,16},{16,24},{24,32},{32,40},{40,48},{48,56},{56,64},{64,7... | collective-permute-start | bytes 307208 | tf_op jit(solution)/shard_map/ppermute | solution.py:257
  19.3 0.7 copy-start.12
  20.0 0.7 copy-start.11
  20.0 0.7 copy-start.8
  20.0 0.7 copy-start.9
  20.7 1.0 copy-start
  21.7 1.0 copy-start.2
  24.3 11.6 %copy-start.7 = (s32[2]{0:T(128)S(1)}, s32[2]{0:T(128)}, u32[]{:S(2)}) copy-start(s32[2]{0:T(128)} %bucket.5) | copy-start | bytes 28
  37.1 4.3 %collective-permute-start.3 = (f32[4,32,512]{2,1,0:T(8,128)S(1)}, f32[4,32,512]{2,1,0:T(8,128)S(1)}, u32[]{:S(2)}, u32[]{:S(2)}) collective-permute-start(f32[4,32,512]{2,1,0:T(8,128)S(1)} %get-tuple-element.38), channel_id=1, source_target_pairs={{0,1},{1,0},{2,3},{3,2},{4,5},{5,4},{6,7},{7,6},{8,9},{9,8},{10,11... | collective-permute-start | bytes 786440 | tf_op jit(solution)/shard_map/ppermute | solution.py:275
  65.4 6.8 %collective-permute-start.4 = (f32[4,32,512]{2,1,0:T(8,128)S(1)}, f32[4,32,512]{2,1,0:T(8,128)S(1)}, u32[]{:S(2)}, u32[]{:S(2)}) collective-permute-start(f32[4,32,512]{2,1,0:T(8,128)S(1)} %all_to_all.36.w_mine), channel_id=1, source_target_pairs={{0,1},{1,0},{2,3},{3,2},{4,5},{5,4},{6,7},{7,6},{8,9},{9,8},{10,11... | collective-permute-start | bytes 786440 | tf_op jit(solution)/shard_map/ppermute | solution.py:279
  73.8 13.8 %collective-permute-start.5 = (f32[100,512]{1,0:T(8,128)S(1)}, f32[100,512]{1,0:T(8,128)S(1)}, u32[]{:S(2)}, u32[]{:S(2)}) collective-permute-start(f32[100,512]{1,0:T(8,128)S(1)} %get-tuple-element.42), channel_id=1, source_target_pairs={{0,48},{8,56},{16,0},{24,8},{32,16},{40,24},{48,32},{56,40},{1,49}... | collective-permute-start | bytes 614408 | tf_op jit(solution)/shard_map/ppermute | solution.py:283
  87.6 12.8 %all-to-all-start.3 = ((f32[8,50,128]{2,1,0:T(8,128)}), f32[8,50,128]{2,1,0:T(8,128)S(1)}, u32[]{:S(2)}, u32[]{:S(2)}) async-start(f32[8,50,128]{2,1,0:T(8,128)} %place.1), calls=%async_computation.3 | async-start | bytes 458752 | tf_op jit(solution)/shard_map/all_to_all | solution.py:261
  91.6 11.1 %collective-permute-start.7 = (f32[100,512]{1,0:T(8,128)S(1)}, f32[100,512]{1,0:T(8,128)S(1)}, u32[]{:S(2)}, u32[]{:S(2)}) collective-permute-start(f32[100,512]{1,0:T(8,128)S(1)} %carry.1), channel_id=1, source_target_pairs={{0,56},{8,0},{16,8},{24,16},{32,24},{40,32},{48,40},{56,48},{1,57}... | collective-permute-start | bytes 614408 | tf_op jit(solution)/shard_map/ppermute | solution.py:288
  100.4 8.5 %collective-permute-start.6 = (f32[50,128]{1,0:T(8,128)S(1)}, f32[50,128]{1,0:T(8,128)S(1)}, u32[]{:S(2)}, u32[]{:S(2)}) collective-permute-start(f32[50,128]{1,0:T(8,128)S(1)} %fold.1.a), channel_id=1, source_target_pairs={{0,256},{256,0},{1,257},{257,1},{2,258},{258,2},{3,259},{259,3},{4... | collective-permute-start | bytes 76808 | tf_op jit(solution)/shard_map/ppermute | solution.py:290
  110.1 12.3 %all-to-all-start.4 = ((f32[8,50,128]{2,1,0:T(8,128)}), f32[8,50,128]{2,1,0:T(8,128)S(1)}, u32[]{:S(2)}, u32[]{:S(2)}) async-start(f32[8,50,128]{2,1,0:T(8,128)} %get-tuple-element.49), calls=%async_computation.4 | async-start | bytes 458752 | tf_op jit(solution)/shard_map/all_to_all | solution.py:261
  113.6 0.7 collective-permute-start.8
  133.4 14.8 %copy-start.1 = (f32[25,4096]{1,0:T(8,128)S(1)}, f32[25,4096]{1,0:T(8,128)}, u32[]{:S(2)}) copy-start(f32[25,4096]{1,0:T(8,128)} %rel_re.3) | copy-start | bytes 1228804
  133.4 14.8 %copy-start.3 = (f32[25,4096]{1,0:T(8,128)S(1)}, f32[25,4096]{1,0:T(8,128)}, u32[]{:S(2)}) copy-start(f32[25,4096]{1,0:T(8,128)} %rel_im.3) | copy-start | bytes 1228804
  133.5 14.7 %copy-start.6 = (f32[4096]{0:T(1024)S(1)}, f32[4096]{0:T(1024)}, u32[]{:S(2)}) copy-start(f32[4096]{0:T(1024)} %param.16) | copy-start | bytes 49156
  148.2 0.7 copy-start.10

commit v9 on v7

--- a/solution.py
+++ b/solution.py
@@ -14,6 +14,8 @@
 REL = 4096
 DOM = ("yh", "x", "z")
 DIM = ("yl", "core")
+NEAR = {True}
+FAR = {False}
 SWAP = [(0, 1), (1, 0)]
 F32 = jnp.float32
 BF16 = jnp.bfloat16
@@ -77,7 +79,8 @@
     return jnp.concatenate([ref[0:1, :], ref[1:2, :]], 1)
 
 
-def query_kernel(info, ent_re, ent_im, rel_re, rel_im, lhs, rhs, rel_ids, neg, head_o, relc_o, q_o, m_o, hit_o):
+def query_kernel(info, ent_re, ent_im, rel_re, rel_im, lhs, rhs, rel_ids, neg, eacc, head_o, relc_o, q_o, m_o, hit_o, eacc_o):
+    eacc_o[...] = eacc[...]
     own = jnp.concatenate([pad32(ent_re[...]), pad32(ent_im[...])], 0)
     head = join3(nn(split3(own), onehot_rows(edge_ids(lhs), ROWS)))
     ids = edge_ids(rel_ids)
@@ -106,9 +109,11 @@
     return b
 
 
-def score_kernel(info, bucket, q_r, b0, b1, b2, b3, keep_o, send_o):
+def score_kernel(info, bucket, q_r, b0, near1, near2, b3, far2, far1, keep_o, send_o, b1_o, b2_o):
     core = info[0]
-    blocks = [pack(b[...]) for b in (b0, b1, b2, b3)]
+    b1_o[...] = jnp.where(info[4] < 1, far1[...], near1[...])
+    b2_o[...] = jnp.where(info[4] < 2, far2[...], near2[...])
+    blocks = [pack(b[...]) for b in (b0, b1_o, b2_o, b3)]
     q = [q_r[:, 0:CH], q_r[:, CH : 2 * CH]]
     for first, out in ((1, send_o), (0, keep_o)):
         c = core ^ first
@@ -196,18 +201,27 @@
     out[...] = tot
 
 
-def both_kernel(info, a, b, s0, got1, got2, got3, out, ring_o, wrap_o):
+def both_kernel(a, b, out):
     tot = a[...] + b[...]
-    for i in range(32):
+    for i in range(8):
         out[i] = tot
+
+
+def ring_kernel(info, s0, got1, got2, got3, ring_o, wrap_o):
     z = info[3]
     ring = s0[...]
     wrap = jnp.zeros_like(ring)
-    for s, got in ((1, got1), (2, got2), (3, got3)):
-        ring = ring + jnp.where(z + s < 8, got[...], 0.0)
-        wrap = wrap + jnp.where(z + s < 8, 0.0, got[...])
+    for d, got in ((1, got1), (2, got2), (3, got3)):
+        ring = ring + jnp.where(z + d < 8, got[...], 0.0)
+        wrap = wrap + jnp.where(z + d < 8, 0.0, got[...])
     ring_o[...] = ring
     wrap_o[...] = wrap
+
+
+def copies_kernel(a, out):
+    for x in range(4):
+        for z in range(8):
+            out[x, 2 * W * z : 2 * W * z + 2 * W, :] = a[z]
 
 
 def square_kernel(rel, ring, wrap, ent_o, sq_o):
@@ -217,7 +231,7 @@
     for i in range(8):
         sq_o[i, :, 0:ROWS] = es
     for t in range(32):
-        tot = rel[t]
+        tot = rel[t // 8, 2 * W * (t % 8) : 2 * W * (t % 8) + 2 * W, :]
         rs = jnp.sum(tot * tot, 0, keepdims=True)
         for i in range(8):
             sq_o[i, :, ROWS + 128 * t : ROWS + 128 * t + 128] = rs
@@ -237,13 +251,14 @@
     scale = LEARN_RATE / jnp.sqrt(acc)
     for t in range(32):
         at = slice(128 * t, 128 * t + 128)
-        tot = rel[t]
+        tot = rel[t // 8, 2 * W * (t % 8) : 2 * W * (t % 8) + 2 * W, :]
         rre_o[:, at] = rel_re[:, at] - scale[:, at] * tot[:W]
         rim_o[:, at] = rel_im[:, at] - scale[:, at] * tot[W:]
 
 
-def shift(block, distance):
-    return lax.ppermute(block, DOM, [(i, (i + distance) % 64) for i in range(64)])
+def shift(block, distance, kinds):
+    ends = [(i, (i + distance) % 64) for i in range(64)]
+    return lax.ppermute(block, DOM, [(i, j) for i, j in ends if (i // 32 == j // 32) in kinds])
 
 
 def exchange(pieces, axes):
@@ -251,16 +266,19 @@
 
 
 def per_device(ent_re, ent_im, ent_acc, rel_re, rel_im, rel_acc, lhs_rows, rhs_rows, rel_ids, neg_rows, bucket_step):
-    info = jnp.stack([lax.axis_index("core"), lax.axis_index("x"), lax.axis_index("yl"), lax.axis_index("z")]).astype(I32)
+    info = jnp.stack([lax.axis_index("core"), lax.axis_index("x"), lax.axis_index("yl"), lax.axis_index("z"), lax.axis_index(("x", "z"))]).astype(I32)
     own = jnp.concatenate([ent_re, ent_im], 0)
-    b1, b2, b3 = [shift(own, d) for d in (1, 2, 3)]
+    near1, near2, all3 = shift(own, 1, NEAR), shift(own, 2, NEAR), shift(own, 3, NEAR | FAR)
+    far2, far1 = shift(own, 2, FAR), shift(own, 1, FAR)
     neg = jnp.pad(neg_rows, ((0, 0), (0, 24)), constant_values=-1)
-    head, relc, q, m, hit = call(
-        query_kernel, "query", [(64, 256), (64, 256), (64, 256), (8, ROWS), (CH, ROWS)], [SM] + [VM] * 8,
-    )(info, ent_re, ent_im, rel_re, rel_im, lhs_rows, rhs_rows, rel_ids, neg)
+    head, relc, q, m, hit, eacc = call(
+        query_kernel, "query", [(64, 256), (64, 256), (64, 256), (8, ROWS), (CH, ROWS), (1, ROWS)], [SM] + [VM] * 9,
+    )(info, ent_re, ent_im, rel_re, rel_im, lhs_rows, rhs_rows, rel_ids, neg, ent_acc.reshape(1, ROWS))
     quarter = (4, 32, ROWS)
     block = (2 * W, ROWS)
-    keep, send = call(score_kernel, "score", [quarter, quarter], [SM, SM] + [VM] * 5)(info, bucket_step, q, own, b1, b2, b3)
+    keep, send, b1, b2 = call(
+        score_kernel, "score", [quarter, quarter, block, block], [SM, SM] + [VM] * 7
+    )(info, bucket_step, q, own, near1, near2, all3, far2, far1)
     s = call(add_kernel, "add", quarter, [VM] * 2)(keep, lax.ppermute(send, "core", SWAP))
     s = exchange(s, "yl")
     w = call(weight_kernel, "weight", quarter, [SM, SM] + [VM] * 3)(info, bucket_step, s, m, hit)
@@ -268,20 +286,24 @@
     w_other = lax.ppermute(w_mine, "core", SWAP)
     s0, s1, s2, s3, gr = call(
         grad_kernel, "grad", [block, block, block, block, (4, 2 * W + 1, 256)], [SM, SM] + [VM] * 11,
-    )(info, bucket_step, q, head, relc, w_mine, w_other, own, b1, b2, b3, lhs_rows, rel_ids)
-    got = [lax.ppermute(v, "z", [(i, (i - d) % 8) for i in range(8)]) for d, v in ((1, s1), (2, s2), (3, s3))]
+    )(info, bucket_step, q, head, relc, w_mine, w_other, own, b1, b2, all3, lhs_rows, rel_ids)
+    got1, got2, got3 = [lax.ppermute(v, "z", [(i, (i - d) % 8) for i in range(8)]) for d, v in ((1, s1), (2, s2), (3, s3))]
     gr = exchange(gr, "x")
     pieces = call(place_kernel, "place", (8, 2 * W, 128), [SM, VM])(info, gr)
+    pieces, got1 = lax.optimization_barrier((pieces, got1))
     half = call(fold_kernel, "fold", (2 * W, 128), [VM])(exchange(pieces, "z"))
-    twin, got = lax.optimization_barrier((lax.ppermute(half, "yh", SWAP), got))
-    rel, ring, wrap = call(both_kernel, "both", [(32, 2 * W, 128), block, block], [SM] + [VM] * 6)(info, half, twin, s0, *got)
+    ring, wrap = call(ring_kernel, "ring", [block, block], [SM] + [VM] * 4)(info, s0, got1, got2, got3)
+    twin, wrap = lax.optimization_barrier((lax.ppermute(half, "yh", SWAP), wrap))
+    rel = call(both_kernel, "both", (8, 2 * W, 128), [VM] * 2)(half, twin)
     wrap = lax.ppermute(wrap, DOM, [(i, (i - 8) % 64) for i in range(64) if i % 8 >= 5])
-    rel = exchange(rel, ("x", "z"))
+    rel = call(copies_kernel, "copies", (4, 16 * W, 128), [VM])(exchange(rel, "z"))
+    rel, wrap = lax.optimization_barrier((rel, wrap))
+    rel = exchange(rel, "x")
     ent, sq = call(square_kernel, "square", [block, (8, 1, ROWS + REL)], [VM] * 3)(rel, ring, wrap)
     sq = exchange(sq, DIM)
     new_re, new_im, new_acc, new_rel_re, new_rel_im, new_rel_acc = call(
         update_kernel, "update", [(W, ROWS), (W, ROWS), (1, ROWS), (W, REL), (W, REL), (1, REL)], [VM] * 9
-    )(sq, rel, ent, ent_re, ent_im, ent_acc.reshape(1, ROWS), rel_re, rel_im, rel_acc.reshape(1, REL))
+    )(sq, rel, ent, ent_re, ent_im, eacc, rel_re, rel_im, rel_acc.reshape(1, REL))
     return new_re, new_im, new_acc.reshape(ROWS), new_rel_re, new_rel_im, new_rel_acc.reshape(REL)
 
 

time: 156 us -> 148 us (0.949)
  waiting for transfers between devices: 40.7 us -> 19.7 us
  starting transfers between devices: 53.1 us -> 67.1 us
    all_to_all x2 -> x3, waiting for transfers between devices: 21.3 us -> 9.44 us  [exchange(): return lax.all_to_all(pieces, axes, 0, 0)]
    ppermute x4 -> x6, waiting for transfers between devices: 11.8 us -> 3.49 us  [the longest x5 3.49 us: shift(): lax.ppermute(block, DOM, [(i, j) for i, j in ends if (i // 32 == j // 32)...]
    ppermute x1, starting transfers between devices: 3.12 us -> 7.57 us  [per_device(): lax.ppermute(send, 'core', SWAP)]
    ppermute x4 -> x6, starting transfers between devices: 20.6 us -> 24.5 us  [the longest x5 19 us: shift(): lax.ppermute(block, DOM, [(i, j) for i, j in ends if (i // 32 == j // 32)...]
    all_to_all x2 -> x3, starting transfers between devices: 11.5 us -> 14.8 us  [exchange(): return lax.all_to_all(pieces, axes, 0, 0)]
    ppermute x3, starting transfers between devices: 11.6 us -> 14 us  [per_device(): lax.ppermute(v, 'z', [(i, (i - d) % 8) for i in range(8)])]
  transfers between devices with their start and end apart: 12 -> 15, of which waited for: 9 -> 7; matrix products, arithmetic and copies ran while one was open for 0% -> 0% of each run, Pallas kernels for 1% -> 3%
where the time goes in v9:
time: 148 us; the launch traced here: 147 us
  starting transfers between devices  67.1 us (45%)
  blocking collectives  44 us (30%)
  waiting for transfers between devices  19.7 us (13%)
  Pallas kernels  10.4 us (7%)
  local copies, waits for them, and re-layouts  3.57 us (2%)
    all_to_all x4, blocking collectives, exchange(): return lax.all_to_all(pieces, axes, 0, 0)  44 us
    ppermute x5, starting transfers between devices, shift(): lax.ppermute(block, DOM, [(i, j) for i, j in ends if (i // 32 == j // 32)...  19 us
    all_to_all x3, starting transfers between devices, exchange(): return lax.all_to_all(pieces, axes, 0, 0)  14.8 us
    ppermute x3, starting transfers between devices, per_device(): lax.ppermute(v, 'z', [(i, (i - d) % 8) for i in range(8)])  14 us
    all_to_all x3, waiting for transfers between devices, exchange(): return lax.all_to_all(pieces, axes, 0, 0)  9.44 us
    ppermute x1, starting transfers between devices, per_device(): lax.ppermute(send, 'core', SWAP)  7.57 us
    ppermute x1, starting transfers between devices, per_device(): w_other = lax.ppermute(w_mine, 'core', SWAP)  5.66 us
    ppermute x1, starting transfers between devices, per_device(): lax.ppermute(half, 'yh', SWAP)  5.5 us
  transfers between devices with their start and end apart: 15, of which 7 were waited for; matrix products, arithmetic and copies ran while one was open for 0% of the time, Pallas kernels for 3%

profile of v9, /device:TPU:1, one launch (start us, length us, event | category | flops | bytes accessed | tf_op | source)
XLA Modules:
  0.0 146.6 jit_solution(12996332123037128788)
XLA Ops:
  0.6 0.0 copy-start.4
  0.6 0.0 copy-start.5
  0.7 0.9 pad_maximum_fusion.b0
  1.6 1.3 collective-permute-start.4
  2.9 1.3 collective-permute-start.3
  4.2 7.2 %collective-permute-start.2 = (f32[50,512]{1,0:T(8,128)S(1)}, f32[50,512]{1,0:T(8,128)S(1)}, u32[]{:S(2)}, u32[]{:S(2)}) collective-permute-start(f32[50,512]{1,0:T(8,128)S(1)} %pad_maximum_fusion.b0), channel_id=1, source_target_pairs={{0,24},{8,32},{16,40},{24,48},{32,56},{40,64},{48,72},{56,80},{64,... | collective-permute-start | bytes 307208 | tf_op jit(solution)/shard_map/ppermute | solution.py:261
  11.4 6.1 %collective-permute-start.1 = (f32[50,512]{1,0:T(8,128)S(1)}, f32[50,512]{1,0:T(8,128)S(1)}, u32[]{:S(2)}, u32[]{:S(2)}) collective-permute-start(f32[50,512]{1,0:T(8,128)S(1)} %pad_maximum_fusion.b0), channel_id=1, source_target_pairs={{0,16},{8,24},{16,32},{24,40},{32,48},{40,56},{48,64},{56,72},{64,... | collective-permute-start | bytes 307208 | tf_op jit(solution)/shard_map/ppermute | solution.py:261
  17.5 3.1 %collective-permute-start = (f32[50,512]{1,0:T(8,128)S(1)}, f32[50,512]{1,0:T(8,128)S(1)}, u32[]{:S(2)}, u32[]{:S(2)}) collective-permute-start(f32[50,512]{1,0:T(8,128)S(1)} %pad_maximum_fusion.b0), channel_id=1, source_target_pairs={{0,8},{8,16},{16,24},{24,32},{32,40},{40,48},{48,56},{56,64},{64,7... | collective-permute-start | bytes 307208 | tf_op jit(solution)/shard_map/ppermute | solution.py:261
  20.6 0.0 copy-start.12
  20.6 0.7 copy-done.12
  21.3 0.0 copy-start.9
  21.4 0.0 copy-start.10
  21.4 0.1 stack.23.info
  21.5 0.0 copy-done.4
  21.5 0.0 copy-done.5
  21.5 0.6 copy-done.11
  22.0 0.0 copy-done.9
  22.0 0.0 copy-done.10
  22.0 0.1 copy-done.8
  22.1 1.0 copy-done
  23.2 1.0 copy-done.2
  24.2 1.5 %query.1 = (f32[64,256]{1,0:T(8,128)S(1)}, f32[64,256]{1,0:T(8,128)S(1)}, f32[64,256]{1,0:T(8,128)S(1)}, f32[8,512]{1,0:T(8,128)S(1)}, f32[128,512]{1,0:T(8,128)S(1)}, /*index=5*/f32[1,512]{1,0:T(1,128)S(1)}) custom-call(s32[5]{0:T(128)S(1)} %stack.23.info, f32[25,512]{1,0:T(8,128)S(1)} %copy-done.4, f32[25,512]{1,0:T(8,128)S(1)} %copy-done.5, ...), custom_call_target="tpu_custom_call" | custom-call | tf_op jit(solution)/shard_map/query/pallas_call | solution.py:274
  25.8 0.0 copy-start.7
  25.8 0.0 collective-permute-done.4.far1
  25.8 0.0 collective-permute-done.3.far2
  25.8 3.0 %collective-permute-done.2.b3 = f32[50,512]{1,0:T(8,128)S(1)} collective-permute-done((f32[50,512]{1,0:T(8,128)S(1)}, f32[50,512]{1,0:T(8,128)S(1)}, u32[]{:S(2)}, u32[]{:S(2)}) %collective-permute-start.2) | collective-permute-done | bytes 102432 | tf_op jit(solution)/shard_map/ppermute | solution.py:261
  28.8 0.0 collective-permute-done.1.near2
  28.8 0.4 collective-permute-done.near1
  29.3 0.0 copy-done.7
  29.3 1.2 score.1
  30.5 7.6 %collective-permute-start.5 = (f32[4,32,512]{2,1,0:T(8,128)S(1)}, f32[4,32,512]{2,1,0:T(8,128)S(1)}, u32[]{:S(2)}, u32[]{:S(2)}) collective-permute-start(f32[4,32,512]{2,1,0:T(8,128)S(1)} %get-tuple-element.41), channel_id=1, source_target_pairs={{0,1},{1,0},{2,3},{3,2},{4,5},{5,4},{6,7},{7,6},{8,9},{9,8},{10,11... | collective-permute-start | bytes 786440 | tf_op jit(solution)/shard_map/ppermute | solution.py:282
  38.0 1.1 collective-permute-done.5.b
  39.2 10.7 %all_to_all.35.parts = f32[4,32,512]{2,1,0:T(8,128)S(1)} all-to-all(f32[4,32,512]{2,1,0:T(8,128)S(1)} %add.7), channel_id=1, replica_groups=mesh['yh'=2,'x'=4,'z'=8,'yl'=4,'core'=2] {'yl'}, dimensions={0} | all-to-all | bytes 524288 | tf_op jit(solution)/shard_map/all_to_all | solution.py:265
  49.9 0.8 weight.1
  50.6 8.8 %all_to_all.36.w_mine = f32[4,32,512]{2,1,0:T(8,128)S(1)} all-to-all(f32[4,32,512]{2,1,0:T(8,128)S(1)} %weight.1), channel_id=1, replica_groups=mesh['yh'=2,'x'=4,'z'=8,'yl'=4,'core'=2] {'yl'}, dimensions={0} | all-to-all | bytes 524288 | tf_op jit(solution)/shard_map/all_to_all | solution.py:265
  59.4 5.7 %collective-permute-start.6 = (f32[4,32,512]{2,1,0:T(8,128)S(1)}, f32[4,32,512]{2,1,0:T(8,128)S(1)}, u32[]{:S(2)}, u32[]{:S(2)}) collective-permute-start(f32[4,32,512]{2,1,0:T(8,128)S(1)} %all_to_all.36.w_mine), channel_id=1, source_target_pairs={{0,1},{1,0},{2,3},{3,2},{4,5},{5,4},{6,7},{7,6},{8,9},{9,8},{10,11... | collective-permute-start | bytes 786440 | tf_op jit(solution)/shard_map/ppermute | solution.py:286
  65.1 1.1 collective-permute-done.6.w_other
  66.2 2.2 %grad.1 = (f32[50,512]{1,0:T(8,128)S(1)}, f32[50,512]{1,0:T(8,128)S(1)}, f32[50,512]{1,0:T(8,128)S(1)}, f32[50,512]{1,0:T(8,128)S(1)}, f32[4,51,256]{2,1,0:T(8,128)}) custom-call(s32[5]{0:T(128)S(1)} %stack.23.info, s32[2]{0:T(128)S(1)} %copy-done.7, f32[64,256]{1,0:T(8,128)S(1)} %get-tuple-element.37.q_r, f32[64,256]{1,0:T(8,128)S(1)} %get-tuple-element.38.head_r, ...), custom_call_target="tpu_custom_call" | custom-call | tf_op jit(solution)/shard_map/grad/pallas_call | solution.py:287
  68.4 3.4 %all-to-all-start.2 = ((f32[4,51,256]{2,1,0:T(8,128)}), f32[4,51,256]{2,1,0:T(8,128)S(1)}, u32[]{:S(2)}, u32[]{:S(2)}) async-start(f32[4,51,256]{2,1,0:T(8,128)} %get-tuple-element.46), calls=%async_computation.2 | async-start | bytes 458752 | tf_op jit(solution)/shard_map/all_to_all | solution.py:265
  71.8 4.5 %collective-permute-start.7 = (f32[50,512]{1,0:T(8,128)S(1)}, f32[50,512]{1,0:T(8,128)S(1)}, u32[]{:S(2)}, u32[]{:S(2)}) collective-permute-start(f32[50,512]{1,0:T(8,128)S(1)} %get-tuple-element.47), channel_id=1, source_target_pairs={{0,56},{8,0},{16,8},{24,16},{32,24},{40,32},{48,40},{56,48},{1,57}... | collective-permute-start | bytes 307208 | tf_op jit(solution)/shard_map/ppermute | solution.py:290
  76.3 1.2 all-to-all-done.2.gr
  77.6 2.1 %place.1 = f32[8,50,128]{2,1,0:T(8,128)} custom-call(s32[5]{0:T(128)S(1)} %stack.23.info, f32[4,51,256]{2,1,0:T(8,128)S(1)} %all-to-all-done.2.gr), custom_call_target="tpu_custom_call" | custom-call | tf_op jit(solution)/shard_map/place/pallas_call | solution.py:292
  79.6 0.0 collective-permute-done.7.got1
  79.6 6.1 %all-to-all-start.3 = ((f32[8,50,128]{2,1,0:T(8,128)}), f32[8,50,128]{2,1,0:T(8,128)S(1)}, u32[]{:S(2)}, u32[]{:S(2)}) async-start(f32[8,50,128]{2,1,0:T(8,128)} %place.1), calls=%async_computation.3 | async-start | bytes 458752 | tf_op jit(solution)/shard_map/all_to_all | solution.py:265
  85.7 5.5 %collective-permute-start.9 = (f32[50,512]{1,0:T(8,128)S(1)}, f32[50,512]{1,0:T(8,128)S(1)}, u32[]{:S(2)}, u32[]{:S(2)}) collective-permute-start(f32[50,512]{1,0:T(8,128)S(1)} %get-tuple-element.51), channel_id=1, source_target_pairs={{0,48},{8,56},{16,0},{24,8},{32,16},{40,24},{48,32},{56,40},{1,49}... | collective-permute-start | bytes 307208 | tf_op jit(solution)/shard_map/ppermute | solution.py:290
  91.2 4.0 %collective-permute-start.10 = (f32[50,512]{1,0:T(8,128)S(1)}, f32[50,512]{1,0:T(8,128)S(1)}, u32[]{:S(2)}, u32[]{:S(2)}) collective-permute-start(f32[50,512]{1,0:T(8,128)S(1)} %get-tuple-element.52), channel_id=1, source_target_pairs={{0,40},{8,48},{16,56},{24,0},{32,8},{40,16},{48,24},{56,32},{1,41}... | collective-permute-start | bytes 307208 | tf_op jit(solution)/shard_map/ppermute | solution.py:290
  95.2 0.0 all-to-all-done.3.parts
  95.3 5.5 %collective-permute-start.8 = (f32[50,128]{1,0:T(8,128)S(1)}, f32[50,128]{1,0:T(8,128)S(1)}, u32[]{:S(2)}, u32[]{:S(2)}) collective-permute-start(f32[50,128]{1,0:T(8,128)S(1)} %fold.1.a), channel_id=1, source_target_pairs={{0,256},{256,0},{1,257},{257,1},{2,258},{258,2},{3,259},{259,3},{4... | collective-permute-start | bytes 76808 | tf_op jit(solution)/shard_map/ppermute | solution.py:296
  100.8 0.0 collective-permute-done.9.got2
  100.8 4.4 %collective-permute-done.10.got3 = f32[50,512]{1,0:T(8,128)S(1)} collective-permute-done((f32[50,512]{1,0:T(8,128)S(1)}, f32[50,512]{1,0:T(8,128)S(1)}, u32[]{:S(2)}, u32[]{:S(2)}) %collective-permute-start.10) | collective-permute-done | bytes 102432 | tf_op jit(solution)/shard_map/ppermute | solution.py:290
  105.2 0.6 ring.1
  105.8 0.0 collective-permute-done.8.b
  105.8 0.7 both.1
  106.5 5.3 %all-to-all-start.4 = ((f32[8,50,128]{2,1,0:T(8,128)}), f32[8,50,128]{2,1,0:T(8,128)S(1)}, u32[]{:S(2)}, u32[]{:S(2)}) async-start(f32[8,50,128]{2,1,0:T(8,128)} %both.1), calls=%async_computation.4 | async-start | bytes 458752 | tf_op jit(solution)/shard_map/all_to_all | solution.py:265
  111.8 0.7 collective-permute-start.11
  112.5 8.2 %all-to-all-done.4.a = f32[8,50,128]{2,1,0:T(8,128)S(1)} async-done(((f32[8,50,128]{2,1,0:T(8,128)}), f32[8,50,128]{2,1,0:T(8,128)S(1)}, u32[]{:S(2)}, u32[]{:S(2)}) %all-to-all-start.4) | async-done | bytes 204832 | tf_op jit(solution)/shard_map/all_to_all | solution.py:265
  120.7 0.1 copies.1
  120.7 0.0 collective-permute-done.11.wrap
  120.8 11.6 %all_to_all.37.rel = f32[4,400,128]{2,1,0:T(8,128)S(1)} all-to-all(f32[4,400,128]{2,1,0:T(8,128)S(1)} %copies.1), channel_id=1, replica_groups=mesh['yh'=2,'x'=4,'z'=8,'yl'=4,'core'=2] {'x'}, dimensions={0} | all-to-all | bytes 1638400 | tf_op jit(solution)/shard_map/all_to_all | solution.py:265
  132.4 0.1 square.1
  132.5 0.0 copy-start.6
  132.5 12.9 %all_to_all.38.sq = f32[8,1,4608]{2,1,0:T(1,128)S(1)} all-to-all(f32[8,1,4608]{2,1,0:T(1,128)S(1)} %get-tuple-element.59), channel_id=1, replica_groups=mesh['yh'=2,'x'=4,'z'=8,'yl'=4,'core'=2] {'yl','core'}, dimensions={0} | all-to-all | bytes 294912 | tf_op jit(solution)/shard_map/all_to_all | solution.py:265
  145.4 0.0 copy-done.3
  145.4 1.1 update.1
  (11 shorter events, 0.1 us)
Async XLA Ops:
  0.6 20.8 %copy-start.4 = (f32[25,512]{1,0:T(8,128)S(1)}, f32[25,512]{1,0:T(8,128)}, u32[]{:S(2)}) copy-start(f32[25,512]{1,0:T(8,128)} %ent_re.3) | copy-start | bytes 153604
  0.6 20.8 %copy-start.5 = (f32[25,512]{1,0:T(8,128)S(1)}, f32[25,512]{1,0:T(8,128)}, u32[]{:S(2)}) copy-start(f32[25,512]{1,0:T(8,128)} %ent_im.3) | copy-start | bytes 153604
  1.6 24.2 %collective-permute-start.4 = (f32[50,512]{1,0:T(8,128)S(1)}, f32[50,512]{1,0:T(8,128)S(1)}, u32[]{:S(2)}, u32[]{:S(2)}) collective-permute-start(f32[50,512]{1,0:T(8,128)S(1)} %pad_maximum_fusion.b0), channel_id=1, source_target_pairs={{248,256},{504,0},{249,257},{505,1},{250,258},{506,2},{251,259},{5... | collective-permute-start | bytes 307208 | tf_op jit(solution)/shard_map/ppermute | solution.py:261
  2.9 22.9 %collective-permute-start.3 = (f32[50,512]{1,0:T(8,128)S(1)}, f32[50,512]{1,0:T(8,128)S(1)}, u32[]{:S(2)}, u32[]{:S(2)}) collective-permute-start(f32[50,512]{1,0:T(8,128)S(1)} %pad_maximum_fusion.b0), channel_id=1, source_target_pairs={{240,256},{248,264},{496,0},{504,8},{241,257},{249,265},{497,1},{5... | collective-permute-start | bytes 307208 | tf_op jit(solution)/shard_map/ppermute | solution.py:261
  4.2 24.7 %collective-permute-start.2 = (f32[50,512]{1,0:T(8,128)S(1)}, f32[50,512]{1,0:T(8,128)S(1)}, u32[]{:S(2)}, u32[]{:S(2)}) collective-permute-start(f32[50,512]{1,0:T(8,128)S(1)} %pad_maximum_fusion.b0), channel_id=1, source_target_pairs={{0,24},{8,32},{16,40},{24,48},{32,56},{40,64},{48,72},{56,80},{64,... | collective-permute-start | bytes 307208 | tf_op jit(solution)/shard_map/ppermute | solution.py:261
  11.4 17.5 %collective-permute-start.1 = (f32[50,512]{1,0:T(8,128)S(1)}, f32[50,512]{1,0:T(8,128)S(1)}, u32[]{:S(2)}, u32[]{:S(2)}) collective-permute-start(f32[50,512]{1,0:T(8,128)S(1)} %pad_maximum_fusion.b0), channel_id=1, source_target_pairs={{0,16},{8,24},{16,32},{24,40},{32,48},{40,56},{48,64},{56,72},{64,... | collective-permute-start | bytes 307208 | tf_op jit(solution)/shard_map/ppermute | solution.py:261
  17.5 11.8 %collective-permute-start = (f32[50,512]{1,0:T(8,128)S(1)}, f32[50,512]{1,0:T(8,128)S(1)}, u32[]{:S(2)}, u32[]{:S(2)}) collective-permute-start(f32[50,512]{1,0:T(8,128)S(1)} %pad_maximum_fusion.b0), channel_id=1, source_target_pairs={{0,8},{8,16},{16,24},{24,32},{32,40},{40,48},{48,56},{56,64},{64,7... | collective-permute-start | bytes 307208 | tf_op jit(solution)/shard_map/ppermute | solution.py:261
  20.6 0.7 copy-start.12
  21.3 0.7 copy-start.11
  21.3 0.7 copy-start.9
  21.4 0.7 copy-start.10
  21.5 0.7 copy-start.8
  22.1 1.0 copy-start
  23.2 1.0 copy-start.2
  25.8 3.5 %copy-start.7 = (s32[2]{0:T(128)S(1)}, s32[2]{0:T(128)}, u32[]{:S(2)}) copy-start(s32[2]{0:T(128)} %bucket.5) | copy-start | bytes 28
  30.5 8.7 %collective-permute-start.5 = (f32[4,32,512]{2,1,0:T(8,128)S(1)}, f32[4,32,512]{2,1,0:T(8,128)S(1)}, u32[]{:S(2)}, u32[]{:S(2)}) collective-permute-start(f32[4,32,512]{2,1,0:T(8,128)S(1)} %get-tuple-element.41), channel_id=1, source_target_pairs={{0,1},{1,0},{2,3},{3,2},{4,5},{5,4},{6,7},{7,6},{8,9},{9,8},{10,11... | collective-permute-start | bytes 786440 | tf_op jit(solution)/shard_map/ppermute | solution.py:282
  59.4 6.8 %collective-permute-start.6 = (f32[4,32,512]{2,1,0:T(8,128)S(1)}, f32[4,32,512]{2,1,0:T(8,128)S(1)}, u32[]{:S(2)}, u32[]{:S(2)}) collective-permute-start(f32[4,32,512]{2,1,0:T(8,128)S(1)} %all_to_all.36.w_mine), channel_id=1, source_target_pairs={{0,1},{1,0},{2,3},{3,2},{4,5},{5,4},{6,7},{7,6},{8,9},{9,8},{10,11... | collective-permute-start | bytes 786440 | tf_op jit(solution)/shard_map/ppermute | solution.py:286
  68.4 9.1 %all-to-all-start.2 = ((f32[4,51,256]{2,1,0:T(8,128)}), f32[4,51,256]{2,1,0:T(8,128)S(1)}, u32[]{:S(2)}, u32[]{:S(2)}) async-start(f32[4,51,256]{2,1,0:T(8,128)} %get-tuple-element.46), calls=%async_computation.2 | async-start | bytes 458752 | tf_op jit(solution)/shard_map/all_to_all | solution.py:265
  71.8 7.8 %collective-permute-start.7 = (f32[50,512]{1,0:T(8,128)S(1)}, f32[50,512]{1,0:T(8,128)S(1)}, u32[]{:S(2)}, u32[]{:S(2)}) collective-permute-start(f32[50,512]{1,0:T(8,128)S(1)} %get-tuple-element.47), channel_id=1, source_target_pairs={{0,56},{8,0},{16,8},{24,16},{32,24},{40,32},{48,40},{56,48},{1,57}... | collective-permute-start | bytes 307208 | tf_op jit(solution)/shard_map/ppermute | solution.py:290
  79.6 15.6 %all-to-all-start.3 = ((f32[8,50,128]{2,1,0:T(8,128)}), f32[8,50,128]{2,1,0:T(8,128)S(1)}, u32[]{:S(2)}, u32[]{:S(2)}) async-start(f32[8,50,128]{2,1,0:T(8,128)} %place.1), calls=%async_computation.3 | async-start | bytes 458752 | tf_op jit(solution)/shard_map/all_to_all | solution.py:265
  85.7 15.0 %collective-permute-start.9 = (f32[50,512]{1,0:T(8,128)S(1)}, f32[50,512]{1,0:T(8,128)S(1)}, u32[]{:S(2)}, u32[]{:S(2)}) collective-permute-start(f32[50,512]{1,0:T(8,128)S(1)} %get-tuple-element.51), channel_id=1, source_target_pairs={{0,48},{8,56},{16,0},{24,8},{32,16},{40,24},{48,32},{56,40},{1,49}... | collective-permute-start | bytes 307208 | tf_op jit(solution)/shard_map/ppermute | solution.py:290
  91.2 14.0 %collective-permute-start.10 = (f32[50,512]{1,0:T(8,128)S(1)}, f32[50,512]{1,0:T(8,128)S(1)}, u32[]{:S(2)}, u32[]{:S(2)}) collective-permute-start(f32[50,512]{1,0:T(8,128)S(1)} %get-tuple-element.52), channel_id=1, source_target_pairs={{0,40},{8,48},{16,56},{24,0},{32,8},{40,16},{48,24},{56,32},{1,41}... | collective-permute-start | bytes 307208 | tf_op jit(solution)/shard_map/ppermute | solution.py:290
  95.3 10.6 %collective-permute-start.8 = (f32[50,128]{1,0:T(8,128)S(1)}, f32[50,128]{1,0:T(8,128)S(1)}, u32[]{:S(2)}, u32[]{:S(2)}) collective-permute-start(f32[50,128]{1,0:T(8,128)S(1)} %fold.1.a), channel_id=1, source_target_pairs={{0,256},{256,0},{1,257},{257,1},{2,258},{258,2},{3,259},{259,3},{4... | collective-permute-start | bytes 76808 | tf_op jit(solution)/shard_map/ppermute | solution.py:296
  106.5 14.2 %all-to-all-start.4 = ((f32[8,50,128]{2,1,0:T(8,128)}), f32[8,50,128]{2,1,0:T(8,128)S(1)}, u32[]{:S(2)}, u32[]{:S(2)}) async-start(f32[8,50,128]{2,1,0:T(8,128)} %both.1), calls=%async_computation.4 | async-start | bytes 458752 | tf_op jit(solution)/shard_map/all_to_all | solution.py:265
  111.8 9.0 %collective-permute-start.11 = (f32[50,512]{1,0:T(8,128)S(1)}, f32[50,512]{1,0:T(8,128)S(1)}, u32[]{:S(2)}, u32[]{:S(2)}) collective-permute-start(f32[50,512]{1,0:T(8,128)S(1)} %get-tuple-element.55), channel_id=1, source_target_pairs={{40,488},{48,496},{56,504},{104,40},{112,48},{120,56},{168,104},{1... | collective-permute-start | bytes 307208 | tf_op jit(solution)/shard_map/ppermute | solution.py:298
  132.4 13.1 %copy-start.1 = (f32[25,4096]{1,0:T(8,128)S(1)}, f32[25,4096]{1,0:T(8,128)}, u32[]{:S(2)}) copy-start(f32[25,4096]{1,0:T(8,128)} %rel_re.3) | copy-start | bytes 1228804
  132.4 13.1 %copy-start.3 = (f32[25,4096]{1,0:T(8,128)S(1)}, f32[25,4096]{1,0:T(8,128)}, u32[]{:S(2)}) copy-start(f32[25,4096]{1,0:T(8,128)} %rel_im.3) | copy-start | bytes 1228804
  132.5 12.9 %copy-start.6 = (f32[4096]{0:T(1024)S(1)}, f32[4096]{0:T(1024)}, u32[]{:S(2)}) copy-start(f32[4096]{0:T(1024)} %param.16) | copy-start | bytes 49156

commit v10 on v9

--- a/solution.py
+++ b/solution.py
@@ -147,22 +147,25 @@
         w_o[i] = w
 
 
-def grad_kernel(info, bucket, q_r, head_r, relc_r, w_mine, w_other, b0, b1, b2, b3, lhs, rel_ids, s0_o, s1_o, s2_o, s3_o, gr_o):
+def group_grads(c, bucket, q_r, w, b0, b1, b2, b3):
+    step = jnp.minimum(jnp.where(c == 0, bucket[0], bucket[1]), STEPS - 1)
+    block = choose(step, [pack(b[...]) for b in (b0, b1, b2, b3)])
+    query = jnp.where(c == 0, q_r[:, 0:CH], q_r[:, CH : 2 * CH])
+    gq = lax.dot_general(block, w, (((1,), (1,)), ((), ())), precision=HIGHEST, preferred_element_type=F32)
+    return step, gq, lax.dot_general(query, w, (((1,), (0,)), ((), ())), precision=HIGHEST, preferred_element_type=F32)
+
+
+def mine_kernel(info, bucket, q_r, w_mine, b0, b1, b2, b3, gq_o, g_o):
+    _, gq_o[...], g_o[...] = group_grads(info[0], bucket, q_r, w_mine[...].reshape(CH, ROWS), b0, b1, b2, b3)
+
+
+def grad_kernel(info, bucket, q_r, head_r, relc_r, gq_mine, g_mine, w_other, b0, b1, b2, b3, lhs, rel_ids, s0_o, s1_o, s2_o, s3_o, gr_o):
     core = info[0]
-    mine = w_mine[...].reshape(CH, ROWS)
-    other = w_other[...].reshape(CH, ROWS)
-    blocks = [pack(b[...]) for b in (b0, b1, b2, b3)]
-    gq = []
-    slots = [jnp.zeros((64, ROWS), F32) for _ in range(STEPS)]
-    for c in range(2):
-        w = jnp.where(core == c, mine, other)
-        step = jnp.minimum(bucket[c], STEPS - 1)
-        block = choose(step, blocks)
-        gq.append(lax.dot_general(block, w, (((1,), (1,)), ((), ())), precision=HIGHEST, preferred_element_type=F32))
-        g = lax.dot_general(q_r[:, c * CH : (c + 1) * CH], w, (((1,), (0,)), ((), ())), precision=HIGHEST, preferred_element_type=F32)
-        for s in range(STEPS):
-            slots[s] = slots[s] + jnp.where(step == s, g, 0.0)
-    gq = jnp.concatenate(gq, 1)
+    step, gq, g = group_grads(1 - core, bucket, q_r, w_other[...].reshape(CH, ROWS), b0, b1, b2, b3)
+    own_step = jnp.minimum(jnp.where(core == 0, bucket[0], bucket[1]), STEPS - 1)
+    slots = [jnp.where(own_step == s, g_mine[...], 0.0) + jnp.where(step == s, g, 0.0) for s in range(STEPS)]
+    mine = gq_mine[...]
+    gq = jnp.concatenate([jnp.where(core == 0, mine, gq), jnp.where(core == 0, gq, mine)], 1)
     g_re, g_im = gq[:32], gq[32:]
     h_re, h_im = head_r[:32, :], head_r[32:, :]
     r_re, r_im = relc_r[:32, :], relc_r[32:, :]
@@ -284,9 +287,10 @@
     w = call(weight_kernel, "weight", quarter, [SM, SM] + [VM] * 3)(info, bucket_step, s, m, hit)
     w_mine = exchange(w, "yl")
     w_other = lax.ppermute(w_mine, "core", SWAP)
+    gq, g = call(mine_kernel, "mine", [(64, CH), (64, ROWS)], [SM, SM] + [VM] * 6)(info, bucket_step, q, w_mine, own, b1, b2, all3)
     s0, s1, s2, s3, gr = call(
-        grad_kernel, "grad", [block, block, block, block, (4, 2 * W + 1, 256)], [SM, SM] + [VM] * 11,
-    )(info, bucket_step, q, head, relc, w_mine, w_other, own, b1, b2, all3, lhs_rows, rel_ids)
+        grad_kernel, "grad", [block, block, block, block, (4, 2 * W + 1, 256)], [SM, SM] + [VM] * 12,
+    )(info, bucket_step, q, head, relc, gq, g, w_other, own, b1, b2, all3, lhs_rows, rel_ids)
     got1, got2, got3 = [lax.ppermute(v, "z", [(i, (i - d) % 8) for i in range(8)]) for d, v in ((1, s1), (2, s2), (3, s3))]
     gr = exchange(gr, "x")
     pieces = call(place_kernel, "place", (8, 2 * W, 128), [SM, VM])(info, gr)

time: 148 us -> 147 us (level)
  transfers between devices with their start and end apart: 15 -> 15, of which waited for: 7 -> 7; matrix products, arithmetic and copies ran while one was open for 0% -> 0% of each run, Pallas kernels for 3% -> 4%
where the time goes in v10:
time: 147 us; the launch traced here: 146 us
  starting transfers between devices  67.1 us (46%)
  blocking collectives  44 us (30%)
  waiting for transfers between devices  18.6 us (13%)
  Pallas kernels  11.2 us (8%)
  local copies, waits for them, and re-layouts  3.57 us (2%)
    all_to_all x4, blocking collectives, exchange(): return lax.all_to_all(pieces, axes, 0, 0)  44 us
    ppermute x5, starting transfers between devices, shift(): lax.ppermute(block, DOM, [(i, j) for i, j in ends if (i // 32 == j // 32)...  19 us
    all_to_all x3, starting transfers between devices, exchange(): return lax.all_to_all(pieces, axes, 0, 0)  14.7 us
    ppermute x3, starting transfers between devices, per_device(): lax.ppermute(v, 'z', [(i, (i - d) % 8) for i in range(8)])  14 us
    all_to_all x3, waiting for transfers between devices, exchange(): return lax.all_to_all(pieces, axes, 0, 0)  9.44 us
    ppermute x1, starting transfers between devices, per_device(): lax.ppermute(send, 'core', SWAP)  7.57 us
    ppermute x1, starting transfers between devices, per_device(): w_other = lax.ppermute(w_mine, 'core', SWAP)  5.66 us
    ppermute x1, starting transfers between devices, per_device(): lax.ppermute(half, 'yh', SWAP)  5.5 us
  transfers between devices with their start and end apart: 15, of which 7 were waited for; matrix products, arithmetic and copies ran while one was open for 0% of the time, Pallas kernels for 4%

profile of v10, /device:TPU:1, one launch (start us, length us, event | category | flops | bytes accessed | tf_op | source)
XLA Modules:
  0.0 146.4 jit_solution(6695832844612055616)
XLA Ops:
  0.6 0.0 copy-start.4
  0.6 0.0 copy-start.5
  0.7 0.9 pad_maximum_fusion.b0
  1.6 1.3 collective-permute-start.4
  2.9 1.3 collective-permute-start.3
  4.2 7.2 %collective-permute-start.2 = (f32[50,512]{1,0:T(8,128)S(1)}, f32[50,512]{1,0:T(8,128)S(1)}, u32[]{:S(2)}, u32[]{:S(2)}) collective-permute-start(f32[50,512]{1,0:T(8,128)S(1)} %pad_maximum_fusion.b0), channel_id=1, source_target_pairs={{0,24},{8,32},{16,40},{24,48},{32,56},{40,64},{48,72},{56,80},{64,... | collective-permute-start | bytes 307208 | tf_op jit(solution)/shard_map/ppermute | solution.py:264
  11.4 6.1 %collective-permute-start.1 = (f32[50,512]{1,0:T(8,128)S(1)}, f32[50,512]{1,0:T(8,128)S(1)}, u32[]{:S(2)}, u32[]{:S(2)}) collective-permute-start(f32[50,512]{1,0:T(8,128)S(1)} %pad_maximum_fusion.b0), channel_id=1, source_target_pairs={{0,16},{8,24},{16,32},{24,40},{32,48},{40,56},{48,64},{56,72},{64,... | collective-permute-start | bytes 307208 | tf_op jit(solution)/shard_map/ppermute | solution.py:264
  17.5 3.1 %collective-permute-start = (f32[50,512]{1,0:T(8,128)S(1)}, f32[50,512]{1,0:T(8,128)S(1)}, u32[]{:S(2)}, u32[]{:S(2)}) collective-permute-start(f32[50,512]{1,0:T(8,128)S(1)} %pad_maximum_fusion.b0), channel_id=1, source_target_pairs={{0,8},{8,16},{16,24},{24,32},{32,40},{40,48},{48,56},{56,64},{64,7... | collective-permute-start | bytes 307208 | tf_op jit(solution)/shard_map/ppermute | solution.py:264
  20.6 0.0 copy-start.12
  20.6 0.7 copy-done.12
  21.3 0.0 copy-start.9
  21.4 0.0 copy-start.10
  21.4 0.1 stack.23.info
  21.5 0.0 copy-done.4
  21.5 0.6 copy-done.11
  22.0 0.0 copy-done.9
  22.0 0.0 copy-done.10
  22.0 0.1 copy-done.8
  22.1 1.0 copy-done
  23.2 1.0 copy-done.2
  24.2 1.5 %query.1 = (f32[64,256]{1,0:T(8,128)S(1)}, f32[64,256]{1,0:T(8,128)S(1)}, f32[64,256]{1,0:T(8,128)S(1)}, f32[8,512]{1,0:T(8,128)S(1)}, f32[128,512]{1,0:T(8,128)S(1)}, /*index=5*/f32[1,512]{1,0:T(1,128)S(1)}) custom-call(s32[5]{0:T(128)S(1)} %stack.23.info, f32[25,512]{1,0:T(8,128)S(1)} %copy-done.4, f32[25,512]{1,0:T(8,128)S(1)} %copy-done.5, ...), custom_call_target="tpu_custom_call" | custom-call | tf_op jit(solution)/shard_map/query/pallas_call | solution.py:277
  25.8 0.0 copy-start.7
  25.8 0.0 collective-permute-done.4.far1
  25.8 0.0 collective-permute-done.3.far2
  25.8 3.0 %collective-permute-done.2.b3 = f32[50,512]{1,0:T(8,128)S(1)} collective-permute-done((f32[50,512]{1,0:T(8,128)S(1)}, f32[50,512]{1,0:T(8,128)S(1)}, u32[]{:S(2)}, u32[]{:S(2)}) %collective-permute-start.2) | collective-permute-done | bytes 102432 | tf_op jit(solution)/shard_map/ppermute | solution.py:264
  28.8 0.0 collective-permute-done.1.near2
  28.8 0.4 collective-permute-done.near1
  29.3 0.0 copy-done.7
  29.3 1.2 score.1
  30.5 7.6 %collective-permute-start.5 = (f32[4,32,512]{2,1,0:T(8,128)S(1)}, f32[4,32,512]{2,1,0:T(8,128)S(1)}, u32[]{:S(2)}, u32[]{:S(2)}) collective-permute-start(f32[4,32,512]{2,1,0:T(8,128)S(1)} %get-tuple-element.43), channel_id=1, source_target_pairs={{0,1},{1,0},{2,3},{3,2},{4,5},{5,4},{6,7},{7,6},{8,9},{9,8},{10,11... | collective-permute-start | bytes 786440 | tf_op jit(solution)/shard_map/ppermute | solution.py:285
  38.0 1.1 collective-permute-done.5.b
  39.2 10.7 %all_to_all.35.parts = f32[4,32,512]{2,1,0:T(8,128)S(1)} all-to-all(f32[4,32,512]{2,1,0:T(8,128)S(1)} %add.7), channel_id=1, replica_groups=mesh['yh'=2,'x'=4,'z'=8,'yl'=4,'core'=2] {'yl'}, dimensions={0} | all-to-all | bytes 524288 | tf_op jit(solution)/shard_map/all_to_all | solution.py:268
  49.9 0.8 weight.1
  50.6 8.8 %all_to_all.36.w_mine = f32[4,32,512]{2,1,0:T(8,128)S(1)} all-to-all(f32[4,32,512]{2,1,0:T(8,128)S(1)} %weight.1), channel_id=1, replica_groups=mesh['yh'=2,'x'=4,'z'=8,'yl'=4,'core'=2] {'yl'}, dimensions={0} | all-to-all | bytes 524288 | tf_op jit(solution)/shard_map/all_to_all | solution.py:268
  59.4 5.7 %collective-permute-start.6 = (f32[4,32,512]{2,1,0:T(8,128)S(1)}, f32[4,32,512]{2,1,0:T(8,128)S(1)}, u32[]{:S(2)}, u32[]{:S(2)}) collective-permute-start(f32[4,32,512]{2,1,0:T(8,128)S(1)} %all_to_all.36.w_mine), channel_id=1, source_target_pairs={{0,1},{1,0},{2,3},{3,2},{4,5},{5,4},{6,7},{7,6},{8,9},{9,8},{10,11... | collective-permute-start | bytes 786440 | tf_op jit(solution)/shard_map/ppermute | solution.py:289
  65.1 1.0 mine.1
  66.1 0.1 collective-permute-done.6.w_other
  66.2 2.0 %grad.1 = (f32[50,512]{1,0:T(8,128)S(1)}, f32[50,512]{1,0:T(8,128)S(1)}, f32[50,512]{1,0:T(8,128)S(1)}, f32[50,512]{1,0:T(8,128)S(1)}, f32[4,51,256]{2,1,0:T(8,128)}) custom-call(s32[5]{0:T(128)S(1)} %stack.23.info, s32[2]{0:T(128)S(1)} %copy-done.7, f32[64,256]{1,0:T(8,128)S(1)} %get-tuple-element.39.q_r, f32[64,256]{1,0:T(8,128)S(1)} %get-tuple-element.40.head_r, ...), custom_call_target="tpu_custom_call" | custom-call | tf_op jit(solution)/shard_map/grad/pallas_call | solution.py:291
  68.2 3.4 %all-to-all-start.2 = ((f32[4,51,256]{2,1,0:T(8,128)}), f32[4,51,256]{2,1,0:T(8,128)S(1)}, u32[]{:S(2)}, u32[]{:S(2)}) async-start(f32[4,51,256]{2,1,0:T(8,128)} %get-tuple-element.50), calls=%async_computation.2 | async-start | bytes 458752 | tf_op jit(solution)/shard_map/all_to_all | solution.py:268
  71.6 4.5 %collective-permute-start.7 = (f32[50,512]{1,0:T(8,128)S(1)}, f32[50,512]{1,0:T(8,128)S(1)}, u32[]{:S(2)}, u32[]{:S(2)}) collective-permute-start(f32[50,512]{1,0:T(8,128)S(1)} %get-tuple-element.51), channel_id=1, source_target_pairs={{0,56},{8,0},{16,8},{24,16},{32,24},{40,32},{48,40},{56,48},{1,57}... | collective-permute-start | bytes 307208 | tf_op jit(solution)/shard_map/ppermute | solution.py:294
  76.1 1.2 all-to-all-done.2.gr
  77.4 2.1 %place.1 = f32[8,50,128]{2,1,0:T(8,128)} custom-call(s32[5]{0:T(128)S(1)} %stack.23.info, f32[4,51,256]{2,1,0:T(8,128)S(1)} %all-to-all-done.2.gr), custom_call_target="tpu_custom_call" | custom-call | tf_op jit(solution)/shard_map/place/pallas_call | solution.py:296
  79.4 0.0 collective-permute-done.7.got1
  79.4 6.1 %all-to-all-start.3 = ((f32[8,50,128]{2,1,0:T(8,128)}), f32[8,50,128]{2,1,0:T(8,128)S(1)}, u32[]{:S(2)}, u32[]{:S(2)}) async-start(f32[8,50,128]{2,1,0:T(8,128)} %place.1), calls=%async_computation.3 | async-start | bytes 458752 | tf_op jit(solution)/shard_map/all_to_all | solution.py:268
  85.5 5.5 %collective-permute-start.9 = (f32[50,512]{1,0:T(8,128)S(1)}, f32[50,512]{1,0:T(8,128)S(1)}, u32[]{:S(2)}, u32[]{:S(2)}) collective-permute-start(f32[50,512]{1,0:T(8,128)S(1)} %get-tuple-element.55), channel_id=1, source_target_pairs={{0,48},{8,56},{16,0},{24,8},{32,16},{40,24},{48,32},{56,40},{1,49}... | collective-permute-start | bytes 307208 | tf_op jit(solution)/shard_map/ppermute | solution.py:294
  91.0 4.0 %collective-permute-start.10 = (f32[50,512]{1,0:T(8,128)S(1)}, f32[50,512]{1,0:T(8,128)S(1)}, u32[]{:S(2)}, u32[]{:S(2)}) collective-permute-start(f32[50,512]{1,0:T(8,128)S(1)} %get-tuple-element.56), channel_id=1, source_target_pairs={{0,40},{8,48},{16,56},{24,0},{32,8},{40,16},{48,24},{56,32},{1,41}... | collective-permute-start | bytes 307208 | tf_op jit(solution)/shard_map/ppermute | solution.py:294
  95.0 0.0 all-to-all-done.3.parts
  95.1 5.5 %collective-permute-start.8 = (f32[50,128]{1,0:T(8,128)S(1)}, f32[50,128]{1,0:T(8,128)S(1)}, u32[]{:S(2)}, u32[]{:S(2)}) collective-permute-start(f32[50,128]{1,0:T(8,128)S(1)} %fold.1.a), channel_id=1, source_target_pairs={{0,256},{256,0},{1,257},{257,1},{2,258},{258,2},{3,259},{259,3},{4... | collective-permute-start | bytes 76808 | tf_op jit(solution)/shard_map/ppermute | solution.py:300
  100.6 0.0 collective-permute-done.9.got2
  100.6 4.5 %collective-permute-done.10.got3 = f32[50,512]{1,0:T(8,128)S(1)} collective-permute-done((f32[50,512]{1,0:T(8,128)S(1)}, f32[50,512]{1,0:T(8,128)S(1)}, u32[]{:S(2)}, u32[]{:S(2)}) %collective-permute-start.10) | collective-permute-done | bytes 102432 | tf_op jit(solution)/shard_map/ppermute | solution.py:294
  105.0 0.6 ring.1
  105.6 0.0 collective-permute-done.8.b
  105.6 0.7 both.1
  106.3 5.3 %all-to-all-start.4 = ((f32[8,50,128]{2,1,0:T(8,128)}), f32[8,50,128]{2,1,0:T(8,128)S(1)}, u32[]{:S(2)}, u32[]{:S(2)}) async-start(f32[8,50,128]{2,1,0:T(8,128)} %both.1), calls=%async_computation.4 | async-start | bytes 458752 | tf_op jit(solution)/shard_map/all_to_all | solution.py:268
  111.6 0.7 collective-permute-start.11
  112.3 8.2 %all-to-all-done.4.a = f32[8,50,128]{2,1,0:T(8,128)S(1)} async-done(((f32[8,50,128]{2,1,0:T(8,128)}), f32[8,50,128]{2,1,0:T(8,128)S(1)}, u32[]{:S(2)}, u32[]{:S(2)}) %all-to-all-start.4) | async-done | bytes 204832 | tf_op jit(solution)/shard_map/all_to_all | solution.py:268
  120.5 0.1 copies.1
  120.5 0.0 collective-permute-done.11.wrap
  120.6 11.6 %all_to_all.37.rel = f32[4,400,128]{2,1,0:T(8,128)S(1)} all-to-all(f32[4,400,128]{2,1,0:T(8,128)S(1)} %copies.1), channel_id=1, replica_groups=mesh['yh'=2,'x'=4,'z'=8,'yl'=4,'core'=2] {'x'}, dimensions={0} | all-to-all | bytes 1638400 | tf_op jit(solution)/shard_map/all_to_all | solution.py:268
  132.2 0.1 square.1
  132.3 0.0 copy-start.6
  132.3 12.9 %all_to_all.38.sq = f32[8,1,4608]{2,1,0:T(1,128)S(1)} all-to-all(f32[8,1,4608]{2,1,0:T(1,128)S(1)} %get-tuple-element.63), channel_id=1, replica_groups=mesh['yh'=2,'x'=4,'z'=8,'yl'=4,'core'=2] {'yl','core'}, dimensions={0} | all-to-all | bytes 294912 | tf_op jit(solution)/shard_map/all_to_all | solution.py:268
  145.2 0.0 copy-done.6
  145.2 1.1 update.1
  (12 shorter events, 0.1 us)
Async XLA Ops:
  0.6 20.8 %copy-start.4 = (f32[25,512]{1,0:T(8,128)S(1)}, f32[25,512]{1,0:T(8,128)}, u32[]{:S(2)}) copy-start(f32[25,512]{1,0:T(8,128)} %ent_re.3) | copy-start | bytes 153604
  0.6 20.8 %copy-start.5 = (f32[25,512]{1,0:T(8,128)S(1)}, f32[25,512]{1,0:T(8,128)}, u32[]{:S(2)}) copy-start(f32[25,512]{1,0:T(8,128)} %ent_im.3) | copy-start | bytes 153604
  1.6 24.2 %collective-permute-start.4 = (f32[50,512]{1,0:T(8,128)S(1)}, f32[50,512]{1,0:T(8,128)S(1)}, u32[]{:S(2)}, u32[]{:S(2)}) collective-permute-start(f32[50,512]{1,0:T(8,128)S(1)} %pad_maximum_fusion.b0), channel_id=1, source_target_pairs={{248,256},{504,0},{249,257},{505,1},{250,258},{506,2},{251,259},{5... | collective-permute-start | bytes 307208 | tf_op jit(solution)/shard_map/ppermute | solution.py:264
  2.9 22.9 %collective-permute-start.3 = (f32[50,512]{1,0:T(8,128)S(1)}, f32[50,512]{1,0:T(8,128)S(1)}, u32[]{:S(2)}, u32[]{:S(2)}) collective-permute-start(f32[50,512]{1,0:T(8,128)S(1)} %pad_maximum_fusion.b0), channel_id=1, source_target_pairs={{240,256},{248,264},{496,0},{504,8},{241,257},{249,265},{497,1},{5... | collective-permute-start | bytes 307208 | tf_op jit(solution)/shard_map/ppermute | solution.py:264
  4.2 24.7 %collective-permute-start.2 = (f32[50,512]{1,0:T(8,128)S(1)}, f32[50,512]{1,0:T(8,128)S(1)}, u32[]{:S(2)}, u32[]{:S(2)}) collective-permute-start(f32[50,512]{1,0:T(8,128)S(1)} %pad_maximum_fusion.b0), channel_id=1, source_target_pairs={{0,24},{8,32},{16,40},{24,48},{32,56},{40,64},{48,72},{56,80},{64,... | collective-permute-start | bytes 307208 | tf_op jit(solution)/shard_map/ppermute | solution.py:264
  11.4 17.5 %collective-permute-start.1 = (f32[50,512]{1,0:T(8,128)S(1)}, f32[50,512]{1,0:T(8,128)S(1)}, u32[]{:S(2)}, u32[]{:S(2)}) collective-permute-start(f32[50,512]{1,0:T(8,128)S(1)} %pad_maximum_fusion.b0), channel_id=1, source_target_pairs={{0,16},{8,24},{16,32},{24,40},{32,48},{40,56},{48,64},{56,72},{64,... | collective-permute-start | bytes 307208 | tf_op jit(solution)/shard_map/ppermute | solution.py:264
  17.5 11.8 %collective-permute-start = (f32[50,512]{1,0:T(8,128)S(1)}, f32[50,512]{1,0:T(8,128)S(1)}, u32[]{:S(2)}, u32[]{:S(2)}) collective-permute-start(f32[50,512]{1,0:T(8,128)S(1)} %pad_maximum_fusion.b0), channel_id=1, source_target_pairs={{0,8},{8,16},{16,24},{24,32},{32,40},{40,48},{48,56},{56,64},{64,7... | collective-permute-start | bytes 307208 | tf_op jit(solution)/shard_map/ppermute | solution.py:264
  20.6 0.7 copy-start.12
  21.3 0.7 copy-start.11
  21.3 0.7 copy-start.9
  21.4 0.7 copy-start.10
  21.5 0.7 copy-start.8
  22.1 1.0 copy-start
  23.2 1.0 copy-start.2
  25.8 3.5 %copy-start.7 = (s32[2]{0:T(128)S(1)}, s32[2]{0:T(128)}, u32[]{:S(2)}) copy-start(s32[2]{0:T(128)} %bucket.7) | copy-start | bytes 28
  30.5 8.7 %collective-permute-start.5 = (f32[4,32,512]{2,1,0:T(8,128)S(1)}, f32[4,32,512]{2,1,0:T(8,128)S(1)}, u32[]{:S(2)}, u32[]{:S(2)}) collective-permute-start(f32[4,32,512]{2,1,0:T(8,128)S(1)} %get-tuple-element.43), channel_id=1, source_target_pairs={{0,1},{1,0},{2,3},{3,2},{4,5},{5,4},{6,7},{7,6},{8,9},{9,8},{10,11... | collective-permute-start | bytes 786440 | tf_op jit(solution)/shard_map/ppermute | solution.py:285
  59.4 6.8 %collective-permute-start.6 = (f32[4,32,512]{2,1,0:T(8,128)S(1)}, f32[4,32,512]{2,1,0:T(8,128)S(1)}, u32[]{:S(2)}, u32[]{:S(2)}) collective-permute-start(f32[4,32,512]{2,1,0:T(8,128)S(1)} %all_to_all.36.w_mine), channel_id=1, source_target_pairs={{0,1},{1,0},{2,3},{3,2},{4,5},{5,4},{6,7},{7,6},{8,9},{9,8},{10,11... | collective-permute-start | bytes 786440 | tf_op jit(solution)/shard_map/ppermute | solution.py:289
  68.2 9.1 %all-to-all-start.2 = ((f32[4,51,256]{2,1,0:T(8,128)}), f32[4,51,256]{2,1,0:T(8,128)S(1)}, u32[]{:S(2)}, u32[]{:S(2)}) async-start(f32[4,51,256]{2,1,0:T(8,128)} %get-tuple-element.50), calls=%async_computation.2 | async-start | bytes 458752 | tf_op jit(solution)/shard_map/all_to_all | solution.py:268
  71.6 7.8 %collective-permute-start.7 = (f32[50,512]{1,0:T(8,128)S(1)}, f32[50,512]{1,0:T(8,128)S(1)}, u32[]{:S(2)}, u32[]{:S(2)}) collective-permute-start(f32[50,512]{1,0:T(8,128)S(1)} %get-tuple-element.51), channel_id=1, source_target_pairs={{0,56},{8,0},{16,8},{24,16},{32,24},{40,32},{48,40},{56,48},{1,57}... | collective-permute-start | bytes 307208 | tf_op jit(solution)/shard_map/ppermute | solution.py:294
  79.4 15.6 %all-to-all-start.3 = ((f32[8,50,128]{2,1,0:T(8,128)}), f32[8,50,128]{2,1,0:T(8,128)S(1)}, u32[]{:S(2)}, u32[]{:S(2)}) async-start(f32[8,50,128]{2,1,0:T(8,128)} %place.1), calls=%async_computation.3 | async-start | bytes 458752 | tf_op jit(solution)/shard_map/all_to_all | solution.py:268
  85.5 15.0 %collective-permute-start.9 = (f32[50,512]{1,0:T(8,128)S(1)}, f32[50,512]{1,0:T(8,128)S(1)}, u32[]{:S(2)}, u32[]{:S(2)}) collective-permute-start(f32[50,512]{1,0:T(8,128)S(1)} %get-tuple-element.55), channel_id=1, source_target_pairs={{0,48},{8,56},{16,0},{24,8},{32,16},{40,24},{48,32},{56,40},{1,49}... | collective-permute-start | bytes 307208 | tf_op jit(solution)/shard_map/ppermute | solution.py:294
  91.0 14.0 %collective-permute-start.10 = (f32[50,512]{1,0:T(8,128)S(1)}, f32[50,512]{1,0:T(8,128)S(1)}, u32[]{:S(2)}, u32[]{:S(2)}) collective-permute-start(f32[50,512]{1,0:T(8,128)S(1)} %get-tuple-element.56), channel_id=1, source_target_pairs={{0,40},{8,48},{16,56},{24,0},{32,8},{40,16},{48,24},{56,32},{1,41}... | collective-permute-start | bytes 307208 | tf_op jit(solution)/shard_map/ppermute | solution.py:294
  95.1 10.6 %collective-permute-start.8 = (f32[50,128]{1,0:T(8,128)S(1)}, f32[50,128]{1,0:T(8,128)S(1)}, u32[]{:S(2)}, u32[]{:S(2)}) collective-permute-start(f32[50,128]{1,0:T(8,128)S(1)} %fold.1.a), channel_id=1, source_target_pairs={{0,256},{256,0},{1,257},{257,1},{2,258},{258,2},{3,259},{259,3},{4... | collective-permute-start | bytes 76808 | tf_op jit(solution)/shard_map/ppermute | solution.py:300
  106.3 14.1 %all-to-all-start.4 = ((f32[8,50,128]{2,1,0:T(8,128)}), f32[8,50,128]{2,1,0:T(8,128)S(1)}, u32[]{:S(2)}, u32[]{:S(2)}) async-start(f32[8,50,128]{2,1,0:T(8,128)} %both.1), calls=%async_computation.4 | async-start | bytes 458752 | tf_op jit(solution)/shard_map/all_to_all | solution.py:268
  111.6 9.0 %collective-permute-start.11 = (f32[50,512]{1,0:T(8,128)S(1)}, f32[50,512]{1,0:T(8,128)S(1)}, u32[]{:S(2)}, u32[]{:S(2)}) collective-permute-start(f32[50,512]{1,0:T(8,128)S(1)} %get-tuple-element.59), channel_id=1, source_target_pairs={{40,488},{48,496},{56,504},{104,40},{112,48},{120,56},{168,104},{1... | collective-permute-start | bytes 307208 | tf_op jit(solution)/shard_map/ppermute | solution.py:302
  132.2 13.0 %copy-start.1 = (f32[25,4096]{1,0:T(8,128)S(1)}, f32[25,4096]{1,0:T(8,128)}, u32[]{:S(2)}) copy-start(f32[25,4096]{1,0:T(8,128)} %rel_re.3) | copy-start | bytes 1228804
  132.2 13.0 %copy-start.3 = (f32[25,4096]{1,0:T(8,128)S(1)}, f32[25,4096]{1,0:T(8,128)}, u32[]{:S(2)}) copy-start(f32[25,4096]{1,0:T(8,128)} %rel_im.3) | copy-start | bytes 1228804
  132.3 12.9 %copy-start.6 = (f32[4096]{0:T(1024)S(1)}, f32[4096]{0:T(1024)}, u32[]{:S(2)}) copy-start(f32[4096]{0:T(1024)} %param.16) | copy-start | bytes 49156

commit v11 on v9

--- a/solution.py
+++ b/solution.py
@@ -48,6 +48,16 @@
     mid = rest.astype(BF16)
     lo = (rest - mid.astype(F32)).astype(BF16)
     return jnp.concatenate([hi, mid, lo], 0)
+
+
+def split2(x):
+    hi = x.astype(BF16)
+    return jnp.concatenate([hi, (x - hi.astype(F32)).astype(BF16)], 0)
+
+
+def join2(y):
+    r = y.shape[0] // 2
+    return y[:r] + y[r:]
 
 
 def join3(y):
@@ -167,7 +177,7 @@
     h_re, h_im = head_r[:32, :], head_r[32:, :]
     r_re, r_im = relc_r[:32, :], relc_r[32:, :]
     gh = jnp.concatenate([g_re * r_re + g_im * r_im, g_im * r_re - g_re * r_im], 0)
-    slots[0] = slots[0] + join3(nt(split3(gh), onehot_rows(edge_ids(lhs), ROWS)))
+    slots[0] = slots[0] + join2(nt(split2(gh), onehot_rows(edge_ids(lhs), ROWS)))
     gr_re = (g_re * h_re + g_im * h_im)[:W]
     gr_im = (g_im * h_re - g_re * h_im)[:W]
     ids = edge_ids(rel_ids).astype(F32)
@@ -185,10 +195,10 @@
     vals = []
     cols = []
     for i in range(4):
-        vals.append(split3(pack(gr[i, 0 : 2 * W, :])))
+        vals.append(split2(pack(gr[i, 0 : 2 * W, :])))
         ids = gr[i, 2 * W : 2 * W + 1, :].astype(I32)
         cols.append(jnp.where(jnp.right_shift(ids, 10) == x, jnp.bitwise_and(ids, 1023), -1))
-    total = join3(nt(jnp.concatenate(vals, 1), onehot_rows(jnp.concatenate(cols, 1), 1024)))
+    total = join2(nt(jnp.concatenate(vals, 1), onehot_rows(jnp.concatenate(cols, 1), 1024)))
     for z in range(8):
         out[z, 0:W, :] = total[:W, 128 * z : 128 * z + 128]
         out[z, W : 2 * W, :] = total[32 : 32 + W, 128 * z : 128 * z + 128]

time: 148 us -> 148 us (level)
  no operation moved by 1% of the time
where the time goes in v11:
time: 148 us; the launch traced here: 147 us
  starting transfers between devices  67.1 us (45%)
  blocking collectives  44 us (30%)
  waiting for transfers between devices  19.7 us (13%)
  Pallas kernels  10.4 us (7%)
  local copies, waits for them, and re-layouts  3.57 us (2%)
    all_to_all x4, blocking collectives, exchange(): return lax.all_to_all(pieces, axes, 0, 0)  44 us
    ppermute x5, starting transfers between devices, shift(): lax.ppermute(block, DOM, [(i, j) for i, j in ends if (i // 32 == j // 32)...  19 us
    all_to_all x3, starting transfers between devices, exchange(): return lax.all_to_all(pieces, axes, 0, 0)  14.7 us
    ppermute x3, starting transfers between devices, per_device(): lax.ppermute(v, 'z', [(i, (i - d) % 8) for i in range(8)])  14 us
    all_to_all x3, waiting for transfers between devices, exchange(): return lax.all_to_all(pieces, axes, 0, 0)  9.44 us
    ppermute x1, starting transfers between devices, per_device(): lax.ppermute(send, 'core', SWAP)  7.57 us
    ppermute x1, starting transfers between devices, per_device(): w_other = lax.ppermute(w_mine, 'core', SWAP)  5.66 us
    ppermute x1, starting transfers between devices, per_device(): lax.ppermute(half, 'yh', SWAP)  5.49 us
  transfers between devices with their start and end apart: 15, of which 7 were waited for; matrix products, arithmetic and copies ran while one was open for 0% of the time, Pallas kernels for 3%

profile of v11, /device:TPU:1, one launch (start us, length us, event | category | flops | bytes accessed | tf_op | source)
XLA Modules:
  0.0 146.6 jit_solution(2527457004732895709)
XLA Ops:
  0.6 0.0 copy-start.4
  0.6 0.0 copy-start.5
  0.7 0.9 pad_maximum_fusion.b0
  1.6 1.3 collective-permute-start.4
  2.9 1.3 collective-permute-start.3
  4.2 7.2 %collective-permute-start.2 = (f32[50,512]{1,0:T(8,128)S(1)}, f32[50,512]{1,0:T(8,128)S(1)}, u32[]{:S(2)}, u32[]{:S(2)}) collective-permute-start(f32[50,512]{1,0:T(8,128)S(1)} %pad_maximum_fusion.b0), channel_id=1, source_target_pairs={{0,24},{8,32},{16,40},{24,48},{32,56},{40,64},{48,72},{56,80},{64,... | collective-permute-start | bytes 307208 | tf_op jit(solution)/shard_map/ppermute | solution.py:271
  11.4 6.1 %collective-permute-start.1 = (f32[50,512]{1,0:T(8,128)S(1)}, f32[50,512]{1,0:T(8,128)S(1)}, u32[]{:S(2)}, u32[]{:S(2)}) collective-permute-start(f32[50,512]{1,0:T(8,128)S(1)} %pad_maximum_fusion.b0), channel_id=1, source_target_pairs={{0,16},{8,24},{16,32},{24,40},{32,48},{40,56},{48,64},{56,72},{64,... | collective-permute-start | bytes 307208 | tf_op jit(solution)/shard_map/ppermute | solution.py:271
  17.5 3.1 %collective-permute-start = (f32[50,512]{1,0:T(8,128)S(1)}, f32[50,512]{1,0:T(8,128)S(1)}, u32[]{:S(2)}, u32[]{:S(2)}) collective-permute-start(f32[50,512]{1,0:T(8,128)S(1)} %pad_maximum_fusion.b0), channel_id=1, source_target_pairs={{0,8},{8,16},{16,24},{24,32},{32,40},{40,48},{48,56},{56,64},{64,7... | collective-permute-start | bytes 307208 | tf_op jit(solution)/shard_map/ppermute | solution.py:271
  20.6 0.0 copy-start.12
  20.6 0.7 copy-done.12
  21.3 0.0 copy-start.9
  21.4 0.0 copy-start.10
  21.4 0.1 stack.23.info
  21.5 0.0 copy-done.4
  21.5 0.0 copy-done.5
  21.5 0.6 copy-done.11
  22.0 0.0 copy-done.9
  22.0 0.0 copy-done.10
  22.0 0.1 copy-done.8
  22.1 1.0 copy-done
  23.2 1.0 copy-done.2
  24.2 1.5 %query.1 = (f32[64,256]{1,0:T(8,128)S(1)}, f32[64,256]{1,0:T(8,128)S(1)}, f32[64,256]{1,0:T(8,128)S(1)}, f32[8,512]{1,0:T(8,128)S(1)}, f32[128,512]{1,0:T(8,128)S(1)}, /*index=5*/f32[1,512]{1,0:T(1,128)S(1)}) custom-call(s32[5]{0:T(128)S(1)} %stack.23.info, f32[25,512]{1,0:T(8,128)S(1)} %copy-done.4, f32[25,512]{1,0:T(8,128)S(1)} %copy-done.5, ...), custom_call_target="tpu_custom_call" | custom-call | tf_op jit(solution)/shard_map/query/pallas_call | solution.py:284
  25.8 0.0 copy-start.7
  25.8 0.0 collective-permute-done.4.far1
  25.8 0.0 collective-permute-done.3.far2
  25.8 3.0 %collective-permute-done.2.b3 = f32[50,512]{1,0:T(8,128)S(1)} collective-permute-done((f32[50,512]{1,0:T(8,128)S(1)}, f32[50,512]{1,0:T(8,128)S(1)}, u32[]{:S(2)}, u32[]{:S(2)}) %collective-permute-start.2) | collective-permute-done | bytes 102432 | tf_op jit(solution)/shard_map/ppermute | solution.py:271
  28.8 0.0 collective-permute-done.1.near2
  28.8 0.4 collective-permute-done.near1
  29.3 1.2 score.1
  30.5 7.6 %collective-permute-start.5 = (f32[4,32,512]{2,1,0:T(8,128)S(1)}, f32[4,32,512]{2,1,0:T(8,128)S(1)}, u32[]{:S(2)}, u32[]{:S(2)}) collective-permute-start(f32[4,32,512]{2,1,0:T(8,128)S(1)} %get-tuple-element.41), channel_id=1, source_target_pairs={{0,1},{1,0},{2,3},{3,2},{4,5},{5,4},{6,7},{7,6},{8,9},{9,8},{10,11... | collective-permute-start | bytes 786440 | tf_op jit(solution)/shard_map/ppermute | solution.py:292
  38.0 1.1 collective-permute-done.5.b
  39.2 10.7 %all_to_all.35.parts = f32[4,32,512]{2,1,0:T(8,128)S(1)} all-to-all(f32[4,32,512]{2,1,0:T(8,128)S(1)} %add.7), channel_id=1, replica_groups=mesh['yh'=2,'x'=4,'z'=8,'yl'=4,'core'=2] {'yl'}, dimensions={0} | all-to-all | bytes 524288 | tf_op jit(solution)/shard_map/all_to_all | solution.py:275
  49.9 0.8 weight.1
  50.6 8.8 %all_to_all.36.w_mine = f32[4,32,512]{2,1,0:T(8,128)S(1)} all-to-all(f32[4,32,512]{2,1,0:T(8,128)S(1)} %weight.1), channel_id=1, replica_groups=mesh['yh'=2,'x'=4,'z'=8,'yl'=4,'core'=2] {'yl'}, dimensions={0} | all-to-all | bytes 524288 | tf_op jit(solution)/shard_map/all_to_all | solution.py:275
  59.4 5.7 %collective-permute-start.6 = (f32[4,32,512]{2,1,0:T(8,128)S(1)}, f32[4,32,512]{2,1,0:T(8,128)S(1)}, u32[]{:S(2)}, u32[]{:S(2)}) collective-permute-start(f32[4,32,512]{2,1,0:T(8,128)S(1)} %all_to_all.36.w_mine), channel_id=1, source_target_pairs={{0,1},{1,0},{2,3},{3,2},{4,5},{5,4},{6,7},{7,6},{8,9},{9,8},{10,11... | collective-permute-start | bytes 786440 | tf_op jit(solution)/shard_map/ppermute | solution.py:296
  65.1 1.1 collective-permute-done.6.w_other
  66.2 2.2 %grad.1 = (f32[50,512]{1,0:T(8,128)S(1)}, f32[50,512]{1,0:T(8,128)S(1)}, f32[50,512]{1,0:T(8,128)S(1)}, f32[50,512]{1,0:T(8,128)S(1)}, f32[4,51,256]{2,1,0:T(8,128)}) custom-call(s32[5]{0:T(128)S(1)} %stack.23.info, s32[2]{0:T(128)S(1)} %copy-done.7, f32[64,256]{1,0:T(8,128)S(1)} %get-tuple-element.37.q_r, f32[64,256]{1,0:T(8,128)S(1)} %get-tuple-element.38.head_r, ...), custom_call_target="tpu_custom_call" | custom-call | tf_op jit(solution)/shard_map/grad/pallas_call | solution.py:297
  68.4 3.4 %all-to-all-start.2 = ((f32[4,51,256]{2,1,0:T(8,128)}), f32[4,51,256]{2,1,0:T(8,128)S(1)}, u32[]{:S(2)}, u32[]{:S(2)}) async-start(f32[4,51,256]{2,1,0:T(8,128)} %get-tuple-element.46), calls=%async_computation.2 | async-start | bytes 458752 | tf_op jit(solution)/shard_map/all_to_all | solution.py:275
  71.8 4.5 %collective-permute-start.7 = (f32[50,512]{1,0:T(8,128)S(1)}, f32[50,512]{1,0:T(8,128)S(1)}, u32[]{:S(2)}, u32[]{:S(2)}) collective-permute-start(f32[50,512]{1,0:T(8,128)S(1)} %get-tuple-element.47), channel_id=1, source_target_pairs={{0,56},{8,0},{16,8},{24,16},{32,24},{40,32},{48,40},{56,48},{1,57}... | collective-permute-start | bytes 307208 | tf_op jit(solution)/shard_map/ppermute | solution.py:300
  76.3 1.2 all-to-all-done.2.gr
  77.5 2.1 %place.1 = f32[8,50,128]{2,1,0:T(8,128)} custom-call(s32[5]{0:T(128)S(1)} %stack.23.info, f32[4,51,256]{2,1,0:T(8,128)S(1)} %all-to-all-done.2.gr), custom_call_target="tpu_custom_call" | custom-call | tf_op jit(solution)/shard_map/place/pallas_call | solution.py:302
  79.6 0.0 collective-permute-done.7.got1
  79.6 6.1 %all-to-all-start.3 = ((f32[8,50,128]{2,1,0:T(8,128)}), f32[8,50,128]{2,1,0:T(8,128)S(1)}, u32[]{:S(2)}, u32[]{:S(2)}) async-start(f32[8,50,128]{2,1,0:T(8,128)} %place.1), calls=%async_computation.3 | async-start | bytes 458752 | tf_op jit(solution)/shard_map/all_to_all | solution.py:275
  85.7 5.5 %collective-permute-start.9 = (f32[50,512]{1,0:T(8,128)S(1)}, f32[50,512]{1,0:T(8,128)S(1)}, u32[]{:S(2)}, u32[]{:S(2)}) collective-permute-start(f32[50,512]{1,0:T(8,128)S(1)} %get-tuple-element.51), channel_id=1, source_target_pairs={{0,48},{8,56},{16,0},{24,8},{32,16},{40,24},{48,32},{56,40},{1,49}... | collective-permute-start | bytes 307208 | tf_op jit(solution)/shard_map/ppermute | solution.py:300
  91.2 4.0 %collective-permute-start.10 = (f32[50,512]{1,0:T(8,128)S(1)}, f32[50,512]{1,0:T(8,128)S(1)}, u32[]{:S(2)}, u32[]{:S(2)}) collective-permute-start(f32[50,512]{1,0:T(8,128)S(1)} %get-tuple-element.52), channel_id=1, source_target_pairs={{0,40},{8,48},{16,56},{24,0},{32,8},{40,16},{48,24},{56,32},{1,41}... | collective-permute-start | bytes 307208 | tf_op jit(solution)/shard_map/ppermute | solution.py:300
  95.2 0.0 all-to-all-done.3.parts
  95.2 5.5 %collective-permute-start.8 = (f32[50,128]{1,0:T(8,128)S(1)}, f32[50,128]{1,0:T(8,128)S(1)}, u32[]{:S(2)}, u32[]{:S(2)}) collective-permute-start(f32[50,128]{1,0:T(8,128)S(1)} %fold.1.a), channel_id=1, source_target_pairs={{0,256},{256,0},{1,257},{257,1},{2,258},{258,2},{3,259},{259,3},{4... | collective-permute-start | bytes 76808 | tf_op jit(solution)/shard_map/ppermute | solution.py:306
  100.7 0.0 collective-permute-done.9.got2
  100.7 4.5 %collective-permute-done.10.got3 = f32[50,512]{1,0:T(8,128)S(1)} collective-permute-done((f32[50,512]{1,0:T(8,128)S(1)}, f32[50,512]{1,0:T(8,128)S(1)}, u32[]{:S(2)}, u32[]{:S(2)}) %collective-permute-start.10) | collective-permute-done | bytes 102432 | tf_op jit(solution)/shard_map/ppermute | solution.py:300
  105.2 0.6 ring.1
  105.8 0.0 collective-permute-done.8.b
  105.8 0.7 both.1
  106.5 5.3 %all-to-all-start.4 = ((f32[8,50,128]{2,1,0:T(8,128)}), f32[8,50,128]{2,1,0:T(8,128)S(1)}, u32[]{:S(2)}, u32[]{:S(2)}) async-start(f32[8,50,128]{2,1,0:T(8,128)} %both.1), calls=%async_computation.4 | async-start | bytes 458752 | tf_op jit(solution)/shard_map/all_to_all | solution.py:275
  111.8 0.7 collective-permute-start.11
  112.4 8.2 %all-to-all-done.4.a = f32[8,50,128]{2,1,0:T(8,128)S(1)} async-done(((f32[8,50,128]{2,1,0:T(8,128)}), f32[8,50,128]{2,1,0:T(8,128)S(1)}, u32[]{:S(2)}, u32[]{:S(2)}) %all-to-all-start.4) | async-done | bytes 204832 | tf_op jit(solution)/shard_map/all_to_all | solution.py:275
  120.6 0.1 copies.1
  120.7 0.0 collective-permute-done.11.wrap
  120.7 11.6 %all_to_all.37.rel = f32[4,400,128]{2,1,0:T(8,128)S(1)} all-to-all(f32[4,400,128]{2,1,0:T(8,128)S(1)} %copies.1), channel_id=1, replica_groups=mesh['yh'=2,'x'=4,'z'=8,'yl'=4,'core'=2] {'x'}, dimensions={0} | all-to-all | bytes 1638400 | tf_op jit(solution)/shard_map/all_to_all | solution.py:275
  132.3 0.1 square.1
  132.4 0.0 copy-start.6
  132.4 13.0 %all_to_all.38.sq = f32[8,1,4608]{2,1,0:T(1,128)S(1)} all-to-all(f32[8,1,4608]{2,1,0:T(1,128)S(1)} %get-tuple-element.59), channel_id=1, replica_groups=mesh['yh'=2,'x'=4,'z'=8,'yl'=4,'core'=2] {'yl','core'}, dimensions={0} | all-to-all | bytes 294912 | tf_op jit(solution)/shard_map/all_to_all | solution.py:275
  145.4 0.0 copy-done.1
  145.4 0.0 copy-done.6
  145.4 1.1 update.1
  (11 shorter events, 0.1 us)
Async XLA Ops:
  0.6 20.8 %copy-start.4 = (f32[25,512]{1,0:T(8,128)S(1)}, f32[25,512]{1,0:T(8,128)}, u32[]{:S(2)}) copy-start(f32[25,512]{1,0:T(8,128)} %ent_re.3) | copy-start | bytes 153604
  0.6 20.8 %copy-start.5 = (f32[25,512]{1,0:T(8,128)S(1)}, f32[25,512]{1,0:T(8,128)}, u32[]{:S(2)}) copy-start(f32[25,512]{1,0:T(8,128)} %ent_im.3) | copy-start | bytes 153604
  1.6 24.2 %collective-permute-start.4 = (f32[50,512]{1,0:T(8,128)S(1)}, f32[50,512]{1,0:T(8,128)S(1)}, u32[]{:S(2)}, u32[]{:S(2)}) collective-permute-start(f32[50,512]{1,0:T(8,128)S(1)} %pad_maximum_fusion.b0), channel_id=1, source_target_pairs={{248,256},{504,0},{249,257},{505,1},{250,258},{506,2},{251,259},{5... | collective-permute-start | bytes 307208 | tf_op jit(solution)/shard_map/ppermute | solution.py:271
  2.9 22.9 %collective-permute-start.3 = (f32[50,512]{1,0:T(8,128)S(1)}, f32[50,512]{1,0:T(8,128)S(1)}, u32[]{:S(2)}, u32[]{:S(2)}) collective-permute-start(f32[50,512]{1,0:T(8,128)S(1)} %pad_maximum_fusion.b0), channel_id=1, source_target_pairs={{240,256},{248,264},{496,0},{504,8},{241,257},{249,265},{497,1},{5... | collective-permute-start | bytes 307208 | tf_op jit(solution)/shard_map/ppermute | solution.py:271
  4.2 24.7 %collective-permute-start.2 = (f32[50,512]{1,0:T(8,128)S(1)}, f32[50,512]{1,0:T(8,128)S(1)}, u32[]{:S(2)}, u32[]{:S(2)}) collective-permute-start(f32[50,512]{1,0:T(8,128)S(1)} %pad_maximum_fusion.b0), channel_id=1, source_target_pairs={{0,24},{8,32},{16,40},{24,48},{32,56},{40,64},{48,72},{56,80},{64,... | collective-permute-start | bytes 307208 | tf_op jit(solution)/shard_map/ppermute | solution.py:271
  11.4 17.5 %collective-permute-start.1 = (f32[50,512]{1,0:T(8,128)S(1)}, f32[50,512]{1,0:T(8,128)S(1)}, u32[]{:S(2)}, u32[]{:S(2)}) collective-permute-start(f32[50,512]{1,0:T(8,128)S(1)} %pad_maximum_fusion.b0), channel_id=1, source_target_pairs={{0,16},{8,24},{16,32},{24,40},{32,48},{40,56},{48,64},{56,72},{64,... | collective-permute-start | bytes 307208 | tf_op jit(solution)/shard_map/ppermute | solution.py:271
  17.5 11.8 %collective-permute-start = (f32[50,512]{1,0:T(8,128)S(1)}, f32[50,512]{1,0:T(8,128)S(1)}, u32[]{:S(2)}, u32[]{:S(2)}) collective-permute-start(f32[50,512]{1,0:T(8,128)S(1)} %pad_maximum_fusion.b0), channel_id=1, source_target_pairs={{0,8},{8,16},{16,24},{24,32},{32,40},{40,48},{48,56},{56,64},{64,7... | collective-permute-start | bytes 307208 | tf_op jit(solution)/shard_map/ppermute | solution.py:271
  20.6 0.7 copy-start.12
  21.3 0.7 copy-start.11
  21.3 0.7 copy-start.9
  21.4 0.7 copy-start.10
  21.5 0.7 copy-start.8
  22.1 1.0 copy-start
  23.2 1.0 copy-start.2
  25.8 3.5 %copy-start.7 = (s32[2]{0:T(128)S(1)}, s32[2]{0:T(128)}, u32[]{:S(2)}) copy-start(s32[2]{0:T(128)} %bucket.5) | copy-start | bytes 28
  30.5 8.7 %collective-permute-start.5 = (f32[4,32,512]{2,1,0:T(8,128)S(1)}, f32[4,32,512]{2,1,0:T(8,128)S(1)}, u32[]{:S(2)}, u32[]{:S(2)}) collective-permute-start(f32[4,32,512]{2,1,0:T(8,128)S(1)} %get-tuple-element.41), channel_id=1, source_target_pairs={{0,1},{1,0},{2,3},{3,2},{4,5},{5,4},{6,7},{7,6},{8,9},{9,8},{10,11... | collective-permute-start | bytes 786440 | tf_op jit(solution)/shard_map/ppermute | solution.py:292
  59.4 6.8 %collective-permute-start.6 = (f32[4,32,512]{2,1,0:T(8,128)S(1)}, f32[4,32,512]{2,1,0:T(8,128)S(1)}, u32[]{:S(2)}, u32[]{:S(2)}) collective-permute-start(f32[4,32,512]{2,1,0:T(8,128)S(1)} %all_to_all.36.w_mine), channel_id=1, source_target_pairs={{0,1},{1,0},{2,3},{3,2},{4,5},{5,4},{6,7},{7,6},{8,9},{9,8},{10,11... | collective-permute-start | bytes 786440 | tf_op jit(solution)/shard_map/ppermute | solution.py:296
  68.4 9.1 %all-to-all-start.2 = ((f32[4,51,256]{2,1,0:T(8,128)}), f32[4,51,256]{2,1,0:T(8,128)S(1)}, u32[]{:S(2)}, u32[]{:S(2)}) async-start(f32[4,51,256]{2,1,0:T(8,128)} %get-tuple-element.46), calls=%async_computation.2 | async-start | bytes 458752 | tf_op jit(solution)/shard_map/all_to_all | solution.py:275
  71.8 7.8 %collective-permute-start.7 = (f32[50,512]{1,0:T(8,128)S(1)}, f32[50,512]{1,0:T(8,128)S(1)}, u32[]{:S(2)}, u32[]{:S(2)}) collective-permute-start(f32[50,512]{1,0:T(8,128)S(1)} %get-tuple-element.47), channel_id=1, source_target_pairs={{0,56},{8,0},{16,8},{24,16},{32,24},{40,32},{48,40},{56,48},{1,57}... | collective-permute-start | bytes 307208 | tf_op jit(solution)/shard_map/ppermute | solution.py:300
  79.6 15.6 %all-to-all-start.3 = ((f32[8,50,128]{2,1,0:T(8,128)}), f32[8,50,128]{2,1,0:T(8,128)S(1)}, u32[]{:S(2)}, u32[]{:S(2)}) async-start(f32[8,50,128]{2,1,0:T(8,128)} %place.1), calls=%async_computation.3 | async-start | bytes 458752 | tf_op jit(solution)/shard_map/all_to_all | solution.py:275
  85.7 15.0 %collective-permute-start.9 = (f32[50,512]{1,0:T(8,128)S(1)}, f32[50,512]{1,0:T(8,128)S(1)}, u32[]{:S(2)}, u32[]{:S(2)}) collective-permute-start(f32[50,512]{1,0:T(8,128)S(1)} %get-tuple-element.51), channel_id=1, source_target_pairs={{0,48},{8,56},{16,0},{24,8},{32,16},{40,24},{48,32},{56,40},{1,49}... | collective-permute-start | bytes 307208 | tf_op jit(solution)/shard_map/ppermute | solution.py:300
  91.2 14.0 %collective-permute-start.10 = (f32[50,512]{1,0:T(8,128)S(1)}, f32[50,512]{1,0:T(8,128)S(1)}, u32[]{:S(2)}, u32[]{:S(2)}) collective-permute-start(f32[50,512]{1,0:T(8,128)S(1)} %get-tuple-element.52), channel_id=1, source_target_pairs={{0,40},{8,48},{16,56},{24,0},{32,8},{40,16},{48,24},{56,32},{1,41}... | collective-permute-start | bytes 307208 | tf_op jit(solution)/shard_map/ppermute | solution.py:300
  95.2 10.6 %collective-permute-start.8 = (f32[50,128]{1,0:T(8,128)S(1)}, f32[50,128]{1,0:T(8,128)S(1)}, u32[]{:S(2)}, u32[]{:S(2)}) collective-permute-start(f32[50,128]{1,0:T(8,128)S(1)} %fold.1.a), channel_id=1, source_target_pairs={{0,256},{256,0},{1,257},{257,1},{2,258},{258,2},{3,259},{259,3},{4... | collective-permute-start | bytes 76808 | tf_op jit(solution)/shard_map/ppermute | solution.py:306
  106.5 14.1 %all-to-all-start.4 = ((f32[8,50,128]{2,1,0:T(8,128)}), f32[8,50,128]{2,1,0:T(8,128)S(1)}, u32[]{:S(2)}, u32[]{:S(2)}) async-start(f32[8,50,128]{2,1,0:T(8,128)} %both.1), calls=%async_computation.4 | async-start | bytes 458752 | tf_op jit(solution)/shard_map/all_to_all | solution.py:275
  111.8 9.0 %collective-permute-start.11 = (f32[50,512]{1,0:T(8,128)S(1)}, f32[50,512]{1,0:T(8,128)S(1)}, u32[]{:S(2)}, u32[]{:S(2)}) collective-permute-start(f32[50,512]{1,0:T(8,128)S(1)} %get-tuple-element.55), channel_id=1, source_target_pairs={{40,488},{48,496},{56,504},{104,40},{112,48},{120,56},{168,104},{1... | collective-permute-start | bytes 307208 | tf_op jit(solution)/shard_map/ppermute | solution.py:308
  132.3 13.1 %copy-start.1 = (f32[25,4096]{1,0:T(8,128)S(1)}, f32[25,4096]{1,0:T(8,128)}, u32[]{:S(2)}) copy-start(f32[25,4096]{1,0:T(8,128)} %rel_re.3) | copy-start | bytes 1228804
  132.3 13.1 %copy-start.3 = (f32[25,4096]{1,0:T(8,128)S(1)}, f32[25,4096]{1,0:T(8,128)}, u32[]{:S(2)}) copy-start(f32[25,4096]{1,0:T(8,128)} %rel_im.3) | copy-start | bytes 1228804
  132.4 13.0 %copy-start.6 = (f32[4096]{0:T(1024)S(1)}, f32[4096]{0:T(1024)}, u32[]{:S(2)}) copy-start(f32[4096]{0:T(1024)} %param.16) | copy-start | bytes 49156
